TPU v7x, 1024 devices: a whole 8x8x8 slice. The times are simulated.
1024 devices in a mesh: pole: 16 (over y_hi, z), row: 16 (over x, core), col: 4 (over y_lo).
Axes of the slice: x: 8, y: 8 (y_hi: 2, y_lo: 4; y = y_hi * 4 + y_lo), z: 8, core: 2. Of those that a mesh axis runs over, the one named last changes fastest.
Arguments:
- hamiltonian: float32 [4096, 256], P(('row', 'col')), may hold values from -6 to 6
- margin: float32 [4096, 256], P(('row', 'col')), may hold values from -3 to 3
- owner: int32 [4096], P(('row', 'col')), may hold values from 0 to 4095, as said below
- inverse_blocks: float32 [16, 2, 4096, 4096], P('pole', None, 'col', 'row'), may hold values from -0.125 to 0.125
- pole_index: int32 [16], P('pole'), may hold values from 0 to 63
Outputs:
- density: float32 [4096, 256], P(('col', 'row', 'pole'))
Inputs may be any that keep to these rules, and one draw needn't show every extreme that they name: `owner`: A permutation of the 4096 supernodal rows; among the orbital rows of one device along row+col at most 8 have owners in one block of 256 consecutive supernodal rows, and some device reaches 8 for every block.
All inputs are finite; a program needn't handle non-finite values.
Results may differ from a plain program's by a relative error of at most 0.0001.
Values sent between devices are 32-bit elements; how exact they have to be, the bound alone decides.
No kernel may reach another device: no remote copies, remote signals or barrier semaphores. Data moves between devices by JAX's collectives and lax.ppermute only.
A program may use at most 32 MiB of HBM per device.

v0:
```python
import math

import jax
import jax.numpy as jnp
from jax import lax
from jax.sharding import PartitionSpec as P

POLES = 64


pole_radius = 1.5
weight_scale = 0.3


def exact_dot(left, right):
    return jnp.dot(left, right, precision=lax.Precision.HIGHEST, preferred_element_type=jnp.float32)


def per_device(hamiltonian, margin, owner, inverse_blocks, pole_index):
    rows_axis = lax.axis_size("row")
    cols_axis = lax.axis_size("col")
    share_rows, level_cols = hamiltonian.shape
    block_rows = inverse_blocks.shape[3]
    capacity = 2 * share_rows // rows_axis
    width_part = level_cols // cols_axis
    target = owner // block_rows
    within = owner % block_rows
    hits_table = (target[:, None] == jnp.arange(rows_axis)[None, :]).astype(jnp.int32)
    ranking = jnp.sum((jnp.cumsum(hits_table, axis=0) - hits_table) * hits_table, axis=1)
    slot_index = target * capacity + ranking
    packer = (jnp.arange(rows_axis * capacity)[:, None] == slot_index[None, :]).astype(jnp.float32)
    stacked = jnp.stack([hamiltonian, margin], axis=1).reshape(share_rows, 2 * level_cols)
    packed = exact_dot(packer, stacked).reshape(rows_axis, capacity, 2, level_cols)
    labels = exact_dot(packer, (within + 1).astype(jnp.float32)[:, None]).reshape(
        rows_axis, capacity
    )
    direct = packed.reshape(rows_axis, capacity, 2, cols_axis, width_part)
    direct = direct.transpose(0, 3, 1, 2, 4).reshape(rows_axis * cols_axis, capacity, 2, width_part)
    label_copies = jnp.broadcast_to(labels[:, None, :], (rows_axis, cols_axis, capacity))
    label_copies = label_copies.reshape(rows_axis * cols_axis, capacity)
    arrived, labels_in = (
        lax.all_to_all(direct, ("row", "col"), split_axis=0, concat_axis=0, tiled=True),
        lax.all_to_all(label_copies, ("row", "col"), split_axis=0, concat_axis=0, tiled=True),
    )
    arrived = arrived.reshape(-1, 2 * width_part)
    labels_in = labels_in.reshape(-1)
    wanted = (jnp.arange(block_rows) + 1).astype(jnp.float32)
    placer = (wanted[:, None] == labels_in[None, :]).astype(jnp.float32)
    placed_rows = exact_dot(placer, arrived).reshape(block_rows, 2, width_part)
    pole_level = pole_index[0].astype(jnp.float32)
    theta_pole = math.pi * (pole_level + 0.5) / POLES
    energy = pole_radius * jnp.cos(theta_pole)
    damping = pole_radius * jnp.sin(theta_pole)
    weight_re = weight_scale * jnp.cos(theta_pole)
    weight_im = weight_scale * jnp.sin(theta_pole)
    panel = jnp.stack(
        [placed_rows[:, 0] - energy * placed_rows[:, 1], -damping * placed_rows[:, 1]], axis=1
    )
    blocks = inverse_blocks[0]
    segment = lax.all_gather(panel, "col", axis=2, tiled=True)
    real_part = exact_dot(blocks[0], segment[:, 0]) - exact_dot(blocks[1], segment[:, 1])
    imag_part = exact_dot(blocks[0], segment[:, 1]) + exact_dot(blocks[1], segment[:, 0])
    partial_value = -jnp.stack([real_part, imag_part], axis=1)
    shares = lax.psum_scatter(partial_value, "row", scatter_dimension=0, tiled=True)
    weighted = weight_re * shares[:, 1] + weight_im * shares[:, 0]
    return lax.psum_scatter(weighted, "pole", scatter_dimension=0, tiled=True)


def solution(mesh):
    in_specs = (
        P(("row", "col"), None),
        P(("row", "col"), None),
        P(("row", "col")),
        P("pole", None, "col", "row"),
        P("pole"),
    )
    out_specs = P(("col", "row", "pole"), None)
    return jax.shard_map(
        per_device, mesh=mesh, in_specs=in_specs, out_specs=out_specs, check_vma=False
    )
```

profile of v0, /device:TPU:2, one launch (start us, length us, event | category | flops | bytes accessed | tf_op | source)
XLA Modules:
  0.0 421.5 jit_solution(12434777764270464368)
XLA Ops:
  7.6 0.7 multiply_add_fusion.1
  8.2 1.0 fusion.17
  10.0 17.3 %all-to-all-start = ((f32[64,1,8]{2,1,0:T(1,128)}), f32[64,1,8]{2,1,0:T(1,128)S(1)}, u32[]{:S(2)}, u32[]{:S(2)}) async-start(f32[64,1,8]{2,1,0:T(1,128)} %bitcast.3), calls=%async_computation | async-start | bytes 65536 | tf_op jit(solution)/shard_map/all_to_all | solution.py:43
  27.3 0.9 maximum_bitcast_fusion
  29.2 1.0 reshape.114
  30.2 6.1 %all-to-all-done = f32[64,1,8]{2,1,0:T(1,128)S(1)} async-done(((f32[64,1,8]{2,1,0:T(1,128)}), f32[64,1,8]{2,1,0:T(1,128)S(1)}, u32[]{:S(2)}, u32[]{:S(2)}) %all-to-all-start) | async-done | bytes 2080 | tf_op jit(solution)/shard_map/all_to_all | solution.py:43
  36.3 5.5 %all-to-all-start.1 = ((f32[64,1,1024]{2,1,0:T(1,128)}), f32[64,1,1024]{2,1,0:T(1,128)S(1)}, u32[]{:S(2)}, u32[]{:S(2)}) async-start(f32[64,1,1024]{2,1,0:T(1,128)} %reshape.114), calls=%async_computation.1 | async-start | bytes 524288 | tf_op jit(solution)/shard_map/all_to_all | solution.py:42
  43.1 0.7 reduce.3
  44.0 11.1 %all-to-all-done.1 = f32[64,1,1024]{2,1,0:T(1,128)S(1)} async-done(((f32[64,1,1024]{2,1,0:T(1,128)}), f32[64,1,1024]{2,1,0:T(1,128)S(1)}, u32[]{:S(2)}, u32[]{:S(2)}) %all-to-all-start.1) | async-done | bytes 262176 | tf_op jit(solution)/shard_map/all_to_all | solution.py:42
  55.6 1.3 reduce.4
  58.2 15.6 %all_gather.3 = f32[256,2,256]{0,2,1:T(8,128)S(1)} all-gather(f32[256,2,64]{0,2,1:T(8,128)S(1)} %pad_maximum_fusion), channel_id=1, replica_groups=mesh['pole'=16,'row'=16,'col'=4] {'col'}, dimensions={2}, use_global_device_ids=true | all-gather | bytes 655360 | tf_op jit(solution)/shard_map/all_gather | solution.py:60
  73.8 1.0 fusion.6
  74.9 1.0 fusion.4
  75.9 1.1 fusion.1
  77.0 1.1 fusion
  78.3 2.4 copy.18
  80.8 1.3 dynamic-slice
  82.7 123.0 %all-reduce.5.cloned.1.call-done = f32[1024,2,256]{2,1,0:T(2,128)} async-done(((f32[1024,2,256]{2,1,0:T(2,128)}), f32[1024,2,256]{2,1,0:T(2,128)}) %all-reduce.5.cloned.1.call-update) | async-done | bytes 2097168
  205.7 1.1 fusion.19
  206.8 0.8 copy.23
  207.6 1.3 dynamic-slice.2
  209.5 203.5 %all-reduce.7.cloned.1.call-done = f32[64,256]{0,1:T(8,128)} async-done(((f32[64,256]{0,1:T(8,128)}), f32[64,256]{0,1:T(8,128)}) %all-reduce.7.cloned.1.call-update) | async-done | bytes 65552
  413.0 1.0 constant_dynamic-slice_fusion
  414.0 0.7 copy.20
  (29 shorter events, 5.6 us)
Async XLA Ops:
  10.0 26.3 %all-to-all-start = ((f32[64,1,8]{2,1,0:T(1,128)}), f32[64,1,8]{2,1,0:T(1,128)S(1)}, u32[]{:S(2)}, u32[]{:S(2)}) async-start(f32[64,1,8]{2,1,0:T(1,128)} %bitcast.3), calls=%async_computation | async-start | bytes 65536 | tf_op jit(solution)/shard_map/all_to_all | solution.py:43
  36.3 18.8 %all-to-all-start.1 = ((f32[64,1,1024]{2,1,0:T(1,128)}), f32[64,1,1024]{2,1,0:T(1,128)S(1)}, u32[]{:S(2)}, u32[]{:S(2)}) async-start(f32[64,1,1024]{2,1,0:T(1,128)} %reshape.114), calls=%async_computation.1 | async-start | bytes 524288 | tf_op jit(solution)/shard_map/all_to_all | solution.py:42
  41.8 163.9 %all-reduce.5.cloned.1.call-start = ((), (), s32[]{:S(2)}) async-start(), calls=%async_computation.2 | async-start | bytes 4194304
  57.0 16.8 %copy-start = (f32[1,2,1024,256]{3,2,1,0:T(8,128)S(1)}, f32[1,2,1024,256]{3,2,1,0:T(8,128)}, u32[]{:S(2)}) copy-start(f32[1,2,1024,256]{3,2,1,0:T(8,128)} %param.8) | copy-start | bytes 6291460
  80.7 332.3 %all-reduce.7.cloned.1.call-start = ((), (), s32[]{:S(2)}) async-start(), calls=%async_computation.3 | async-start | bytes 262144
Sparse Core Ops, SparseCore 0:
  80.8 124.8 all-reduce.4
  209.2 203.7 all-reduce.6
where the time goes:
time: 422 us
  waiting for transfers between devices  344 us (82%)
  starting transfers between devices  22.8 us (5%)
  between operations  15.7 us (4%)
  blocking collectives  15.6 us (4%)
  local copies, waits for them, and re-layouts  11.5 us (3%)
  matrix products  6.29 us (1%)
  other arithmetic  5.93 us (1%)
    unnamed x4, waiting for transfers between devices  327 us
    all_to_all x1, starting transfers between devices, per_device(): lax.all_to_all(label_copies, ('row', 'col'), split_axis=0, concat_axis=0,...  17.3 us
    all_gather x1, blocking collectives, per_device(): segment = lax.all_gather(panel, 'col', axis=2, tiled=True)  15.6 us
    all_to_all x1, waiting for transfers between devices, per_device(): lax.all_to_all(direct, ('row', 'col'), split_axis=0, concat_axis=0, tiled...  11.1 us
  transfers between devices with their start and end apart: 4, of which 4 were waited for; matrix products, arithmetic and copies ran while one was open for 2% of the time, Pallas kernels for 0%

commit v1 on v0

v1 whole, which is shorter than its diff:
```python
import math

import jax
import jax.numpy as jnp
from jax import lax
from jax.experimental import pallas as pl
from jax.experimental.pallas import tpu as pltpu
from jax.sharding import Mesh, PartitionSpec as P

POLES = 64
pole_radius = 1.5
weight_scale = 0.3

LANES = 128
SLOTS = 8
VMEM = pl.BlockSpec(memory_space=pltpu.VMEM)
SMEM = pl.BlockSpec(memory_space=pltpu.SMEM)
PARAMS = pltpu.CompilerParams(vmem_limit_bytes=40 * 1024 * 1024)


def iota(shape, axis):
    return lax.broadcasted_iota(jnp.int32, shape, axis)


def pack_kernel(rows_axis, cols_axis, ham_ref, mar_ref, owner_ref, out_ref):
    share, width = ham_ref.shape
    shift = (4096 // rows_axis).bit_length() - 1
    own_r = jnp.broadcast_to(owner_ref[...].astype(jnp.float32), (share, share))
    own_c = jnp.sum(jnp.where(iota((share, share), 0) == iota((share, share), 1), own_r, 0.0), axis=1, keepdims=True)
    own_c = jnp.broadcast_to(own_c, (share, share)).astype(jnp.int32)
    own_r = own_r.astype(jnp.int32)
    same = (own_r >> shift) == (own_c >> shift)
    first, second = iota((share, share), 0), iota((share, share), 1)
    rank_r = jnp.sum(jnp.where(same & (first < second), 1.0, 0.0), axis=0, keepdims=True)
    rank_c = jnp.sum(jnp.where(same & (second < first), 1.0, 0.0), axis=1, keepdims=True)
    slot_r = (own_r[:1] >> shift) * SLOTS + rank_r.astype(jnp.int32)
    slot_c = (own_c[:, :1] >> shift) * SLOTS + rank_c.astype(jnp.int32)
    total = rows_axis * SLOTS
    packer = jnp.where(iota((total, share), 0) == jnp.broadcast_to(slot_r, (total, share)), 1.0, 0.0)
    within = (own_c[:, :1] & ((1 << shift) - 1)) + 1
    labels = jnp.where(
        iota((share, total), 1) == jnp.broadcast_to(slot_c, (share, total)),
        jnp.broadcast_to(within, (share, total)).astype(jnp.float32),
        0.0,
    )
    labels = jnp.sum(labels, axis=0, keepdims=True)
    chunk = 2 * width // LANES * SLOTS + 1
    for which, ref in enumerate((ham_ref, mar_ref)):
        packed = jnp.dot(packer, ref[...], precision=lax.Precision.HIGHEST, preferred_element_type=jnp.float32)
        for part in range(width // LANES):
            offset = (which * (width // LANES) + part) * SLOTS
            for row in range(rows_axis):
                tile = packed[row * SLOTS : (row + 1) * SLOTS, part * LANES : (part + 1) * LANES]
                for col in range(cols_axis):
                    base = (row * cols_axis + col) * chunk + offset
                    out_ref[base : base + SLOTS, :] = tile
    for target in range(rows_axis * cols_axis):
        base = (target + 1) * chunk - 1
        out_ref[base : base + 1, :] = labels


def split(value):
    high = value.astype(jnp.bfloat16)
    return high, (value - high.astype(jnp.float32)).astype(jnp.bfloat16)


def coefficient_kernel(coef_ref, blocks_ref, high_ref, low_ref):
    rows, depth = blocks_ref.shape[1:]
    piece = rows // 16
    for index in range(16):
        x, core = divmod(index, 2)
        re = blocks_ref[0, index * piece : (index + 1) * piece, :]
        im = blocks_ref[1, index * piece : (index + 1) * piece, :]
        for which in range(2):
            high, low = split(coef_ref[2 * which] * re + coef_ref[2 * which + 1] * im)
            at = (core, slice(x * piece, (x + 1) * piece), slice(which * depth, (which + 1) * depth))
            high_ref[at] = high
            low_ref[at] = low


def product(high, low, panel_high, panel_low):
    dot = lambda a, b: jnp.dot(a, b, preferred_element_type=jnp.float32)
    return dot(high, panel_high) + (dot(low, panel_high) + dot(high, panel_low))


def store_chunks(out_ref, value):
    pairs = value.shape[0] // 8
    left = value[:, :LANES].reshape(pairs, 8, LANES)
    right = value[:, LANES:].reshape(pairs, 8, LANES)
    upper = iota((pairs, 8, LANES), 1) < 4
    out_ref[:, 0] = jnp.where(upper, left, pltpu.roll(right, 4, 1))
    out_ref[:, 1] = jnp.where(upper, pltpu.roll(left, 4, 1), right)


def first_kernel(senders, place_ref, rows_ref, high_ref, low_ref, out_ref, panel_high_ref, panel_low_ref):
    row, core = place_ref[0], place_ref[1]
    chunk = rows_ref.shape[0] // senders
    depth = panel_high_ref.shape[0] // 2
    parts = (chunk - 1) // SLOTS
    labels = rows_ref[pl.ds(chunk - 1, senders, stride=chunk), :]
    lane = iota((senders, LANES), 1)
    wanted = (iota((senders, depth), 1) + 1).astype(jnp.float32)
    places = []
    for slot in range(SLOTS):
        label = jnp.sum(jnp.where(lane == row * SLOTS + slot, labels, 0.0), axis=1, keepdims=True)
        places.append(jnp.where(jnp.broadcast_to(label, (senders, depth)) == wanted, 1.0, 0.0))
    places = jnp.concatenate(places, axis=0).astype(jnp.bfloat16)
    for part in range(parts):
        values = [rows_ref[pl.ds(part * SLOTS + slot, senders, stride=chunk), :] for slot in range(SLOTS)]
        pieces = split(jnp.concatenate(values, axis=0))
        which, left = divmod(part, parts // 2)
        at = (slice(which * depth, (which + 1) * depth), slice(left * LANES, (left + 1) * LANES))
        for ref, piece in zip((panel_high_ref, panel_low_ref), pieces):
            placed = lax.dot_general(places, piece, (((0,), (0,)), ((), ())), preferred_element_type=jnp.float32)
            ref[at] = placed.astype(jnp.bfloat16)
    other = 1 - core
    store_chunks(out_ref, product(high_ref[other], low_ref[other], panel_high_ref[...], panel_low_ref[...]))


def second_kernel(place_ref, high_ref, low_ref, panel_high_ref, panel_low_ref, out_ref):
    core = place_ref[1]
    store_chunks(out_ref, product(high_ref[core], low_ref[core], panel_high_ref[...], panel_low_ref[...]))


def last_kernel(parts_ref, out_ref):
    total = jnp.sum(parts_ref[...], axis=0)
    out_ref[:, :LANES] = total[:4]
    out_ref[:, LANES:] = total[4:]


def per_device(hamiltonian, margin, owner, inverse_blocks, pole_index):
    rows_axis = lax.axis_size("x") * lax.axis_size("core")
    cols_axis = lax.axis_size("yl")
    share, width = hamiltonian.shape
    senders = rows_axis * cols_axis
    chunk = 2 * width // LANES * SLOTS + 1
    packed = pl.pallas_call(
        lambda *refs: pack_kernel(rows_axis, cols_axis, *refs),
        out_shape=jax.ShapeDtypeStruct((senders * chunk, LANES), jnp.float32),
        in_specs=[VMEM] * 3,
        out_specs=VMEM,
        compiler_params=PARAMS,
        name="pack_rows",
    )(hamiltonian, margin, owner.reshape(1, share))
    arrived = lax.all_to_all(
        packed.reshape(senders, 1, chunk * LANES), ("x", "core", "yl"), split_axis=0, concat_axis=0, tiled=True
    ).reshape(senders * chunk, LANES)

    theta = math.pi * (pole_index[0].astype(jnp.float32) + 0.5) / POLES
    energy, damping = pole_radius * jnp.cos(theta), pole_radius * jnp.sin(theta)
    weight_re, weight_im = weight_scale * jnp.cos(theta), weight_scale * jnp.sin(theta)
    shifted_re = weight_re * energy - weight_im * damping
    shifted_im = weight_re * damping + weight_im * energy
    coefs = jnp.stack([-weight_im, -weight_re, shifted_im, shifted_re])
    block_rows, depth = inverse_blocks.shape[2:]
    half = jax.ShapeDtypeStruct((2, block_rows // 2, 2 * depth), jnp.bfloat16)
    high, low = pl.pallas_call(
        coefficient_kernel,
        out_shape=(half, half),
        in_specs=[SMEM, VMEM],
        out_specs=(VMEM, VMEM),
        compiler_params=PARAMS,
        cost_estimate=pl.CostEstimate(flops=4 * block_rows * depth, bytes_accessed=16 * block_rows * depth, transcendentals=0),
        name="left_factors",
    )(coefs, inverse_blocks[0])

    core = lax.axis_index("core")
    place = jnp.stack([lax.axis_index("x") * lax.axis_size("core") + core, core]).astype(jnp.int32)
    chunks = jax.ShapeDtypeStruct((block_rows // 16, 2, 8, LANES), jnp.float32)
    panel = jax.ShapeDtypeStruct((2 * depth, width), jnp.bfloat16)
    sent, panel_high, panel_low = pl.pallas_call(
        lambda *refs: first_kernel(senders, *refs),
        out_shape=(chunks, panel, panel),
        in_specs=[SMEM] + [VMEM] * 3,
        out_specs=(VMEM,) * 3,
        compiler_params=PARAMS,
        name="place_and_multiply",
    )(place, arrived, high, low)
    received = lax.ppermute(sent, "core", [(0, 1), (1, 0)])
    kept = pl.pallas_call(
        second_kernel,
        out_shape=chunks,
        in_specs=[SMEM] + [VMEM] * 4,
        out_specs=VMEM,
        compiler_params=PARAMS,
        cost_estimate=pl.CostEstimate(flops=3 * 2 * block_rows * depth * width, bytes_accessed=2 * block_rows * depth * 4, transcendentals=0),
        name="multiply_own",
    )(place, high, low, panel_high, panel_low)
    both = (kept + received).reshape(block_rows // 8, 8, LANES)
    parts = lax.all_to_all(both, ("x", "yh", "z"), split_axis=0, concat_axis=0, tiled=True)
    return pl.pallas_call(
        last_kernel,
        out_shape=jax.ShapeDtypeStruct((4, width), jnp.float32),
        in_specs=[VMEM],
        out_specs=VMEM,
        compiler_params=PARAMS,
        name="sum_parts",
    )(parts)


def solution(mesh):
    fine = Mesh(mesh.devices.reshape(2, 8, 8, 2, 4), ("yh", "z", "x", "core", "yl"))
    in_specs = (
        P(("x", "core", "yl"), None),
        P(("x", "core", "yl"), None),
        P(("x", "core", "yl")),
        P(("yh", "z"), None, "yl", ("x", "core")),
        P(("yh", "z")),
    )
    out_specs = P(("yl", "x", "core", "yh", "z"), None)
    return jax.shard_map(per_device, mesh=fine, in_specs=in_specs, out_specs=out_specs, check_vma=False)
```

time: 422 us -> 99.4 us (0.24)
  the two profiles are of different devices: /device:TPU:2 before, /device:TPU:1 now
where the time goes in v1:
time: 99.4 us; the launch traced here: 98.1 us
  blocking collectives  39.7 us (40%)
  waiting for transfers between devices  25.1 us (25%)
  starting transfers between devices  22.1 us (22%)
  Pallas kernels  6.25 us (6%)
  local copies, waits for them, and re-layouts  3.93 us (4%)
    all_to_all x1, blocking collectives, per_device(): lax.all_to_all(both, ('x', 'yh', 'z'), split_axis=0, concat_axis=0, tiled...  39.7 us
    all_to_all x1, waiting for transfers between devices, per_device(): lax.all_to_all(packed.reshape(senders, 1, chunk * LANES), ('x', 'core', '...  24.7 us
    all_to_all x1, starting transfers between devices, per_device(): lax.all_to_all(packed.reshape(senders, 1, chunk * LANES), ('x', 'core', '...  18.3 us
    unnamed x8, local copies, waits for them, and re-layouts  3.93 us
    ppermute x1, starting transfers between devices, per_device(): received = lax.ppermute(sent, 'core', [(0, 1), (1, 0)])  3.79 us
  transfers between devices with their start and end apart: 2, of which 2 were waited for; matrix products, arithmetic and copies ran while one was open for 0% of the time, Pallas kernels for 2%

profile of v1, /device:TPU:1, one launch (start us, length us, event | category | flops | bytes accessed | tf_op | source)
XLA Modules:
  0.0 98.1 jit_solution(12858140156351970144)
XLA Ops:
  0.0 0.0 copy-start.1
  0.0 0.8 copy-done.1
  0.8 0.0 copy-start.2
  0.8 0.8 copy-done.2
  1.7 0.0 copy-start.3
  1.7 0.7 copy-done.3
  2.3 1.5 %pack_rows.1 = f32[2112,128]{1,0:T(8,128)} custom-call(f32[64,256]{1,0:T(8,128)S(1)} %copy-done.1, f32[64,256]{1,0:T(8,128)S(1)} %copy-done.2, s32[1,64]{1,0:T(1,128)S(1)} %bitcast.9), custom_call_target="tpu_custom_call" | custom-call | tf_op jit(solution)/shard_map/pack_rows/pallas_call | solution.py:137
  3.8 18.3 %all-to-all-start = ((f32[64,1,4224]{2,1,0:T(1,128)}), f32[64,1,4224]{2,1,0:T(1,128)S(1)}, u32[]{:S(2)}, u32[]{:S(2)}) async-start(f32[64,1,4224]{2,1,0:T(1,128)} %bitcast.4), calls=%async_computation | async-start | bytes 2162688 | tf_op jit(solution)/shard_map/all_to_all | solution.py:145
  22.9 0.1 pad_maximum_fusion.coef_ref
  23.0 0.0 copy-start
  23.0 1.6 %copy-done = f32[1,2,1024,256]{3,2,1,0:T(8,128)S(1)} copy-done((f32[1,2,1024,256]{3,2,1,0:T(8,128)S(1)}, f32[1,2,1024,256]{3,2,1,0:T(8,128)}, u32[]{:S(2)}) %copy-start) | copy-done | bytes 2097176
  24.6 1.0 %left_factors.1 = (bf16[2,512,512]{2,1,0:T(8,128)(2,1)S(1)}, bf16[2,512,512]{2,1,0:T(8,128)(2,1)S(1)}) custom-call(f32[4]{0:T(128)S(1)} %pad_maximum_fusion.coef_ref, f32[2,1024,256]{2,1,0:T(8,128)S(1)} %bitcast.8), custom_call_target="tpu_custom_call" | custom-call | flops 1048576 | bytes 4194304 | tf_op jit(solution)/shard_map/left_factors/pallas_call | solution.py:157
  25.6 0.1 pad_add_fusion.refs_0_.place_ref
  25.6 24.7 %all-to-all-done = f32[64,1,4224]{2,1,0:T(1,128)S(1)} async-done(((f32[64,1,4224]{2,1,0:T(1,128)}), f32[64,1,4224]{2,1,0:T(1,128)S(1)}, u32[]{:S(2)}, u32[]{:S(2)}) %all-to-all-start) | async-done | bytes 1081376 | tf_op jit(solution)/shard_map/all_to_all | solution.py:145
  50.3 1.9 %place_and_multiply.1 = (f32[64,2,8,128]{3,2,1,0:T(8,128)S(1)}, bf16[512,256]{1,0:T(8,128)(2,1)S(1)}, bf16[512,256]{1,0:T(8,128)(2,1)S(1)}) custom-call(s32[2]{0:T(128)S(1)} %pad_add_fusion.refs_0_.place_ref, f32[2112,128]{1,0:T(8,128)S(1)} %bitcast.7, bf16[2,512,512]{2,1,0:T(8,128)(2,1)S(1)} %get-tuple-element.10.refs_2_.high_ref, ...), custom_call_target="tpu_custom_call" | custom-call | tf_op jit(solution)/shard_map/place_and_multiply/pallas_call | solution.py:171
  52.3 3.8 %collective-permute-start = (f32[64,2,8,128]{3,2,1,0:T(8,128)S(1)}, f32[64,2,8,128]{3,2,1,0:T(8,128)S(1)}, u32[]{:S(2)}, u32[]{:S(2)}) collective-permute-start(f32[64,2,8,128]{3,2,1,0:T(8,128)S(1)} %get-tuple-element.14), channel_id=1, source_target_pairs={{0,4},{4,0},{1,5},{5,1},{2,6},{6,2},{3,7},{7,3},{8,12},{12,8},{9,1... | collective-permute-start | bytes 1572872 | tf_op jit(solution)/shard_map/ppermute | solution.py:179
  56.1 1.1 %multiply_own.1 = f32[64,2,8,128]{3,2,1,0:T(8,128)S(1)} custom-call(s32[2]{0:T(128)S(1)} %pad_add_fusion.refs_0_.place_ref, bf16[2,512,512]{2,1,0:T(8,128)(2,1)S(1)} %get-tuple-element.10.refs_2_.high_ref, bf16[2,512,512]{2,1,0:T(8,128)(2,1)S(1)} %get-tuple-element.11.refs_3_.low_ref, bf16[512,256]{1,0:T(8,128)(2,1)S(1)} %get-tuple-element.12.panel_high_ref, ...), custom_call_target="tpu_custom_call" | custom-call | flops 402653184 | bytes 2097152 | tf_op jit(solution)/shard_map/multiply_own/pallas_call | solution.py:180
  57.2 0.4 collective-permute-done
  57.6 0.1 add.16
  57.7 39.7 %all_to_all.10.parts_ref = f32[128,8,128]{2,1,0:T(8,128)S(1)} all-to-all(f32[128,8,128]{2,1,0:T(8,128)S(1)} %bitcast.10), channel_id=1, replica_groups=mesh['yh'=2,'z'=8,'x'=8,'core'=2,'yl'=4] {'x','yh','z'}, dimensions={0} | all-to-all | bytes 1048576 | tf_op jit(solution)/shard_map/all_to_all | solution.py:190
  97.4 0.7 sum_parts.1
Async XLA Ops:
  0.0 0.8 copy-start.1
  0.8 0.8 copy-start.2
  1.7 0.7 copy-start.3
  3.8 46.5 %all-to-all-start = ((f32[64,1,4224]{2,1,0:T(1,128)}), f32[64,1,4224]{2,1,0:T(1,128)S(1)}, u32[]{:S(2)}, u32[]{:S(2)}) async-start(f32[64,1,4224]{2,1,0:T(1,128)} %bitcast.4), calls=%async_computation | async-start | bytes 2162688 | tf_op jit(solution)/shard_map/all_to_all | solution.py:145
  23.0 1.6 %copy-start = (f32[1,2,1024,256]{3,2,1,0:T(8,128)S(1)}, f32[1,2,1024,256]{3,2,1,0:T(8,128)}, u32[]{:S(2)}) copy-start(f32[1,2,1024,256]{3,2,1,0:T(8,128)} %param.8) | copy-start | bytes 6291460
  52.3 5.3 %collective-permute-start = (f32[64,2,8,128]{3,2,1,0:T(8,128)S(1)}, f32[64,2,8,128]{3,2,1,0:T(8,128)S(1)}, u32[]{:S(2)}, u32[]{:S(2)}) collective-permute-start(f32[64,2,8,128]{3,2,1,0:T(8,128)S(1)} %get-tuple-element.14), channel_id=1, source_target_pairs={{0,4},{4,0},{1,5},{5,1},{2,6},{6,2},{3,7},{7,3},{8,12},{12,8},{9,1... | collective-permute-start | bytes 1572872 | tf_op jit(solution)/shard_map/ppermute | solution.py:179

commit v2 on v1

v2 whole, which is shorter than its diff:
```python
import math

import jax
import jax.numpy as jnp
from jax import lax
from jax.experimental import pallas as pl
from jax.experimental.pallas import tpu as pltpu
from jax.sharding import Mesh, PartitionSpec as P

POLES = 64
pole_radius = 1.5
weight_scale = 0.3

LANES = 128
SLOTS = 8
CHUNK = 2 * SLOTS + 1
VMEM = pl.BlockSpec(memory_space=pltpu.VMEM)
SMEM = pl.BlockSpec(memory_space=pltpu.SMEM)
HBM = pl.BlockSpec(memory_space=pltpu.HBM)
PARAMS = pltpu.CompilerParams(vmem_limit_bytes=40 * 1024 * 1024)


def iota(shape, axis):
    return lax.broadcasted_iota(jnp.int32, shape, axis)


def pack_kernel(rows_axis, cols_axis, shift, place_ref, ham_ref, mar_ref, owner_ref, out_ref, ham, mar, owner, sems):
    share = ham.shape[0]
    columns = pl.ds(pl.multiple_of(place_ref[2] * LANES, LANES), LANES)
    copies = [
        pltpu.make_async_copy(owner_ref, owner, sems.at[0]),
        pltpu.make_async_copy(ham_ref.at[:, columns], ham, sems.at[1]),
        pltpu.make_async_copy(mar_ref.at[:, columns], mar, sems.at[2]),
    ]
    for copy in copies:
        copy.start()
    copies[0].wait()
    own_r = jnp.broadcast_to(owner[...].astype(jnp.float32), (share, share))
    own_c = jnp.sum(jnp.where(iota((share, share), 0) == iota((share, share), 1), own_r, 0.0), axis=1, keepdims=True)
    own_c = jnp.broadcast_to(own_c, (share, share)).astype(jnp.int32)
    own_r = own_r.astype(jnp.int32)
    same = (own_r >> shift) == (own_c >> shift)
    first, second = iota((share, share), 0), iota((share, share), 1)
    rank_r = jnp.sum(jnp.where(same & (first < second), 1.0, 0.0), axis=0, keepdims=True)
    rank_c = jnp.sum(jnp.where(same & (second < first), 1.0, 0.0), axis=1, keepdims=True)
    slot_r = (own_r[:1] >> shift) * SLOTS + rank_r.astype(jnp.int32)
    slot_c = (own_c[:, :1] >> shift) * SLOTS + rank_c.astype(jnp.int32)
    total = rows_axis * SLOTS
    packer = jnp.where(iota((total, share), 0) == jnp.broadcast_to(slot_r, (total, share)), 1.0, 0.0)
    within = (own_c[:, :1] & ((1 << shift) - 1)) + 1
    labels = jnp.where(
        iota((share, total), 1) == jnp.broadcast_to(slot_c, (share, total)),
        jnp.broadcast_to(within, (share, total)).astype(jnp.float32),
        0.0,
    )
    labels = jnp.sum(labels, axis=0, keepdims=True)
    for target in range(rows_axis * cols_axis):
        base = (target + 1) * CHUNK - 1
        out_ref[base : base + 1, :] = labels
    for which, ref in enumerate((ham, mar)):
        copies[1 + which].wait()
        packed = jnp.dot(packer, ref[...], precision=lax.Precision.HIGHEST, preferred_element_type=jnp.float32)
        for row in range(rows_axis):
            tile = packed[row * SLOTS : (row + 1) * SLOTS]
            for col in range(cols_axis):
                base = (row * cols_axis + col) * CHUNK + which * SLOTS
                out_ref[base : base + SLOTS, :] = tile


def split(value):
    high = value.astype(jnp.bfloat16)
    return high, (value - high.astype(jnp.float32)).astype(jnp.bfloat16)


def coefficient_kernel(pieces, coef_ref, blocks_ref, first_ref, second_ref, blocks, sems):
    rows, depth = blocks.shape[1:]
    piece = rows // pieces
    half = piece // 2
    copies = []
    for x in range(pieces):
        at = pl.ds(x * piece, piece)
        copies.append(pltpu.make_async_copy(blocks_ref.at[:, at], blocks.at[:, at], sems.at[x]))
        copies[-1].start()
    for x in range(pieces):
        copies[x].wait()
        for core, ref in enumerate((first_ref, second_ref)):
            at = slice(x * piece + core * half, x * piece + (core + 1) * half)
            re, im = blocks[0, at, :], blocks[1, at, :]
            for which in range(2):
                value = coef_ref[2 * which] * re + coef_ref[2 * which + 1] * im
                ref[x * half : (x + 1) * half, which * depth : (which + 1) * depth] = value


def combine_kernel(own_ref, other_ref, high_ref, low_ref):
    for at in range(0, own_ref.shape[0], 64):
        rows = slice(at, at + 64)
        high_ref[rows], low_ref[rows] = split(own_ref[rows] + other_ref[rows])


def product(high, low, panel):
    both = jnp.dot(high, panel, preferred_element_type=jnp.float32)
    return both[:, :LANES] + (both[:, LANES:] + jnp.dot(low, panel[:, :LANES], preferred_element_type=jnp.float32))


def multiply(first, out_ref, which, highs, lows, panel_ref):
    for index in range(2):

        @pl.when(which == index)
        def _():
            out_ref[...] = product(highs[index][...], lows[index][...], panel_ref[...])


def first_kernel(senders, place_ref, rows_ref, high0, low0, high1, low1, out_ref, panel_ref):
    row, core = place_ref[0], place_ref[1]
    depth = panel_ref.shape[0] // 2
    labels = rows_ref[pl.ds(CHUNK - 1, senders, stride=CHUNK), :]
    lane = iota((senders, LANES), 1)
    wanted = (iota((senders, depth), 1) + 1).astype(jnp.float32)
    places = []
    for slot in range(SLOTS):
        label = jnp.sum(jnp.where(lane == row * SLOTS + slot, labels, 0.0), axis=1, keepdims=True)
        places.append(jnp.where(jnp.broadcast_to(label, (senders, depth)) == wanted, 1.0, 0.0))
    places = jnp.concatenate(places, axis=0).astype(jnp.bfloat16)
    for which in range(2):
        values = [rows_ref[pl.ds(which * SLOTS + slot, senders, stride=CHUNK), :] for slot in range(SLOTS)]
        pieces = jnp.concatenate(split(jnp.concatenate(values, axis=0)), axis=1)
        placed = lax.dot_general(places, pieces, (((0,), (0,)), ((), ())), preferred_element_type=jnp.float32)
        panel_ref[which * depth : (which + 1) * depth, :] = placed.astype(jnp.bfloat16)
    multiply(True, out_ref, 1 - core, (high0, high1), (low0, low1), panel_ref)


def second_kernel(place_ref, high0, low0, high1, low1, panel_ref, out_ref):
    multiply(False, out_ref, place_ref[1], (high0, high1), (low0, low1), panel_ref)


def last_kernel(parts_ref, out_ref):
    total = jnp.sum(parts_ref[...].reshape(-1, 8, LANES), axis=0)
    out_ref[:, :LANES] = total[:4]
    out_ref[:, LANES:] = total[4:]


def per_device(hamiltonian, margin, owner, inverse_blocks, pole_index):
    rows_axis = lax.axis_size("x") * lax.axis_size("core")
    cols_axis = lax.axis_size("yl")
    z_axis = lax.axis_size("z")
    share, width = hamiltonian.shape
    block_rows, depth = inverse_blocks.shape[2:]
    senders = rows_axis * cols_axis
    core = lax.axis_index("core")
    row = lax.axis_index("x") * lax.axis_size("core") + core
    place = jnp.stack([row, core, lax.axis_index("z") % 2]).astype(jnp.int32)
    packed = pl.pallas_call(
        lambda *refs: pack_kernel(rows_axis, cols_axis, depth.bit_length() - 1, *refs),
        out_shape=jax.ShapeDtypeStruct((senders * CHUNK, LANES), jnp.float32),
        in_specs=[SMEM, HBM, HBM, HBM],
        out_specs=VMEM,
        scratch_shapes=[
            pltpu.VMEM((share, LANES), jnp.float32),
            pltpu.VMEM((share, LANES), jnp.float32),
            pltpu.VMEM((1, share), jnp.int32),
            pltpu.SemaphoreType.DMA((3,)),
        ],
        compiler_params=PARAMS,
        name="pack_rows",
    )(place, hamiltonian, margin, owner.reshape(1, share))
    arrived = lax.all_to_all(
        packed.reshape(senders, 1, CHUNK * LANES), ("x", "core", "yl"), split_axis=0, concat_axis=0, tiled=True
    ).reshape(senders * CHUNK, LANES)

    theta = math.pi * (pole_index[0].astype(jnp.float32) + 0.5) / POLES
    energy, damping = pole_radius * jnp.cos(theta), pole_radius * jnp.sin(theta)
    weight_re, weight_im = weight_scale * jnp.cos(theta), weight_scale * jnp.sin(theta)
    shifted_re = weight_re * energy - weight_im * damping
    shifted_im = weight_re * damping + weight_im * energy
    coefs = jnp.stack([-weight_im, -weight_re, shifted_im, shifted_re])
    pieces = lax.axis_size("x")
    factor = jax.ShapeDtypeStruct((block_rows // 2, 2 * depth), jnp.float32)
    factors = pl.pallas_call(
        lambda *refs: coefficient_kernel(pieces, *refs),
        out_shape=(factor, factor),
        in_specs=[SMEM, HBM],
        out_specs=(VMEM, VMEM),
        scratch_shapes=[pltpu.VMEM((2, block_rows, depth), jnp.float32), pltpu.SemaphoreType.DMA((pieces,))],
        compiler_params=PARAMS,
        cost_estimate=pl.CostEstimate(flops=6 * block_rows * depth, bytes_accessed=16 * block_rows * depth, transcendentals=0),
        name="left_factors",
    )(coefs, inverse_blocks[0])
    pairs = (
        [(i, i ^ 1) for i in range(z_axis)],
        [(i, (i - 1 if i % 2 == 0 else i + 1) % z_axis) for i in range(z_axis)],
    )
    others = [lax.ppermute(own, "z", pair) for own, pair in zip(factors, pairs)]
    part = jax.ShapeDtypeStruct(factor.shape, jnp.bfloat16)
    summed = []
    for own, other in zip(factors, others):
        summed += pl.pallas_call(
            combine_kernel,
            out_shape=(part, part),
            in_specs=[VMEM] * 2,
            out_specs=(VMEM, VMEM),
            compiler_params=PARAMS,
            cost_estimate=pl.CostEstimate(flops=block_rows * depth * 3, bytes_accessed=12 * block_rows * depth, transcendentals=0),
            name="pair_sums",
        )(own, other)

    chunks = jax.ShapeDtypeStruct((block_rows // 2, LANES), jnp.float32)
    sent, panel = pl.pallas_call(
        lambda *refs: first_kernel(senders, *refs),
        out_shape=(chunks, jax.ShapeDtypeStruct((2 * depth, 2 * LANES), jnp.bfloat16)),
        in_specs=[SMEM] + [VMEM] * 5,
        out_specs=(VMEM,) * 2,
        compiler_params=PARAMS,
        name="place_and_multiply",
    )(place, arrived, *summed)
    received = lax.ppermute(sent, "core", [(0, 1), (1, 0)])
    kept = pl.pallas_call(
        second_kernel,
        out_shape=chunks,
        in_specs=[SMEM] + [VMEM] * 5,
        out_specs=VMEM,
        compiler_params=PARAMS,
        cost_estimate=pl.CostEstimate(flops=3 * block_rows * 2 * depth * LANES, bytes_accessed=4 * block_rows * depth, transcendentals=0),
        name="multiply_own",
    )(place, *summed, panel)
    both = (kept + received).reshape(block_rows // 8, 4, LANES)
    parts = lax.all_to_all(both, ("x", "yh", "z"), split_axis=0, concat_axis=0, tiled=True)
    return pl.pallas_call(
        last_kernel,
        out_shape=jax.ShapeDtypeStruct((4, width), jnp.float32),
        in_specs=[VMEM],
        out_specs=VMEM,
        compiler_params=PARAMS,
        name="sum_parts",
    )(parts.reshape(block_rows // 2, LANES))


def solution(mesh):
    fine = Mesh(mesh.devices.reshape(2, 8, 8, 2, 4), ("yh", "z", "x", "core", "yl"))
    in_specs = (
        P(("x", "core", "yl"), None),
        P(("x", "core", "yl"), None),
        P(("x", "core", "yl")),
        P(("yh", "z"), None, "yl", ("x", "core")),
        P(("yh", "z")),
    )
    out_specs = P(("yl", "x", "core", "yh", "z"), None)
    return jax.shard_map(per_device, mesh=fine, in_specs=in_specs, out_specs=out_specs, check_vma=False)
```

time: 99.4 us -> 102 us (1.026)
  starting transfers between devices: 22.1 us -> 34.1 us
  blocking collectives: 39.7 us -> 31.6 us
  waiting for transfers between devices: 25.1 us -> 23.1 us
    all_to_all x1, waiting for transfers between devices: 24.7 us -> 0.01 us  [per_device(): lax.all_to_all(packed.reshape(senders, 1, CHUNK * LANES), ('x', 'core', '...]
    ppermute x0 -> x2, waiting for transfers between devices: none -> 23 us  [per_device(): others = [lax.ppermute(own, 'z', pair) for own, pair in zip(factors, pairs)]]
    ppermute x0 -> x2, starting transfers between devices: none -> 12.9 us  [per_device(): others = [lax.ppermute(own, 'z', pair) for own, pair in zip(factors, pairs)]]
    all_to_all x1, blocking collectives: 39.7 us -> 31.6 us  [per_device(): lax.all_to_all(both, ('x', 'yh', 'z'), split_axis=0, concat_axis=0, tiled...]
    pallas_call x2 -> x4, Pallas kernels: 2.48 us -> 3.4 us  [the longest x1 2.04 us: per_device(): pl.pallas_call(lambda *refs: pack_kernel(rows_axis, cols_axis, depth.bit_...]
  transfers between devices with their start and end apart: 2 -> 4, of which waited for: 2 -> 3; matrix products, arithmetic and copies ran while one was open for 0% -> 0% of each run, Pallas kernels for 2% -> 2%
where the time goes in v2:
time: 102 us; the launch traced here: 100 us
  starting transfers between devices  34.1 us (33%)
  blocking collectives  31.6 us (31%)
  waiting for transfers between devices  23.1 us (23%)
  Pallas kernels  6.47 us (6%)
  local copies, waits for them, and re-layouts  3.93 us (4%)
    all_to_all x1, blocking collectives, per_device(): lax.all_to_all(both, ('x', 'yh', 'z'), split_axis=0, concat_axis=0, tiled...  31.6 us
    ppermute x2, waiting for transfers between devices, per_device(): others = [lax.ppermute(own, 'z', pair) for own, pair in zip(factors, pairs)]  23 us
    all_to_all x1, starting transfers between devices, per_device(): lax.all_to_all(packed.reshape(senders, 1, CHUNK * LANES), ('x', 'core', '...  18.3 us
    ppermute x2, starting transfers between devices, per_device(): others = [lax.ppermute(own, 'z', pair) for own, pair in zip(factors, pairs)]  12.9 us
    unnamed x8, local copies, waits for them, and re-layouts  3.93 us
    ppermute x1, starting transfers between devices, per_device(): received = lax.ppermute(sent, 'core', [(0, 1), (1, 0)])  2.89 us
  transfers between devices with their start and end apart: 4, of which 3 were waited for; matrix products, arithmetic and copies ran while one was open for 0% of the time, Pallas kernels for 2%

profile of v2, /device:TPU:1, one launch (start us, length us, event | category | flops | bytes accessed | tf_op | source)
XLA Modules:
  0.0 100.2 jit_solution(17038975071648545216)
XLA Ops:
  0.0 0.1 pad_add_fusion.refs_0_.place_ref
  0.1 0.0 copy-start.1
  0.1 0.8 copy-done.1
  0.9 0.0 copy-start.2
  0.9 0.8 copy-done.2
  1.8 0.7 copy-done.3
  2.4 2.0 %pack_rows.1 = f32[1088,128]{1,0:T(8,128)} custom-call(s32[3]{0:T(128)S(1)} %pad_add_fusion.refs_0_.place_ref, f32[64,256]{1,0:T(8,128)S(1)} %copy-done.1, f32[64,256]{1,0:T(8,128)S(1)} %copy-done.2, s32[1,64]{1,0:T(1,128)S(1)} %bitcast.12), custom_call_target="tpu_custom_call" | custom-call | tf_op jit(solution)/shard_map/pack_rows/pallas_call | solution.py:152
  4.5 18.3 %all-to-all-start = ((f32[64,1,2176]{2,1,0:T(1,128)}), f32[64,1,2176]{2,1,0:T(1,128)S(1)}, u32[]{:S(2)}, u32[]{:S(2)}) async-start(f32[64,1,2176]{2,1,0:T(1,128)} %bitcast.5), calls=%async_computation | async-start | bytes 1114112 | tf_op jit(solution)/shard_map/all_to_all | solution.py:166
  23.5 0.1 pad_maximum_fusion.refs_0_
  23.6 1.6 %copy-done = f32[1,2,1024,256]{3,2,1,0:T(8,128)S(1)} copy-done((f32[1,2,1024,256]{3,2,1,0:T(8,128)S(1)}, f32[1,2,1024,256]{3,2,1,0:T(8,128)}, u32[]{:S(2)}) %copy-start) | copy-done | bytes 2097176
  25.2 1.0 %left_factors.1 = (f32[512,512]{1,0:T(8,128)S(1)}, f32[512,512]{1,0:T(8,128)S(1)}) custom-call(f32[4]{0:T(128)S(1)} %pad_maximum_fusion.refs_0_, f32[2,1024,256]{2,1,0:T(8,128)S(1)} %bitcast.10), custom_call_target="tpu_custom_call" | custom-call | flops 1572864 | bytes 4194304 | tf_op jit(solution)/shard_map/left_factors/pallas_call | solution.py:178
  26.2 1.9 %collective-permute-start = (f32[512,512]{1,0:T(8,128)S(1)}, f32[512,512]{1,0:T(8,128)S(1)}, u32[]{:S(2)}, u32[]{:S(2)}) collective-permute-start(f32[512,512]{1,0:T(8,128)S(1)} %get-tuple-element.13.own_ref), channel_id=1, source_target_pairs={{0,64},{64,0},{128,192},{192,128},{256,320},{320,256},{384,448},{4... | collective-permute-start | bytes 3145736 | tf_op jit(solution)/shard_map/ppermute | solution.py:192
  28.2 11.0 %collective-permute-start.1 = (f32[512,512]{1,0:T(8,128)S(1)}, f32[512,512]{1,0:T(8,128)S(1)}, u32[]{:S(2)}, u32[]{:S(2)}) collective-permute-start(f32[512,512]{1,0:T(8,128)S(1)} %get-tuple-element.16.own_ref), channel_id=1, source_target_pairs={{0,448},{64,128},{128,64},{192,256},{256,192},{320,384},{384,320},... | collective-permute-start | bytes 3145736 | tf_op jit(solution)/shard_map/ppermute | solution.py:192
  39.2 13.1 %collective-permute-done.other_ref = f32[512,512]{1,0:T(8,128)S(1)} collective-permute-done((f32[512,512]{1,0:T(8,128)S(1)}, f32[512,512]{1,0:T(8,128)S(1)}, u32[]{:S(2)}, u32[]{:S(2)}) %collective-permute-start) | collective-permute-done | bytes 1048608 | tf_op jit(solution)/shard_map/ppermute | solution.py:192
  52.3 0.2 pair_sums.2
  52.5 9.8 %collective-permute-done.1.other_ref = f32[512,512]{1,0:T(8,128)S(1)} collective-permute-done((f32[512,512]{1,0:T(8,128)S(1)}, f32[512,512]{1,0:T(8,128)S(1)}, u32[]{:S(2)}, u32[]{:S(2)}) %collective-permute-start.1) | collective-permute-done | bytes 1048608 | tf_op jit(solution)/shard_map/ppermute | solution.py:192
  62.3 0.2 pair_sums.3
  62.5 0.0 all-to-all-done
  62.5 1.4 %place_and_multiply.1 = (f32[512,128]{1,0:T(8,128)S(1)}, bf16[512,256]{1,0:T(8,128)(2,1)S(1)}) custom-call(s32[3]{0:T(128)S(1)} %pad_add_fusion.refs_0_.place_ref, f32[1088,128]{1,0:T(8,128)S(1)} %bitcast.9, bf16[512,512]{1,0:T(8,128)(2,1)S(1)} %get-tuple-element.14.refs_2_.high0, bf16[512,512]{1,0:T(8,128)(2,1)S(1)} %get-tuple-element.15.refs_3_.low0, ...), custom_call_target="tpu_custom_call" | custom-call | tf_op jit(solution)/shard_map/place_and_multiply/pallas_call | solution.py:207
  63.9 2.9 %collective-permute-start.2 = (f32[512,128]{1,0:T(8,128)S(1)}, f32[512,128]{1,0:T(8,128)S(1)}, u32[]{:S(2)}, u32[]{:S(2)}) collective-permute-start(f32[512,128]{1,0:T(8,128)S(1)} %get-tuple-element.20), channel_id=1, source_target_pairs={{0,4},{4,0},{1,5},{5,1},{2,6},{6,2},{3,7},{7,3},{8,12},{12,8},{9,1... | collective-permute-start | bytes 786440 | tf_op jit(solution)/shard_map/ppermute | solution.py:215
  66.8 1.0 multiply_own.1
  67.8 0.1 collective-permute-done.2
  68.0 31.6 %all_to_all.10 = f32[128,4,128]{2,1,0:T(4,128)S(1)} all-to-all(f32[128,4,128]{2,1,0:T(4,128)S(1)} %bitcast.13), channel_id=1, replica_groups=mesh['yh'=2,'z'=8,'x'=8,'core'=2,'yl'=4] {'x','yh','z'}, dimensions={0} | all-to-all | bytes 524288 | tf_op jit(solution)/shard_map/all_to_all | solution.py:226
  99.5 0.7 sum_parts.1
  (3 shorter events, 0.0 us)
Async XLA Ops:
  0.1 0.8 copy-start.1
  0.9 0.8 copy-start.2
  1.8 0.7 copy-start.3
  4.5 58.0 %all-to-all-start = ((f32[64,1,2176]{2,1,0:T(1,128)}), f32[64,1,2176]{2,1,0:T(1,128)S(1)}, u32[]{:S(2)}, u32[]{:S(2)}) async-start(f32[64,1,2176]{2,1,0:T(1,128)} %bitcast.5), calls=%async_computation | async-start | bytes 1114112 | tf_op jit(solution)/shard_map/all_to_all | solution.py:166
  23.6 1.6 %copy-start = (f32[1,2,1024,256]{3,2,1,0:T(8,128)S(1)}, f32[1,2,1024,256]{3,2,1,0:T(8,128)}, u32[]{:S(2)}) copy-start(f32[1,2,1024,256]{3,2,1,0:T(8,128)} %param.8) | copy-start | bytes 6291460
  26.2 26.1 %collective-permute-start = (f32[512,512]{1,0:T(8,128)S(1)}, f32[512,512]{1,0:T(8,128)S(1)}, u32[]{:S(2)}, u32[]{:S(2)}) collective-permute-start(f32[512,512]{1,0:T(8,128)S(1)} %get-tuple-element.13.own_ref), channel_id=1, source_target_pairs={{0,64},{64,0},{128,192},{192,128},{256,320},{320,256},{384,448},{4... | collective-permute-start | bytes 3145736 | tf_op jit(solution)/shard_map/ppermute | solution.py:192
  28.2 34.1 %collective-permute-start.1 = (f32[512,512]{1,0:T(8,128)S(1)}, f32[512,512]{1,0:T(8,128)S(1)}, u32[]{:S(2)}, u32[]{:S(2)}) collective-permute-start(f32[512,512]{1,0:T(8,128)S(1)} %get-tuple-element.16.own_ref), channel_id=1, source_target_pairs={{0,448},{64,128},{128,64},{192,256},{256,192},{320,384},{384,320},... | collective-permute-start | bytes 3145736 | tf_op jit(solution)/shard_map/ppermute | solution.py:192
  63.9 4.0 %collective-permute-start.2 = (f32[512,128]{1,0:T(8,128)S(1)}, f32[512,128]{1,0:T(8,128)S(1)}, u32[]{:S(2)}, u32[]{:S(2)}) collective-permute-start(f32[512,128]{1,0:T(8,128)S(1)} %get-tuple-element.20), channel_id=1, source_target_pairs={{0,4},{4,0},{1,5},{5,1},{2,6},{6,2},{3,7},{7,3},{8,12},{12,8},{9,1... | collective-permute-start | bytes 786440 | tf_op jit(solution)/shard_map/ppermute | solution.py:215

commit v3 on v2

--- a/solution.py
+++ b/solution.py
@@ -17,6 +17,7 @@
 VMEM = pl.BlockSpec(memory_space=pltpu.VMEM)
 SMEM = pl.BlockSpec(memory_space=pltpu.SMEM)
 HBM = pl.BlockSpec(memory_space=pltpu.HBM)
+PREPARE = pltpu.CompilerParams(vmem_limit_bytes=50 * 1024 * 1024)
 PARAMS = pltpu.CompilerParams(vmem_limit_bytes=40 * 1024 * 1024)
 
 
@@ -24,14 +25,21 @@
     return lax.broadcasted_iota(jnp.int32, shape, axis)
 
 
-def pack_kernel(rows_axis, cols_axis, shift, place_ref, ham_ref, mar_ref, owner_ref, out_ref, ham, mar, owner, sems):
+def prepare_kernel(rows_axis, cols_axis, pieces, place_ref, coef_ref, ham_ref, mar_ref, owner_ref, blocks_ref, *rest):
+    out_ref, first_ref, second_ref, ham, mar, owner, blocks, sems = rest
     share = ham.shape[0]
+    rows, depth = blocks.shape[1:]
+    shift = depth.bit_length() - 1
     columns = pl.ds(pl.multiple_of(place_ref[2] * LANES, LANES), LANES)
     copies = [
         pltpu.make_async_copy(owner_ref, owner, sems.at[0]),
         pltpu.make_async_copy(ham_ref.at[:, columns], ham, sems.at[1]),
         pltpu.make_async_copy(mar_ref.at[:, columns], mar, sems.at[2]),
     ]
+    piece = rows // pieces
+    for x in range(pieces):
+        at = pl.ds(x * piece, piece)
+        copies.append(pltpu.make_async_copy(blocks_ref.at[:, at], blocks.at[:, at], sems.at[3 + x]))
     for copy in copies:
         copy.start()
     copies[0].wait()
@@ -65,24 +73,9 @@
             for col in range(cols_axis):
                 base = (row * cols_axis + col) * CHUNK + which * SLOTS
                 out_ref[base : base + SLOTS, :] = tile
-
-
-def split(value):
-    high = value.astype(jnp.bfloat16)
-    return high, (value - high.astype(jnp.float32)).astype(jnp.bfloat16)
-
-
-def coefficient_kernel(pieces, coef_ref, blocks_ref, first_ref, second_ref, blocks, sems):
-    rows, depth = blocks.shape[1:]
-    piece = rows // pieces
     half = piece // 2
-    copies = []
     for x in range(pieces):
-        at = pl.ds(x * piece, piece)
-        copies.append(pltpu.make_async_copy(blocks_ref.at[:, at], blocks.at[:, at], sems.at[x]))
-        copies[-1].start()
-    for x in range(pieces):
-        copies[x].wait()
+        copies[3 + x].wait()
         for core, ref in enumerate((first_ref, second_ref)):
             at = slice(x * piece + core * half, x * piece + (core + 1) * half)
             re, im = blocks[0, at, :], blocks[1, at, :]
@@ -91,26 +84,24 @@
                 ref[x * half : (x + 1) * half, which * depth : (which + 1) * depth] = value
 
 
-def combine_kernel(own_ref, other_ref, high_ref, low_ref):
-    for at in range(0, own_ref.shape[0], 64):
-        rows = slice(at, at + 64)
-        high_ref[rows], low_ref[rows] = split(own_ref[rows] + other_ref[rows])
-
-
-def product(high, low, panel):
-    both = jnp.dot(high, panel, preferred_element_type=jnp.float32)
-    return both[:, :LANES] + (both[:, LANES:] + jnp.dot(low, panel[:, :LANES], preferred_element_type=jnp.float32))
-
-
-def multiply(first, out_ref, which, highs, lows, panel_ref):
+def split(value):
+    high = value.astype(jnp.bfloat16)
+    return high, (value - high.astype(jnp.float32)).astype(jnp.bfloat16)
+
+
+def multiply(out_ref, which, owns, others, panel_ref):
+    panel = panel_ref[...]
     for index in range(2):
 
         @pl.when(which == index)
         def _():
-            out_ref[...] = product(highs[index][...], lows[index][...], panel_ref[...])
-
-
-def first_kernel(senders, place_ref, rows_ref, high0, low0, high1, low1, out_ref, panel_ref):
+            high, low = split(owns[index][...] + others[index][...])
+            both = jnp.dot(high, panel, preferred_element_type=jnp.float32)
+            more = jnp.dot(low, panel[:, :LANES], preferred_element_type=jnp.float32)
+            out_ref[...] = both[:, :LANES] + (both[:, LANES:] + more)
+
+
+def first_kernel(senders, place_ref, rows_ref, own0, other0, own1, other1, out_ref, panel_ref):
     row, core = place_ref[0], place_ref[1]
     depth = panel_ref.shape[0] // 2
     labels = rows_ref[pl.ds(CHUNK - 1, senders, stride=CHUNK), :]
@@ -126,11 +117,11 @@
         pieces = jnp.concatenate(split(jnp.concatenate(values, axis=0)), axis=1)
         placed = lax.dot_general(places, pieces, (((0,), (0,)), ((), ())), preferred_element_type=jnp.float32)
         panel_ref[which * depth : (which + 1) * depth, :] = placed.astype(jnp.bfloat16)
-    multiply(True, out_ref, 1 - core, (high0, high1), (low0, low1), panel_ref)
-
-
-def second_kernel(place_ref, high0, low0, high1, low1, panel_ref, out_ref):
-    multiply(False, out_ref, place_ref[1], (high0, high1), (low0, low1), panel_ref)
+    multiply(out_ref, 1 - core, (own0, own1), (other0, other1), panel_ref)
+
+
+def second_kernel(place_ref, own0, other0, own1, other1, panel_ref, out_ref):
+    multiply(out_ref, place_ref[1], (own0, own1), (other0, other1), panel_ref)
 
 
 def last_kernel(parts_ref, out_ref):
@@ -149,24 +140,6 @@
     core = lax.axis_index("core")
     row = lax.axis_index("x") * lax.axis_size("core") + core
     place = jnp.stack([row, core, lax.axis_index("z") % 2]).astype(jnp.int32)
-    packed = pl.pallas_call(
-        lambda *refs: pack_kernel(rows_axis, cols_axis, depth.bit_length() - 1, *refs),
-        out_shape=jax.ShapeDtypeStruct((senders * CHUNK, LANES), jnp.float32),
-        in_specs=[SMEM, HBM, HBM, HBM],
-        out_specs=VMEM,
-        scratch_shapes=[
-            pltpu.VMEM((share, LANES), jnp.float32),
-            pltpu.VMEM((share, LANES), jnp.float32),
-            pltpu.VMEM((1, share), jnp.int32),
-            pltpu.SemaphoreType.DMA((3,)),
-        ],
-        compiler_params=PARAMS,
-        name="pack_rows",
-    )(place, hamiltonian, margin, owner.reshape(1, share))
-    arrived = lax.all_to_all(
-        packed.reshape(senders, 1, CHUNK * LANES), ("x", "core", "yl"), split_axis=0, concat_axis=0, tiled=True
-    ).reshape(senders * CHUNK, LANES)
-
     theta = math.pi * (pole_index[0].astype(jnp.float32) + 0.5) / POLES
     energy, damping = pole_radius * jnp.cos(theta), pole_radius * jnp.sin(theta)
     weight_re, weight_im = weight_scale * jnp.cos(theta), weight_scale * jnp.sin(theta)
@@ -175,34 +148,30 @@
     coefs = jnp.stack([-weight_im, -weight_re, shifted_im, shifted_re])
     pieces = lax.axis_size("x")
     factor = jax.ShapeDtypeStruct((block_rows // 2, 2 * depth), jnp.float32)
-    factors = pl.pallas_call(
-        lambda *refs: coefficient_kernel(pieces, *refs),
-        out_shape=(factor, factor),
-        in_specs=[SMEM, HBM],
-        out_specs=(VMEM, VMEM),
-        scratch_shapes=[pltpu.VMEM((2, block_rows, depth), jnp.float32), pltpu.SemaphoreType.DMA((pieces,))],
-        compiler_params=PARAMS,
-        cost_estimate=pl.CostEstimate(flops=6 * block_rows * depth, bytes_accessed=16 * block_rows * depth, transcendentals=0),
-        name="left_factors",
-    )(coefs, inverse_blocks[0])
+    packed, *factors = pl.pallas_call(
+        lambda *refs: prepare_kernel(rows_axis, cols_axis, pieces, *refs),
+        out_shape=(jax.ShapeDtypeStruct((senders * CHUNK, LANES), jnp.float32), factor, factor),
+        in_specs=[SMEM, SMEM] + [HBM] * 4,
+        out_specs=(VMEM,) * 3,
+        scratch_shapes=[
+            pltpu.VMEM((share, LANES), jnp.float32),
+            pltpu.VMEM((share, LANES), jnp.float32),
+            pltpu.VMEM((1, share), jnp.int32),
+            pltpu.VMEM((2, block_rows, depth), jnp.float32),
+            pltpu.SemaphoreType.DMA((3 + pieces,)),
+        ],
+        compiler_params=PREPARE,
+        name="pack_rows_and_left_factors",
+    )(place, coefs, hamiltonian, margin, owner.reshape(1, share), inverse_blocks[0])
+    arrived = lax.all_to_all(
+        packed.reshape(senders, 1, CHUNK * LANES), ("x", "core", "yl"), split_axis=0, concat_axis=0, tiled=True
+    ).reshape(senders * CHUNK, LANES)
     pairs = (
         [(i, i ^ 1) for i in range(z_axis)],
         [(i, (i - 1 if i % 2 == 0 else i + 1) % z_axis) for i in range(z_axis)],
     )
     others = [lax.ppermute(own, "z", pair) for own, pair in zip(factors, pairs)]
-    part = jax.ShapeDtypeStruct(factor.shape, jnp.bfloat16)
-    summed = []
-    for own, other in zip(factors, others):
-        summed += pl.pallas_call(
-            combine_kernel,
-            out_shape=(part, part),
-            in_specs=[VMEM] * 2,
-            out_specs=(VMEM, VMEM),
-            compiler_params=PARAMS,
-            cost_estimate=pl.CostEstimate(flops=block_rows * depth * 3, bytes_accessed=12 * block_rows * depth, transcendentals=0),
-            name="pair_sums",
-        )(own, other)
-
+    summed = [factors[0], others[0], factors[1], others[1]]
     chunks = jax.ShapeDtypeStruct((block_rows // 2, LANES), jnp.float32)
     sent, panel = pl.pallas_call(
         lambda *refs: first_kernel(senders, *refs),

time: 102 us -> 103 us (level)
    unnamed x8 -> x10, local copies, waits for them, and re-layouts: 3.93 us -> 4.53 us
    pallas_call x4 -> x1, Pallas kernels: 3.4 us -> 2.98 us  [per_device(): pl.pallas_call(lambda *refs: prepare_kernel(rows_axis, cols_axis, pieces,...]
  transfers between devices with their start and end apart: 4 -> 4, of which waited for: 3 -> 3; matrix products, arithmetic and copies ran while one was open for 0% -> 0% of each run, Pallas kernels for 2% -> 1%
where the time goes in v3:
time: 103 us; the launch traced here: 101 us
  starting transfers between devices  34.3 us (33%)
  blocking collectives  31.6 us (31%)
  waiting for transfers between devices  23.2 us (23%)
  Pallas kernels  6.63 us (6%)
  local copies, waits for them, and re-layouts  4.53 us (4%)
    all_to_all x1, blocking collectives, per_device(): lax.all_to_all(both, ('x', 'yh', 'z'), split_axis=0, concat_axis=0, tiled...  31.6 us
    ppermute x2, waiting for transfers between devices, per_device(): others = [lax.ppermute(own, 'z', pair) for own, pair in zip(factors, pairs)]  23 us
    all_to_all x1, starting transfers between devices, per_device(): lax.all_to_all(packed.reshape(senders, 1, CHUNK * LANES), ('x', 'core', '...  19 us
    ppermute x2, starting transfers between devices, per_device(): others = [lax.ppermute(own, 'z', pair) for own, pair in zip(factors, pairs)]  12.3 us
    unnamed x10, local copies, waits for them, and re-layouts  4.53 us
    ppermute x1, starting transfers between devices, per_device(): received = lax.ppermute(sent, 'core', [(0, 1), (1, 0)])  2.99 us
    pallas_call x1, Pallas kernels, per_device(): pl.pallas_call(lambda *refs: prepare_kernel(rows_axis, cols_axis, pieces,...  2.98 us
  transfers between devices with their start and end apart: 4, of which 3 were waited for; matrix products, arithmetic and copies ran while one was open for 0% of the time, Pallas kernels for 1%

profile of v3, /device:TPU:1, one launch (start us, length us, event | category | flops | bytes accessed | tf_op | source)
XLA Modules:
  0.0 101.3 jit_solution(8952257794499763879)
XLA Ops:
  0.8 0.1 pad_add_fusion.refs_0_.place_ref
  0.9 0.1 pad_maximum_fusion.refs_1_
  1.0 0.0 copy-start.2
  1.0 0.8 copy-done.2
  1.8 0.0 copy-start.3
  1.8 0.8 copy-done.3
  2.7 0.0 copy-start.4
  2.7 0.7 copy-done.4
  3.3 3.0 %pack_rows_and_left_factors.1 = (f32[1088,128]{1,0:T(8,128)}, f32[512,512]{1,0:T(8,128)S(1)}, f32[512,512]{1,0:T(8,128)S(1)}) custom-call(s32[3]{0:T(128)S(1)} %pad_add_fusion.refs_0_.place_ref, f32[4]{0:T(128)S(1)} %pad_maximum_fusion.refs_1_, f32[64,256]{1,0:T(8,128)S(1)} %copy-done.2, f32[64,256]{1,0:T(8,128)S(1)} %copy-done.3, s32[1,64]{1,0:T(1,128)S(1)} %bitcast.10, ...), custom_call_target="tpu_custom_call" | custom-call | tf_op jit(solution)/shard_map/pack_rows_and_left_factors/pallas_call | solution.py:151
  6.3 19.0 %all-to-all-start = ((f32[64,1,2176]{2,1,0:T(1,128)}), f32[64,1,2176]{2,1,0:T(1,128)}, u32[]{:S(2)}, u32[]{:S(2)}) async-start(f32[64,1,2176]{2,1,0:T(1,128)} %bitcast.5), calls=%async_computation | async-start | bytes 1114112 | tf_op jit(solution)/shard_map/all_to_all | solution.py:166
  25.3 1.9 %collective-permute-start = (f32[512,512]{1,0:T(8,128)S(1)}, f32[512,512]{1,0:T(8,128)S(1)}, u32[]{:S(2)}, u32[]{:S(2)}) collective-permute-start(f32[512,512]{1,0:T(8,128)S(1)} %get-tuple-element.10.refs_2_.own0), channel_id=1, source_target_pairs={{0,64},{64,0},{128,192},{192,128},{256,320},{320,256},{384,448},{4... | collective-permute-start | bytes 3145736 | tf_op jit(solution)/shard_map/ppermute | solution.py:173
  27.3 10.4 %collective-permute-start.1 = (f32[512,512]{1,0:T(8,128)S(1)}, f32[512,512]{1,0:T(8,128)S(1)}, u32[]{:S(2)}, u32[]{:S(2)}) collective-permute-start(f32[512,512]{1,0:T(8,128)S(1)} %get-tuple-element.11.refs_4_.own1), channel_id=1, source_target_pairs={{0,448},{64,128},{128,64},{192,256},{256,192},{320,384},{384,320},... | collective-permute-start | bytes 3145736 | tf_op jit(solution)/shard_map/ppermute | solution.py:173
  37.7 13.7 %collective-permute-done.refs_3_.other0 = f32[512,512]{1,0:T(8,128)S(1)} collective-permute-done((f32[512,512]{1,0:T(8,128)S(1)}, f32[512,512]{1,0:T(8,128)S(1)}, u32[]{:S(2)}, u32[]{:S(2)}) %collective-permute-start) | collective-permute-done | bytes 1048608 | tf_op jit(solution)/shard_map/ppermute | solution.py:173
  51.3 9.4 %collective-permute-done.1.refs_5_.other1 = f32[512,512]{1,0:T(8,128)S(1)} collective-permute-done((f32[512,512]{1,0:T(8,128)S(1)}, f32[512,512]{1,0:T(8,128)S(1)}, u32[]{:S(2)}, u32[]{:S(2)}) %collective-permute-start.1) | collective-permute-done | bytes 1048608 | tf_op jit(solution)/shard_map/ppermute | solution.py:173
  60.7 0.0 copy-start
  60.7 1.0 copy-done
  61.7 0.0 all-to-all-done
  61.7 1.2 %copy-done.1 = f32[512,512]{1,0:T(8,128)S(1)} copy-done((f32[512,512]{1,0:T(8,128)S(1)}, f32[512,512]{1,0:T(8,128)}, u32[]{:S(2)}) %copy-start.1) | copy-done | bytes 1048600
  62.9 2.0 %place_and_multiply.1 = (f32[512,128]{1,0:T(8,128)S(1)}, bf16[512,256]{1,0:T(8,128)(2,1)S(1)}) custom-call(s32[3]{0:T(128)S(1)} %pad_add_fusion.refs_0_.place_ref, f32[1088,128]{1,0:T(8,128)} %bitcast.6.refs_1_, f32[512,512]{1,0:T(8,128)S(1)} %get-tuple-element.10.refs_2_.own0, f32[512,512]{1,0:T(8,128)S(1)} %collective-permute-done.refs_3_.other0, ...), custom_call_target="tpu_custom_call" | custom-call | tf_op jit(solution)/shard_map/place_and_multiply/pallas_call | solution.py:176
  64.9 3.0 %collective-permute-start.2 = (f32[512,128]{1,0:T(8,128)S(1)}, f32[512,128]{1,0:T(8,128)S(1)}, u32[]{:S(2)}, u32[]{:S(2)}) collective-permute-start(f32[512,128]{1,0:T(8,128)S(1)} %get-tuple-element.14), channel_id=1, source_target_pairs={{0,4},{4,0},{1,5},{5,1},{2,6},{6,2},{3,7},{7,3},{8,12},{12,8},{9,1... | collective-permute-start | bytes 786440 | tf_op jit(solution)/shard_map/ppermute | solution.py:184
  67.9 1.0 multiply_own.1
  68.9 0.1 collective-permute-done.2
  69.1 31.6 %all_to_all.10 = f32[128,4,128]{2,1,0:T(4,128)S(1)} all-to-all(f32[128,4,128]{2,1,0:T(4,128)S(1)} %bitcast.12), channel_id=1, replica_groups=mesh['yh'=2,'z'=8,'x'=8,'core'=2,'yl'=4] {'x','yh','z'}, dimensions={0} | all-to-all | bytes 524288 | tf_op jit(solution)/shard_map/all_to_all | solution.py:195
  100.6 0.7 sum_parts.1
  (2 shorter events, 0.0 us)
Async XLA Ops:
  1.0 0.8 copy-start.2
  1.8 0.8 copy-start.3
  2.7 0.7 copy-start.4
  6.3 55.4 %all-to-all-start = ((f32[64,1,2176]{2,1,0:T(1,128)}), f32[64,1,2176]{2,1,0:T(1,128)}, u32[]{:S(2)}, u32[]{:S(2)}) async-start(f32[64,1,2176]{2,1,0:T(1,128)} %bitcast.5), calls=%async_computation | async-start | bytes 1114112 | tf_op jit(solution)/shard_map/all_to_all | solution.py:166
  25.3 26.0 %collective-permute-start = (f32[512,512]{1,0:T(8,128)S(1)}, f32[512,512]{1,0:T(8,128)S(1)}, u32[]{:S(2)}, u32[]{:S(2)}) collective-permute-start(f32[512,512]{1,0:T(8,128)S(1)} %get-tuple-element.10.refs_2_.own0), channel_id=1, source_target_pairs={{0,64},{64,0},{128,192},{192,128},{256,320},{320,256},{384,448},{4... | collective-permute-start | bytes 3145736 | tf_op jit(solution)/shard_map/ppermute | solution.py:173
  27.3 33.5 %collective-permute-start.1 = (f32[512,512]{1,0:T(8,128)S(1)}, f32[512,512]{1,0:T(8,128)S(1)}, u32[]{:S(2)}, u32[]{:S(2)}) collective-permute-start(f32[512,512]{1,0:T(8,128)S(1)} %get-tuple-element.11.refs_4_.own1), channel_id=1, source_target_pairs={{0,448},{64,128},{128,64},{192,256},{256,192},{320,384},{384,320},... | collective-permute-start | bytes 3145736 | tf_op jit(solution)/shard_map/ppermute | solution.py:173
  60.7 1.0 copy-start
  61.7 1.2 %copy-start.1 = (f32[512,512]{1,0:T(8,128)S(1)}, f32[512,512]{1,0:T(8,128)}, u32[]{:S(2)}) copy-start(f32[512,512]{1,0:T(8,128)} %copy-done) | copy-start | bytes 3145732
  64.9 4.1 %collective-permute-start.2 = (f32[512,128]{1,0:T(8,128)S(1)}, f32[512,128]{1,0:T(8,128)S(1)}, u32[]{:S(2)}, u32[]{:S(2)}) collective-permute-start(f32[512,128]{1,0:T(8,128)S(1)} %get-tuple-element.14), channel_id=1, source_target_pairs={{0,4},{4,0},{1,5},{5,1},{2,6},{6,2},{3,7},{7,3},{8,12},{12,8},{9,1... | collective-permute-start | bytes 786440 | tf_op jit(solution)/shard_map/ppermute | solution.py:184

commit v4 on v1

--- a/solution.py
+++ b/solution.py
@@ -64,23 +64,27 @@
     return high, (value - high.astype(jnp.float32)).astype(jnp.bfloat16)
 
 
-def coefficient_kernel(coef_ref, blocks_ref, high_ref, low_ref):
+def left_kernel(place_ref, coef_ref, blocks_ref, *out_refs):
     rows, depth = blocks_ref.shape[1:]
     piece = rows // 16
+    odd_here = place_ref[2] == 1
     for index in range(16):
         x, core = divmod(index, 2)
         re = blocks_ref[0, index * piece : (index + 1) * piece, :]
         im = blocks_ref[1, index * piece : (index + 1) * piece, :]
         for which in range(2):
-            high, low = split(coef_ref[2 * which] * re + coef_ref[2 * which + 1] * im)
-            at = (core, slice(x * piece, (x + 1) * piece), slice(which * depth, (which + 1) * depth))
-            high_ref[at] = high
-            low_ref[at] = low
-
-
-def product(high, low, panel_high, panel_low):
-    dot = lambda a, b: jnp.dot(a, b, preferred_element_type=jnp.float32)
-    return dot(high, panel_high) + (dot(low, panel_high) + dot(high, panel_low))
+            value = (coef_ref[2 * which] * re + coef_ref[2 * which + 1] * im).reshape(piece // 16, 2, 8, depth)
+            first, second = value[:, 0], value[:, 1]
+            upper = iota(first.shape, 1) < 4
+            even = jnp.where(upper, first, pltpu.roll(second, 4, 1)).reshape(piece // 2, depth)
+            odd = jnp.where(upper, pltpu.roll(first, 4, 1), second).reshape(piece // 2, depth)
+            at = (slice(x * piece // 2, (x + 1) * piece // 2), slice(which * depth, (which + 1) * depth))
+            out_refs[core][at] = jnp.where(odd_here, odd, even)
+            out_refs[2 + core][at] = jnp.where(odd_here, even, odd)
+
+
+def pair_kernel(own_ref, other_ref, high_ref, low_ref):
+    high_ref[...], low_ref[...] = split(own_ref[...] + other_ref[...])
 
 
 def store_chunks(out_ref, value):
@@ -92,7 +96,17 @@
     out_ref[:, 1] = jnp.where(upper, pltpu.roll(left, 4, 1), right)
 
 
-def first_kernel(senders, place_ref, rows_ref, high_ref, low_ref, out_ref, panel_high_ref, panel_low_ref):
+def multiply(out_ref, which, highs, lows, panel_high_ref, panel_low_ref):
+    dot = lambda a, b: jnp.dot(a, b, preferred_element_type=jnp.float32)
+    for index in range(2):
+
+        @pl.when(which == index)
+        def _():
+            high, low, panel = highs[index][...], lows[index][...], panel_high_ref[...]
+            store_chunks(out_ref, dot(high, panel) + (dot(low, panel) + dot(high, panel_low_ref[...])))
+
+
+def first_kernel(senders, place_ref, rows_ref, high0, low0, high1, low1, out_ref, panel_high_ref, panel_low_ref):
     row, core = place_ref[0], place_ref[1]
     chunk = rows_ref.shape[0] // senders
     depth = panel_high_ref.shape[0] // 2
@@ -113,13 +127,11 @@
         for ref, piece in zip((panel_high_ref, panel_low_ref), pieces):
             placed = lax.dot_general(places, piece, (((0,), (0,)), ((), ())), preferred_element_type=jnp.float32)
             ref[at] = placed.astype(jnp.bfloat16)
-    other = 1 - core
-    store_chunks(out_ref, product(high_ref[other], low_ref[other], panel_high_ref[...], panel_low_ref[...]))
-
-
-def second_kernel(place_ref, high_ref, low_ref, panel_high_ref, panel_low_ref, out_ref):
-    core = place_ref[1]
-    store_chunks(out_ref, product(high_ref[core], low_ref[core], panel_high_ref[...], panel_low_ref[...]))
+    multiply(out_ref, 1 - core, (high0, high1), (low0, low1), panel_high_ref, panel_low_ref)
+
+
+def second_kernel(place_ref, high0, low0, high1, low1, panel_high_ref, panel_low_ref, out_ref):
+    multiply(out_ref, place_ref[1], (high0, high1), (low0, low1), panel_high_ref, panel_low_ref)
 
 
 def last_kernel(parts_ref, out_ref):
@@ -153,41 +165,59 @@
     shifted_im = weight_re * damping + weight_im * energy
     coefs = jnp.stack([-weight_im, -weight_re, shifted_im, shifted_re])
     block_rows, depth = inverse_blocks.shape[2:]
-    half = jax.ShapeDtypeStruct((2, block_rows // 2, 2 * depth), jnp.bfloat16)
-    high, low = pl.pallas_call(
-        coefficient_kernel,
-        out_shape=(half, half),
-        in_specs=[SMEM, VMEM],
-        out_specs=(VMEM, VMEM),
+    core = lax.axis_index("core")
+    place = jnp.stack(
+        [lax.axis_index("x") * lax.axis_size("core") + core, core, lax.axis_index("zp")]
+    ).astype(jnp.int32)
+    factor = jax.ShapeDtypeStruct((block_rows // 4, 2 * depth), jnp.float32)
+    factors = pl.pallas_call(
+        left_kernel,
+        out_shape=(factor,) * 4,
+        in_specs=[SMEM, SMEM, VMEM],
+        out_specs=(VMEM,) * 4,
         compiler_params=PARAMS,
         cost_estimate=pl.CostEstimate(flops=4 * block_rows * depth, bytes_accessed=16 * block_rows * depth, transcendentals=0),
         name="left_factors",
-    )(coefs, inverse_blocks[0])
-
-    core = lax.axis_index("core")
-    place = jnp.stack([lax.axis_index("x") * lax.axis_size("core") + core, core]).astype(jnp.int32)
-    chunks = jax.ShapeDtypeStruct((block_rows // 16, 2, 8, LANES), jnp.float32)
+    )(place, coefs, inverse_blocks[0])
+    z_axis = lax.axis_size("zq") * lax.axis_size("zp")
+    pairs = (
+        [(i, i ^ 1) for i in range(z_axis)],
+        [(i, (i - 1 if i % 2 == 0 else i + 1) % z_axis) for i in range(z_axis)],
+    )
+    part = jax.ShapeDtypeStruct(factor.shape, jnp.bfloat16)
+    summed = []
+    for own, sent, pair in zip(factors[:2], factors[2:], pairs):
+        summed += pl.pallas_call(
+            pair_kernel,
+            out_shape=(part, part),
+            in_specs=[VMEM] * 2,
+            out_specs=(VMEM, VMEM),
+            compiler_params=PARAMS,
+            cost_estimate=pl.CostEstimate(flops=block_rows * depth, bytes_accessed=6 * block_rows * depth, transcendentals=0),
+            name="pair_sums",
+        )(own, lax.ppermute(sent, ("zq", "zp"), pair))
+    chunks = jax.ShapeDtypeStruct((block_rows // 32, 2, 8, LANES), jnp.float32)
     panel = jax.ShapeDtypeStruct((2 * depth, width), jnp.bfloat16)
     sent, panel_high, panel_low = pl.pallas_call(
         lambda *refs: first_kernel(senders, *refs),
         out_shape=(chunks, panel, panel),
-        in_specs=[SMEM] + [VMEM] * 3,
+        in_specs=[SMEM] + [VMEM] * 5,
         out_specs=(VMEM,) * 3,
         compiler_params=PARAMS,
         name="place_and_multiply",
-    )(place, arrived, high, low)
+    )(place, arrived, *summed)
     received = lax.ppermute(sent, "core", [(0, 1), (1, 0)])
     kept = pl.pallas_call(
         second_kernel,
         out_shape=chunks,
-        in_specs=[SMEM] + [VMEM] * 4,
+        in_specs=[SMEM] + [VMEM] * 6,
         out_specs=VMEM,
         compiler_params=PARAMS,
-        cost_estimate=pl.CostEstimate(flops=3 * 2 * block_rows * depth * width, bytes_accessed=2 * block_rows * depth * 4, transcendentals=0),
+        cost_estimate=pl.CostEstimate(flops=3 * block_rows * depth * width, bytes_accessed=block_rows * depth * 4, transcendentals=0),
         name="multiply_own",
-    )(place, high, low, panel_high, panel_low)
-    both = (kept + received).reshape(block_rows // 8, 8, LANES)
-    parts = lax.all_to_all(both, ("x", "yh", "z"), split_axis=0, concat_axis=0, tiled=True)
+    )(place, *summed, panel_high, panel_low)
+    both = (kept + received).reshape(block_rows // 16, 8, LANES)
+    parts = lax.all_to_all(both, ("x", "yh", "zq"), split_axis=0, concat_axis=0, tiled=True)
     return pl.pallas_call(
         last_kernel,
         out_shape=jax.ShapeDtypeStruct((4, width), jnp.float32),
@@ -199,13 +229,13 @@
 
 
 def solution(mesh):
-    fine = Mesh(mesh.devices.reshape(2, 8, 8, 2, 4), ("yh", "z", "x", "core", "yl"))
+    fine = Mesh(mesh.devices.reshape(2, 4, 2, 8, 2, 4), ("yh", "zq", "zp", "x", "core", "yl"))
     in_specs = (
         P(("x", "core", "yl"), None),
         P(("x", "core", "yl"), None),
         P(("x", "core", "yl")),
-        P(("yh", "z"), None, "yl", ("x", "core")),
-        P(("yh", "z")),
+        P(("yh", "zq", "zp"), None, "yl", ("x", "core")),
+        P(("yh", "zq", "zp")),
     )
-    out_specs = P(("yl", "x", "core", "yh", "z"), None)
+    out_specs = P(("yl", "x", "core", "yh", "zq", "zp"), None)
     return jax.shard_map(per_device, mesh=fine, in_specs=in_specs, out_specs=out_specs, check_vma=False)

time: 99.4 us -> 91.7 us (0.923)
  starting transfers between devices: 22.1 us -> 35.1 us
  waiting for transfers between devices: 25.1 us -> 13.4 us
  blocking collectives: 39.7 us -> 32.7 us
  local copies, waits for them, and re-layouts: 3.93 us -> 2.34 us
    all_to_all x1, waiting for transfers between devices: 24.7 us -> 0.62 us  [per_device(): lax.all_to_all(packed.reshape(senders, 1, chunk * LANES), ('x', 'core', '...]
    ppermute x0 -> x2, starting transfers between devices: none -> 12.9 us  [per_device(): lax.ppermute(sent, ('zq', 'zp'), pair)]
    ppermute x0 -> x2, waiting for transfers between devices: none -> 12.6 us  [per_device(): lax.ppermute(sent, ('zq', 'zp'), pair)]
    all_to_all x1, blocking collectives: 39.7 us -> 32.7 us  [per_device(): lax.all_to_all(both, ('x', 'yh', 'zq'), split_axis=0, concat_axis=0, tile...]
    unnamed x8, local copies, waits for them, and re-layouts: 3.93 us -> 2.34 us
  transfers between devices with their start and end apart: 2 -> 4, of which waited for: 2 -> 4; matrix products, arithmetic and copies ran while one was open for 0% -> 0% of each run, Pallas kernels for 2% -> 2%
where the time goes in v4:
time: 91.7 us; the launch traced here: 90.6 us
  starting transfers between devices  35.1 us (38%)
  blocking collectives  32.7 us (36%)
  waiting for transfers between devices  13.4 us (15%)
  Pallas kernels  6.01 us (7%)
  local copies, waits for them, and re-layouts  2.34 us (3%)
    all_to_all x1, blocking collectives, per_device(): lax.all_to_all(both, ('x', 'yh', 'zq'), split_axis=0, concat_axis=0, tile...  32.7 us
    all_to_all x1, starting transfers between devices, per_device(): lax.all_to_all(packed.reshape(senders, 1, chunk * LANES), ('x', 'core', '...  18.4 us
    ppermute x2, starting transfers between devices, per_device(): lax.ppermute(sent, ('zq', 'zp'), pair)  12.9 us
    ppermute x2, waiting for transfers between devices, per_device(): lax.ppermute(sent, ('zq', 'zp'), pair)  12.6 us
    ppermute x1, starting transfers between devices, per_device(): received = lax.ppermute(sent, 'core', [(0, 1), (1, 0)])  3.79 us
    unnamed x8, local copies, waits for them, and re-layouts  2.34 us
  transfers between devices with their start and end apart: 4, of which 4 were waited for; matrix products, arithmetic and copies ran while one was open for 0% of the time, Pallas kernels for 2%

profile of v4, /device:TPU:1, one launch (start us, length us, event | category | flops | bytes accessed | tf_op | source)
XLA Modules:
  0.0 90.6 jit_solution(17320395694113548611)
XLA Ops:
  0.0 0.0 copy-start.1
  0.0 0.8 copy-done.1
  0.8 0.0 copy-start.2
  0.8 0.8 copy-done.2
  1.7 0.7 copy-done.3
  2.3 1.5 %pack_rows.1 = f32[2112,128]{1,0:T(8,128)} custom-call(f32[64,256]{1,0:T(8,128)S(1)} %copy-done.1, f32[64,256]{1,0:T(8,128)S(1)} %copy-done.2, s32[1,64]{1,0:T(1,128)S(1)} %bitcast.10), custom_call_target="tpu_custom_call" | custom-call | tf_op jit(solution)/shard_map/pack_rows/pallas_call | solution.py:149
  3.8 18.4 %all-to-all-start = ((f32[64,1,4224]{2,1,0:T(1,128)}), f32[64,1,4224]{2,1,0:T(1,128)S(1)}, u32[]{:S(2)}, u32[]{:S(2)}) async-start(f32[64,1,4224]{2,1,0:T(1,128)} %bitcast.5), calls=%async_computation | async-start | bytes 2162688 | tf_op jit(solution)/shard_map/all_to_all | solution.py:157
  23.0 0.1 pad_add_fusion.place_ref.refs_0_
  23.1 0.1 pad_maximum_fusion.coef_ref
  23.2 0.0 copy-done
  23.2 1.0 %left_factors.1 = (f32[256,512]{1,0:T(8,128)S(1)}, f32[256,512]{1,0:T(8,128)S(1)}, f32[256,512]{1,0:T(8,128)S(1)}, f32[256,512]{1,0:T(8,128)S(1)}) custom-call(s32[3]{0:T(128)S(1)} %pad_add_fusion.place_ref.refs_0_, f32[4]{0:T(128)S(1)} %pad_maximum_fusion.coef_ref, f32[2,1024,256]{2,1,0:T(8,128)S(1)} %bitcast.9), custom_call_target="tpu_custom_call" | custom-call | flops 1048576 | bytes 4194304 | tf_op jit(solution)/shard_map/left_factors/pallas_call | solution.py:173
  24.2 11.0 %collective-permute-start.1 = (f32[256,512]{1,0:T(8,128)S(1)}, f32[256,512]{1,0:T(8,128)S(1)}, u32[]{:S(2)}, u32[]{:S(2)}) collective-permute-start(f32[256,512]{1,0:T(8,128)S(1)} %get-tuple-element.21), channel_id=1, source_target_pairs={{0,448},{64,128},{128,64},{192,256},{256,192},{320,384},{384,320},... | collective-permute-start | bytes 1572872 | tf_op jit(solution)/shard_map/ppermute | solution.py:198
  35.2 1.9 %collective-permute-start = (f32[256,512]{1,0:T(8,128)S(1)}, f32[256,512]{1,0:T(8,128)S(1)}, u32[]{:S(2)}, u32[]{:S(2)}) collective-permute-start(f32[256,512]{1,0:T(8,128)S(1)} %get-tuple-element.17), channel_id=1, source_target_pairs={{0,64},{64,0},{128,192},{192,128},{256,320},{320,256},{384,448},{4... | collective-permute-start | bytes 1572872 | tf_op jit(solution)/shard_map/ppermute | solution.py:198
  37.1 10.0 %collective-permute-done.1.other_ref = f32[256,512]{1,0:T(8,128)S(1)} collective-permute-done((f32[256,512]{1,0:T(8,128)S(1)}, f32[256,512]{1,0:T(8,128)S(1)}, u32[]{:S(2)}, u32[]{:S(2)}) %collective-permute-start.1) | collective-permute-done | bytes 524320 | tf_op jit(solution)/shard_map/ppermute | solution.py:198
  47.0 0.1 pair_sums.3
  47.1 2.6 %collective-permute-done.other_ref = f32[256,512]{1,0:T(8,128)S(1)} collective-permute-done((f32[256,512]{1,0:T(8,128)S(1)}, f32[256,512]{1,0:T(8,128)S(1)}, u32[]{:S(2)}, u32[]{:S(2)}) %collective-permute-start) | collective-permute-done | bytes 524320 | tf_op jit(solution)/shard_map/ppermute | solution.py:198
  49.8 0.1 pair_sums.2
  49.9 0.6 all-to-all-done
  50.5 1.8 %place_and_multiply.1 = (f32[32,2,8,128]{3,2,1,0:T(8,128)S(1)}, bf16[512,256]{1,0:T(8,128)(2,1)S(1)}, bf16[512,256]{1,0:T(8,128)(2,1)S(1)}) custom-call(s32[3]{0:T(128)S(1)} %pad_add_fusion.place_ref.refs_0_, f32[2112,128]{1,0:T(8,128)S(1)} %bitcast.8, bf16[256,512]{1,0:T(8,128)(2,1)S(1)} %get-tuple-element.18.refs_2_.high0, ...), custom_call_target="tpu_custom_call" | custom-call | tf_op jit(solution)/shard_map/place_and_multiply/pallas_call | solution.py:201
  52.3 3.8 %collective-permute-start.2 = (f32[32,2,8,128]{3,2,1,0:T(8,128)S(1)}, f32[32,2,8,128]{3,2,1,0:T(8,128)S(1)}, u32[]{:S(2)}, u32[]{:S(2)}) collective-permute-start(f32[32,2,8,128]{3,2,1,0:T(8,128)S(1)} %get-tuple-element.26), channel_id=1, source_target_pairs={{0,4},{4,0},{1,5},{5,1},{2,6},{6,2},{3,7},{7,3},{8,12},{12,8},{9,1... | collective-permute-start | bytes 786440 | tf_op jit(solution)/shard_map/ppermute | solution.py:209
  56.1 0.9 %multiply_own.1 = f32[32,2,8,128]{3,2,1,0:T(8,128)S(1)} custom-call(s32[3]{0:T(128)S(1)} %pad_add_fusion.place_ref.refs_0_, bf16[256,512]{1,0:T(8,128)(2,1)S(1)} %get-tuple-element.18.refs_2_.high0, bf16[256,512]{1,0:T(8,128)(2,1)S(1)} %get-tuple-element.19.refs_3_.low0, bf16[256,512]{1,0:T(8,128)(2,1)S(1)} %get-tuple-element.22.refs_4_.high1, ...), custom_call_target="tpu_custom_call" | custom-call | flops 201326592 | bytes 1048576 | tf_op jit(solution)/shard_map/multiply_own/pallas_call | solution.py:210
  57.0 0.2 collective-permute-done.2
  57.3 32.7 %all_to_all.10.parts_ref = f32[64,8,128]{2,1,0:T(8,128)S(1)} all-to-all(f32[64,8,128]{2,1,0:T(8,128)S(1)} %bitcast.11), channel_id=1, replica_groups=mesh['yh'=2,'zq'=4,'zp'=2,'x'=8,'core'=2,'yl'=4] {'x','yh','zq'}, dimensions={0} | all-to-all | bytes 524288 | tf_op jit(solution)/shard_map/all_to_all | solution.py:220
  90.0 0.7 sum_parts.1
  (3 shorter events, 0.0 us)
Async XLA Ops:
  0.0 0.8 copy-start.1
  0.8 0.8 copy-start.2
  1.7 0.7 copy-start.3
  3.8 19.4 %copy-start = (f32[1,2,1024,256]{3,2,1,0:T(8,128)S(1)}, f32[1,2,1024,256]{3,2,1,0:T(8,128)}, u32[]{:S(2)}) copy-start(f32[1,2,1024,256]{3,2,1,0:T(8,128)} %param.8) | copy-start | bytes 6291460
  3.8 46.7 %all-to-all-start = ((f32[64,1,4224]{2,1,0:T(1,128)}), f32[64,1,4224]{2,1,0:T(1,128)S(1)}, u32[]{:S(2)}, u32[]{:S(2)}) async-start(f32[64,1,4224]{2,1,0:T(1,128)} %bitcast.5), calls=%async_computation | async-start | bytes 2162688 | tf_op jit(solution)/shard_map/all_to_all | solution.py:157
  24.2 22.9 %collective-permute-start.1 = (f32[256,512]{1,0:T(8,128)S(1)}, f32[256,512]{1,0:T(8,128)S(1)}, u32[]{:S(2)}, u32[]{:S(2)}) collective-permute-start(f32[256,512]{1,0:T(8,128)S(1)} %get-tuple-element.21), channel_id=1, source_target_pairs={{0,448},{64,128},{128,64},{192,256},{256,192},{320,384},{384,320},... | collective-permute-start | bytes 1572872 | tf_op jit(solution)/shard_map/ppermute | solution.py:198
  35.2 14.6 %collective-permute-start = (f32[256,512]{1,0:T(8,128)S(1)}, f32[256,512]{1,0:T(8,128)S(1)}, u32[]{:S(2)}, u32[]{:S(2)}) collective-permute-start(f32[256,512]{1,0:T(8,128)S(1)} %get-tuple-element.17), channel_id=1, source_target_pairs={{0,64},{64,0},{128,192},{192,128},{256,320},{320,256},{384,448},{4... | collective-permute-start | bytes 1572872 | tf_op jit(solution)/shard_map/ppermute | solution.py:198
  52.3 4.9 %collective-permute-start.2 = (f32[32,2,8,128]{3,2,1,0:T(8,128)S(1)}, f32[32,2,8,128]{3,2,1,0:T(8,128)S(1)}, u32[]{:S(2)}, u32[]{:S(2)}) collective-permute-start(f32[32,2,8,128]{3,2,1,0:T(8,128)S(1)} %get-tuple-element.26), channel_id=1, source_target_pairs={{0,4},{4,0},{1,5},{5,1},{2,6},{6,2},{3,7},{7,3},{8,12},{12,8},{9,1... | collective-permute-start | bytes 786440 | tf_op jit(solution)/shard_map/ppermute | solution.py:209

commit v5 on v2

--- a/solution.py
+++ b/solution.py
@@ -16,8 +16,11 @@
 CHUNK = 2 * SLOTS + 1
 VMEM = pl.BlockSpec(memory_space=pltpu.VMEM)
 SMEM = pl.BlockSpec(memory_space=pltpu.SMEM)
-HBM = pl.BlockSpec(memory_space=pltpu.HBM)
+ANY = pl.BlockSpec(memory_space=pl.ANY)
+INPUTS = pltpu.CompilerParams(vmem_limit_bytes=56 * 1024 * 1024)
+PAIR = pltpu.CompilerParams(vmem_limit_bytes=51 * 1024 * 1024)
 PARAMS = pltpu.CompilerParams(vmem_limit_bytes=40 * 1024 * 1024)
+PAIR_FLOPS = 5 * 10**9
 
 
 def iota(shape, axis):
@@ -91,26 +94,39 @@
                 ref[x * half : (x + 1) * half, which * depth : (which + 1) * depth] = value
 
 
-def combine_kernel(own_ref, other_ref, high_ref, low_ref):
-    for at in range(0, own_ref.shape[0], 64):
-        rows = slice(at, at + 64)
-        high_ref[rows], low_ref[rows] = split(own_ref[rows] + other_ref[rows])
-
-
-def product(high, low, panel):
-    both = jnp.dot(high, panel, preferred_element_type=jnp.float32)
-    return both[:, :LANES] + (both[:, LANES:] + jnp.dot(low, panel[:, :LANES], preferred_element_type=jnp.float32))
-
-
-def multiply(first, out_ref, which, highs, lows, panel_ref):
+def pair_kernel(core, coef_ref, blocks_ref, other_ref, sum_ref, blocks, sems):
+    pieces, half, depth = blocks.shape[1:]
+    steps = sems.shape[0]
+    step = pieces // steps
+    copies = []
+    for at in range(steps):
+        x = pl.ds(at * step, step)
+        copies.append(pltpu.make_async_copy(blocks_ref.at[:, x, core], blocks.at[:, x], sems.at[at]))
+        copies[-1].start()
+    for at in range(steps):
+        copies[at].wait()
+        for x in range(at * step, (at + 1) * step):
+            re, im = blocks[0, x], blocks[1, x]
+            rows = slice(x * half, (x + 1) * half)
+            for which in range(2):
+                columns = slice(which * depth, (which + 1) * depth)
+                own = coef_ref[2 * which] * re + coef_ref[2 * which + 1] * im
+                sum_ref[rows, columns] = own + other_ref[rows, columns]
+
+
+def multiply(out_ref, which, sums, panel_ref):
+    panel = panel_ref[...]
     for index in range(2):
 
         @pl.when(which == index)
         def _():
-            out_ref[...] = product(highs[index][...], lows[index][...], panel_ref[...])
-
-
-def first_kernel(senders, place_ref, rows_ref, high0, low0, high1, low1, out_ref, panel_ref):
+            high, low = split(sums[index][...])
+            both = jnp.dot(high, panel, preferred_element_type=jnp.float32)
+            more = jnp.dot(low, panel[:, :LANES], preferred_element_type=jnp.float32)
+            out_ref[...] = both[:, :LANES] + (both[:, LANES:] + more)
+
+
+def first_kernel(senders, place_ref, rows_ref, sum0, sum1, out_ref, panel_ref):
     row, core = place_ref[0], place_ref[1]
     depth = panel_ref.shape[0] // 2
     labels = rows_ref[pl.ds(CHUNK - 1, senders, stride=CHUNK), :]
@@ -126,11 +142,11 @@
         pieces = jnp.concatenate(split(jnp.concatenate(values, axis=0)), axis=1)
         placed = lax.dot_general(places, pieces, (((0,), (0,)), ((), ())), preferred_element_type=jnp.float32)
         panel_ref[which * depth : (which + 1) * depth, :] = placed.astype(jnp.bfloat16)
-    multiply(True, out_ref, 1 - core, (high0, high1), (low0, low1), panel_ref)
-
-
-def second_kernel(place_ref, high0, low0, high1, low1, panel_ref, out_ref):
-    multiply(False, out_ref, place_ref[1], (high0, high1), (low0, low1), panel_ref)
+    multiply(out_ref, 1 - core, (sum0, sum1), panel_ref)
+
+
+def second_kernel(place_ref, sum0, sum1, panel_ref, out_ref):
+    multiply(out_ref, place_ref[1], (sum0, sum1), panel_ref)
 
 
 def last_kernel(parts_ref, out_ref):
@@ -152,7 +168,7 @@
     packed = pl.pallas_call(
         lambda *refs: pack_kernel(rows_axis, cols_axis, depth.bit_length() - 1, *refs),
         out_shape=jax.ShapeDtypeStruct((senders * CHUNK, LANES), jnp.float32),
-        in_specs=[SMEM, HBM, HBM, HBM],
+        in_specs=[SMEM, ANY, ANY, ANY],
         out_specs=VMEM,
         scratch_shapes=[
             pltpu.VMEM((share, LANES), jnp.float32),
@@ -160,7 +176,7 @@
             pltpu.VMEM((1, share), jnp.int32),
             pltpu.SemaphoreType.DMA((3,)),
         ],
-        compiler_params=PARAMS,
+        compiler_params=INPUTS,
         name="pack_rows",
     )(place, hamiltonian, margin, owner.reshape(1, share))
     arrived = lax.all_to_all(
@@ -178,10 +194,10 @@
     factors = pl.pallas_call(
         lambda *refs: coefficient_kernel(pieces, *refs),
         out_shape=(factor, factor),
-        in_specs=[SMEM, HBM],
+        in_specs=[SMEM, ANY],
         out_specs=(VMEM, VMEM),
         scratch_shapes=[pltpu.VMEM((2, block_rows, depth), jnp.float32), pltpu.SemaphoreType.DMA((pieces,))],
-        compiler_params=PARAMS,
+        compiler_params=INPUTS,
         cost_estimate=pl.CostEstimate(flops=6 * block_rows * depth, bytes_accessed=16 * block_rows * depth, transcendentals=0),
         name="left_factors",
     )(coefs, inverse_blocks[0])
@@ -190,24 +206,31 @@
         [(i, (i - 1 if i % 2 == 0 else i + 1) % z_axis) for i in range(z_axis)],
     )
     others = [lax.ppermute(own, "z", pair) for own, pair in zip(factors, pairs)]
-    part = jax.ShapeDtypeStruct(factor.shape, jnp.bfloat16)
+    split_blocks = inverse_blocks[0].reshape(2, pieces, 2, block_rows // pieces // 2, depth)
     summed = []
-    for own, other in zip(factors, others):
-        summed += pl.pallas_call(
-            combine_kernel,
-            out_shape=(part, part),
-            in_specs=[VMEM] * 2,
-            out_specs=(VMEM, VMEM),
-            compiler_params=PARAMS,
-            cost_estimate=pl.CostEstimate(flops=block_rows * depth * 3, bytes_accessed=12 * block_rows * depth, transcendentals=0),
-            name="pair_sums",
-        )(own, other)
+    for which, other in enumerate(others):
+        summed.append(
+            pl.pallas_call(
+                lambda *refs, which=which: pair_kernel(which, *refs),
+                out_shape=factor,
+                in_specs=[SMEM, ANY, VMEM],
+                out_specs=VMEM,
+                scratch_shapes=[
+                    pltpu.VMEM((2, pieces, block_rows // pieces // 2, depth), jnp.float32),
+                    pltpu.SemaphoreType.DMA((4,)),
+                ],
+                input_output_aliases={2: 0},
+                compiler_params=PAIR,
+                cost_estimate=pl.CostEstimate(flops=PAIR_FLOPS, bytes_accessed=12 * block_rows * depth, transcendentals=0),
+                name="pair_sums",
+            )(coefs, split_blocks, other)
+        )
 
     chunks = jax.ShapeDtypeStruct((block_rows // 2, LANES), jnp.float32)
     sent, panel = pl.pallas_call(
         lambda *refs: first_kernel(senders, *refs),
         out_shape=(chunks, jax.ShapeDtypeStruct((2 * depth, 2 * LANES), jnp.bfloat16)),
-        in_specs=[SMEM] + [VMEM] * 5,
+        in_specs=[SMEM] + [VMEM] * 3,
         out_specs=(VMEM,) * 2,
         compiler_params=PARAMS,
         name="place_and_multiply",
@@ -216,7 +239,7 @@
     kept = pl.pallas_call(
         second_kernel,
         out_shape=chunks,
-        in_specs=[SMEM] + [VMEM] * 5,
+        in_specs=[SMEM] + [VMEM] * 3,
         out_specs=VMEM,
         compiler_params=PARAMS,
         cost_estimate=pl.CostEstimate(flops=3 * block_rows * 2 * depth * LANES, bytes_accessed=4 * block_rows * depth, transcendentals=0),

time: 102 us -> 94.3 us (0.925)
  waiting for transfers between devices: 23.1 us -> 13.8 us
  Pallas kernels: 6.47 us -> 13.6 us
  local copies, waits for them, and re-layouts: 3.93 us -> 0.01 us
  blocking collectives: 31.6 us -> 28.8 us
  other arithmetic: 0.18 us -> 1.25 us
    ppermute x2, waiting for transfers between devices: 23 us -> 5.4 us  [per_device(): others = [lax.ppermute(own, 'z', pair) for own, pair in zip(factors, pairs)]]
    all_to_all x1, waiting for transfers between devices: 0.01 us -> 8.3 us  [per_device(): lax.all_to_all(packed.reshape(senders, 1, CHUNK * LANES), ('x', 'core', '...]
    ppermute x2, starting transfers between devices: 12.9 us -> 19.8 us  [per_device(): others = [lax.ppermute(own, 'z', pair) for own, pair in zip(factors, pairs)]]
    all_to_all x1, starting transfers between devices: 18.3 us -> 11.7 us  [per_device(): lax.all_to_all(packed.reshape(senders, 1, CHUNK * LANES), ('x', 'core', '...]
    unnamed x8 -> x4, local copies, waits for them, and re-layouts: 3.93 us -> 0.01 us
    pallas_call x2, Pallas kernels: 0.34 us -> 3.96 us  [per_device(): pl.pallas_call(lambda *refs, which=which: pair_kernel(which, *refs), out_...]
    all_to_all x1, blocking collectives: 31.6 us -> 28.8 us  [per_device(): lax.all_to_all(both, ('x', 'yh', 'z'), split_axis=0, concat_axis=0, tiled...]
    pallas_call x1, Pallas kernels: 1.03 us -> 3.7 us  [per_device(): pl.pallas_call(lambda *refs: coefficient_kernel(pieces, *refs), out_shape...]
  transfers between devices with their start and end apart: 4 -> 4, of which waited for: 3 -> 3; matrix products, arithmetic and copies ran while one was open for 0% -> 1% of each run, Pallas kernels for 2% -> 8%
where the time goes in v5:
time: 94.3 us; the launch traced here: 93.2 us
  starting transfers between devices  34.8 us (37%)
  blocking collectives  28.8 us (31%)
  waiting for transfers between devices  13.8 us (15%)
  Pallas kernels  13.6 us (14%)
  other arithmetic  1.25 us (1%)
    all_to_all x1, blocking collectives, per_device(): lax.all_to_all(both, ('x', 'yh', 'z'), split_axis=0, concat_axis=0, tiled...  28.8 us
    ppermute x2, starting transfers between devices, per_device(): others = [lax.ppermute(own, 'z', pair) for own, pair in zip(factors, pairs)]  19.8 us
    all_to_all x1, starting transfers between devices, per_device(): lax.all_to_all(packed.reshape(senders, 1, CHUNK * LANES), ('x', 'core', '...  11.7 us
    all_to_all x1, waiting for transfers between devices, per_device(): lax.all_to_all(packed.reshape(senders, 1, CHUNK * LANES), ('x', 'core', '...  8.3 us
    ppermute x2, waiting for transfers between devices, per_device(): others = [lax.ppermute(own, 'z', pair) for own, pair in zip(factors, pairs)]  5.4 us
    pallas_call x2, Pallas kernels, per_device(): pl.pallas_call(lambda *refs, which=which: pair_kernel(which, *refs), out_...  3.96 us
    pallas_call x1, Pallas kernels, per_device(): pl.pallas_call(lambda *refs: coefficient_kernel(pieces, *refs), out_shape...  3.7 us
    ppermute x1, starting transfers between devices, per_device(): received = lax.ppermute(sent, 'core', [(0, 1), (1, 0)])  3.37 us
  transfers between devices with their start and end apart: 4, of which 3 were waited for; matrix products, arithmetic and copies ran while one was open for 1% of the time, Pallas kernels for 8%

profile of v5, /device:TPU:1, one launch (start us, length us, event | category | flops | bytes accessed | tf_op | source)
XLA Modules:
  0.0 93.2 jit_solution(11669214412446099589)
XLA Ops:
  0.8 0.6 pad_maximum_fusion.refs_0_
  1.4 0.0 copy-start.1
  1.4 3.7 %left_factors.1 = (f32[512,512]{1,0:T(8,128)}, f32[512,512]{1,0:T(8,128)}) custom-call(f32[4]{0:T(128)} %pad_maximum_fusion.refs_0_, f32[2,1024,256]{2,1,0:T(8,128)} %bitcast.13), custom_call_target="tpu_custom_call" | custom-call | flops 1572864 | bytes 4194304 | tf_op jit(solution)/shard_map/left_factors/pallas_call | solution.py:194
  5.1 5.7 %collective-permute-start = (f32[512,512]{1,0:T(8,128)}, f32[512,512]{1,0:T(8,128)S(1)}, u32[]{:S(2)}, u32[]{:S(2)}) collective-permute-start(f32[512,512]{1,0:T(8,128)} %get-tuple-element.9), channel_id=1, source_target_pairs={{0,64},{64,0},{128,192},{192,128},{256,320},{320,256},{384,448},{4... | collective-permute-start | bytes 3145736 | tf_op jit(solution)/shard_map/ppermute | solution.py:208
  10.9 14.0 %collective-permute-start.1 = (f32[512,512]{1,0:T(8,128)}, f32[512,512]{1,0:T(8,128)S(1)}, u32[]{:S(2)}, u32[]{:S(2)}) collective-permute-start(f32[512,512]{1,0:T(8,128)} %get-tuple-element.10), channel_id=1, source_target_pairs={{0,448},{64,128},{128,64},{192,256},{256,192},{320,384},{384,320},... | collective-permute-start | bytes 3145736 | tf_op jit(solution)/shard_map/ppermute | solution.py:208
  24.9 0.6 pad_add_fusion.refs_0_.place_ref
  25.6 2.8 %pack_rows.1 = f32[1088,128]{1,0:T(8,128)} custom-call(s32[3]{0:T(128)} %pad_add_fusion.refs_0_.place_ref, f32[64,256]{1,0:T(8,128)} %refs_1_.1, f32[64,256]{1,0:T(8,128)} %refs_2_.1, s32[1,64]{1,0:T(1,128)} %bitcast.17), custom_call_target="tpu_custom_call" | custom-call | tf_op jit(solution)/shard_map/pack_rows/pallas_call | solution.py:168
  28.4 11.7 %all-to-all-start = ((f32[64,1,2176]{2,1,0:T(1,128)}), f32[64,1,2176]{2,1,0:T(1,128)S(1)}, u32[]{:S(2)}, u32[]{:S(2)}) async-start(f32[64,1,2176]{2,1,0:T(1,128)} %bitcast.12), calls=%async_computation | async-start | bytes 1114112 | tf_op jit(solution)/shard_map/all_to_all | solution.py:182
  40.0 0.0 collective-permute-done.refs_2_
  40.1 0.0 copy-done.1
  40.1 2.0 %pair_sums.2.refs_2_.sum0 = f32[512,512]{1,0:T(8,128)S(1)} custom-call(f32[4]{0:T(128)S(1)} %copy-done.1, f32[2,8,2,64,256]{4,3,2,1,0:T(8,128)} %bitcast.14, f32[512,512]{1,0:T(8,128)S(1)} %collective-permute-done.refs_2_), custom_call_target="tpu_custom_call", output_to_operand_aliasing={{}: (2, {})} | custom-call | flops 5000000000 | bytes 3145728 | tf_op jit(solution)/shard_map/pair_sums/pallas_call | solution.py:213
  42.1 0.0 copy-start
  42.1 5.4 %collective-permute-done.1.refs_2_ = f32[512,512]{1,0:T(8,128)S(1)} collective-permute-done((f32[512,512]{1,0:T(8,128)}, f32[512,512]{1,0:T(8,128)S(1)}, u32[]{:S(2)}, u32[]{:S(2)}) %collective-permute-start.1) | collective-permute-done | bytes 1048608 | tf_op jit(solution)/shard_map/ppermute | solution.py:208
  47.5 2.0 %pair_sums.3.refs_3_.sum1 = f32[512,512]{1,0:T(8,128)S(1)} custom-call(f32[4]{0:T(128)S(1)} %copy-done.1, f32[2,8,2,64,256]{4,3,2,1,0:T(8,128)} %bitcast.15, f32[512,512]{1,0:T(8,128)S(1)} %collective-permute-done.1.refs_2_), custom_call_target="tpu_custom_call", output_to_operand_aliasing={{}: (2, {})} | custom-call | flops 5000000000 | bytes 3145728 | tf_op jit(solution)/shard_map/pair_sums/pallas_call | solution.py:213
  49.5 8.3 %all-to-all-done = f32[64,1,2176]{2,1,0:T(1,128)S(1)} async-done(((f32[64,1,2176]{2,1,0:T(1,128)}), f32[64,1,2176]{2,1,0:T(1,128)S(1)}, u32[]{:S(2)}, u32[]{:S(2)}) %all-to-all-start) | async-done | bytes 557088 | tf_op jit(solution)/shard_map/all_to_all | solution.py:182
  57.7 0.0 copy-done
  57.8 1.4 %place_and_multiply.1 = (f32[512,128]{1,0:T(8,128)S(1)}, bf16[512,256]{1,0:T(8,128)(2,1)S(1)}) custom-call(s32[3]{0:T(128)S(1)} %copy-done, f32[1088,128]{1,0:T(8,128)S(1)} %bitcast.10, f32[512,512]{1,0:T(8,128)S(1)} %pair_sums.2.refs_2_.sum0, f32[512,512]{1,0:T(8,128)S(1)} %pair_sums.3.refs_3_.sum1), custom_call_target="tpu_custom_call" | custom-call | tf_op jit(solution)/shard_map/place_and_multiply/pallas_call | solution.py:230
  59.2 3.4 %collective-permute-start.2 = (f32[512,128]{1,0:T(8,128)S(1)}, f32[512,128]{1,0:T(8,128)S(1)}, u32[]{:S(2)}, u32[]{:S(2)}) collective-permute-start(f32[512,128]{1,0:T(8,128)S(1)} %get-tuple-element.12), channel_id=1, source_target_pairs={{0,4},{4,0},{1,5},{5,1},{2,6},{6,2},{3,7},{7,3},{8,12},{12,8},{9,1... | collective-permute-start | bytes 786440 | tf_op jit(solution)/shard_map/ppermute | solution.py:238
  62.6 1.0 %multiply_own.1 = f32[512,128]{1,0:T(8,128)S(1)} custom-call(s32[3]{0:T(128)S(1)} %copy-done, f32[512,512]{1,0:T(8,128)S(1)} %pair_sums.2.refs_2_.sum0, f32[512,512]{1,0:T(8,128)S(1)} %pair_sums.3.refs_3_.sum1, bf16[512,256]{1,0:T(8,128)(2,1)S(1)} %get-tuple-element.11.panel_ref), custom_call_target="tpu_custom_call" | custom-call | flops 201326592 | bytes 1048576 | tf_op jit(solution)/shard_map/multiply_own/pallas_call | solution.py:239
  63.6 0.1 collective-permute-done.2
  63.8 28.8 %all_to_all.10 = f32[128,4,128]{2,1,0:T(4,128)S(1)} all-to-all(f32[128,4,128]{2,1,0:T(4,128)S(1)} %bitcast.16), channel_id=1, replica_groups=mesh['yh'=2,'z'=8,'x'=8,'core'=2,'yl'=4] {'x','yh','z'}, dimensions={0} | all-to-all | bytes 524288 | tf_op jit(solution)/shard_map/all_to_all | solution.py:249
  92.5 0.7 sum_parts.1
  (1 shorter events, 0.0 us)
Async XLA Ops:
  1.4 38.6 %copy-start.1 = (f32[4]{0:T(128)S(1)}, f32[4]{0:T(128)}, u32[]{:S(2)}) copy-start(f32[4]{0:T(128)} %pad_maximum_fusion.refs_0_) | copy-start | bytes 52
  5.1 34.9 %collective-permute-start = (f32[512,512]{1,0:T(8,128)}, f32[512,512]{1,0:T(8,128)S(1)}, u32[]{:S(2)}, u32[]{:S(2)}) collective-permute-start(f32[512,512]{1,0:T(8,128)} %get-tuple-element.9), channel_id=1, source_target_pairs={{0,64},{64,0},{128,192},{192,128},{256,320},{320,256},{384,448},{4... | collective-permute-start | bytes 3145736 | tf_op jit(solution)/shard_map/ppermute | solution.py:208
  10.9 36.6 %collective-permute-start.1 = (f32[512,512]{1,0:T(8,128)}, f32[512,512]{1,0:T(8,128)S(1)}, u32[]{:S(2)}, u32[]{:S(2)}) collective-permute-start(f32[512,512]{1,0:T(8,128)} %get-tuple-element.10), channel_id=1, source_target_pairs={{0,448},{64,128},{128,64},{192,256},{256,192},{320,384},{384,320},... | collective-permute-start | bytes 3145736 | tf_op jit(solution)/shard_map/ppermute | solution.py:208
  28.4 29.4 %all-to-all-start = ((f32[64,1,2176]{2,1,0:T(1,128)}), f32[64,1,2176]{2,1,0:T(1,128)S(1)}, u32[]{:S(2)}, u32[]{:S(2)}) async-start(f32[64,1,2176]{2,1,0:T(1,128)} %bitcast.12), calls=%async_computation | async-start | bytes 1114112 | tf_op jit(solution)/shard_map/all_to_all | solution.py:182
  42.1 15.7 %copy-start = (s32[3]{0:T(128)S(1)}, s32[3]{0:T(128)}, u32[]{:S(2)}) copy-start(s32[3]{0:T(128)} %pad_add_fusion.refs_0_.place_ref) | copy-start | bytes 40
  59.2 4.5 %collective-permute-start.2 = (f32[512,128]{1,0:T(8,128)S(1)}, f32[512,128]{1,0:T(8,128)S(1)}, u32[]{:S(2)}, u32[]{:S(2)}) collective-permute-start(f32[512,128]{1,0:T(8,128)S(1)} %get-tuple-element.12), channel_id=1, source_target_pairs={{0,4},{4,0},{1,5},{5,1},{2,6},{6,2},{3,7},{7,3},{8,12},{12,8},{9,1... | collective-permute-start | bytes 786440 | tf_op jit(solution)/shard_map/ppermute | solution.py:238

commit v6 on v4

--- a/solution.py
+++ b/solution.py
@@ -15,6 +15,8 @@
 SLOTS = 8
 VMEM = pl.BlockSpec(memory_space=pltpu.VMEM)
 SMEM = pl.BlockSpec(memory_space=pltpu.SMEM)
+ANY = pl.BlockSpec(memory_space=pl.ANY)
+INPUTS = pltpu.CompilerParams(vmem_limit_bytes=56 * 1024 * 1024)
 PARAMS = pltpu.CompilerParams(vmem_limit_bytes=40 * 1024 * 1024)
 
 
@@ -22,10 +24,16 @@
     return lax.broadcasted_iota(jnp.int32, shape, axis)
 
 
-def pack_kernel(rows_axis, cols_axis, ham_ref, mar_ref, owner_ref, out_ref):
-    share, width = ham_ref.shape
-    shift = (4096 // rows_axis).bit_length() - 1
-    own_r = jnp.broadcast_to(owner_ref[...].astype(jnp.float32), (share, share))
+def pack_kernel(rows_axis, cols_axis, *refs):
+    ham, mar, owner, sems = refs[4:]
+    out_ref = refs[3]
+    share, width = ham.shape
+    shift = (share * cols_axis).bit_length() - 1
+    copies = [pltpu.make_async_copy(ref, to, sems.at[i]) for i, (ref, to) in enumerate(zip(refs[:3], (ham, mar, owner)))]
+    for copy in reversed(copies):
+        copy.start()
+    copies[2].wait()
+    own_r = jnp.broadcast_to(owner[...].astype(jnp.float32), (share, share))
     own_c = jnp.sum(jnp.where(iota((share, share), 0) == iota((share, share), 1), own_r, 0.0), axis=1, keepdims=True)
     own_c = jnp.broadcast_to(own_c, (share, share)).astype(jnp.int32)
     own_r = own_r.astype(jnp.int32)
@@ -45,7 +53,11 @@
     )
     labels = jnp.sum(labels, axis=0, keepdims=True)
     chunk = 2 * width // LANES * SLOTS + 1
-    for which, ref in enumerate((ham_ref, mar_ref)):
+    for target in range(rows_axis * cols_axis):
+        base = (target + 1) * chunk - 1
+        out_ref[base : base + 1, :] = labels
+    for which, ref in enumerate((ham, mar)):
+        copies[which].wait()
         packed = jnp.dot(packer, ref[...], precision=lax.Precision.HIGHEST, preferred_element_type=jnp.float32)
         for part in range(width // LANES):
             offset = (which * (width // LANES) + part) * SLOTS
@@ -54,9 +66,6 @@
                 for col in range(cols_axis):
                     base = (row * cols_axis + col) * chunk + offset
                     out_ref[base : base + SLOTS, :] = tile
-    for target in range(rows_axis * cols_axis):
-        base = (target + 1) * chunk - 1
-        out_ref[base : base + 1, :] = labels
 
 
 def split(value):
@@ -73,14 +82,28 @@
         re = blocks_ref[0, index * piece : (index + 1) * piece, :]
         im = blocks_ref[1, index * piece : (index + 1) * piece, :]
         for which in range(2):
-            value = (coef_ref[2 * which] * re + coef_ref[2 * which + 1] * im).reshape(piece // 16, 2, 8, depth)
+            value = coef_ref[2 * which] * re + coef_ref[2 * which + 1] * im
+            value = value.reshape(2, 2, 2, 8, depth)
             first, second = value[:, 0], value[:, 1]
-            upper = iota(first.shape, 1) < 4
-            even = jnp.where(upper, first, pltpu.roll(second, 4, 1)).reshape(piece // 2, depth)
-            odd = jnp.where(upper, pltpu.roll(first, 4, 1), second).reshape(piece // 2, depth)
-            at = (slice(x * piece // 2, (x + 1) * piece // 2), slice(which * depth, (which + 1) * depth))
-            out_refs[core][at] = jnp.where(odd_here, odd, even)
-            out_refs[2 + core][at] = jnp.where(odd_here, even, odd)
+            upper = iota(first.shape, 2) < 4
+            even = jnp.where(upper, first, pltpu.roll(second, 4, 2))
+            odd = jnp.where(upper, pltpu.roll(first, 4, 2), second)
+            here = jnp.where(odd_here, odd, even)
+            there = jnp.where(odd_here, even, odd)
+            columns = slice(which * depth, (which + 1) * depth)
+            for part in range(2):
+                start = part * rows // 8 + x * piece // 4
+                at = (slice(start, start + piece // 4), columns)
+                out_refs[core][at] = here[:, part].reshape(piece // 4, depth)
+                out_refs[2 + core][at] = there[:, part].reshape(piece // 4, depth)
+
+
+def first_pair_kernel(place_ref, own_ref, other_ref, here_ref, there_ref):
+    rows = here_ref.shape[0]
+    half = place_ref[3]
+    for ref, which in ((here_ref, half), (there_ref, 1 - half)):
+        at = pl.ds(pl.multiple_of(which * rows, rows), rows)
+        ref[...] = own_ref[at, :] + other_ref[at, :]
 
 
 def pair_kernel(own_ref, other_ref, high_ref, low_ref):
@@ -149,9 +172,15 @@
     packed = pl.pallas_call(
         lambda *refs: pack_kernel(rows_axis, cols_axis, *refs),
         out_shape=jax.ShapeDtypeStruct((senders * chunk, LANES), jnp.float32),
-        in_specs=[VMEM] * 3,
+        in_specs=[ANY] * 3,
         out_specs=VMEM,
-        compiler_params=PARAMS,
+        scratch_shapes=[
+            pltpu.VMEM((share, width), jnp.float32),
+            pltpu.VMEM((share, width), jnp.float32),
+            pltpu.VMEM((1, share), jnp.int32),
+            pltpu.SemaphoreType.DMA((3,)),
+        ],
+        compiler_params=INPUTS,
         name="pack_rows",
     )(hamiltonian, margin, owner.reshape(1, share))
     arrived = lax.all_to_all(
@@ -167,7 +196,7 @@
     block_rows, depth = inverse_blocks.shape[2:]
     core = lax.axis_index("core")
     place = jnp.stack(
-        [lax.axis_index("x") * lax.axis_size("core") + core, core, lax.axis_index("zp")]
+        [lax.axis_index("x") * lax.axis_size("core") + core, core, lax.axis_index("zp"), lax.axis_index("zqp")]
     ).astype(jnp.int32)
     factor = jax.ShapeDtypeStruct((block_rows // 4, 2 * depth), jnp.float32)
     factors = pl.pallas_call(
@@ -179,24 +208,39 @@
         cost_estimate=pl.CostEstimate(flops=4 * block_rows * depth, bytes_accessed=16 * block_rows * depth, transcendentals=0),
         name="left_factors",
     )(place, coefs, inverse_blocks[0])
-    z_axis = lax.axis_size("zq") * lax.axis_size("zp")
-    pairs = (
-        [(i, i ^ 1) for i in range(z_axis)],
-        [(i, (i - 1 if i % 2 == 0 else i + 1) % z_axis) for i in range(z_axis)],
-    )
-    part = jax.ShapeDtypeStruct(factor.shape, jnp.bfloat16)
+    def pairings(size):
+        return (
+            [(i, i ^ 1) for i in range(size)],
+            [(i, (i - 1 if i % 2 == 0 else i + 1) % size) for i in range(size)],
+        )
+
+    quarter = jax.ShapeDtypeStruct((block_rows // 8, 2 * depth), jnp.float32)
+    part = jax.ShapeDtypeStruct(quarter.shape, jnp.bfloat16)
+    seconds = []
+    for own, sent, pair in zip(factors[:2], factors[2:], pairings(8)):
+        seconds.append(
+            pl.pallas_call(
+                first_pair_kernel,
+                out_shape=(quarter, quarter),
+                in_specs=[SMEM, VMEM, VMEM],
+                out_specs=(VMEM, VMEM),
+                compiler_params=PARAMS,
+                cost_estimate=pl.CostEstimate(flops=block_rows * depth // 2, bytes_accessed=6 * block_rows * depth, transcendentals=0),
+                name="first_pair_sums",
+            )(place, own, lax.ppermute(sent, ("zqq", "zqp", "zp"), pair))
+        )
     summed = []
-    for own, sent, pair in zip(factors[:2], factors[2:], pairs):
+    for (own, sent), pair in zip(seconds, pairings(4)):
         summed += pl.pallas_call(
             pair_kernel,
             out_shape=(part, part),
             in_specs=[VMEM] * 2,
             out_specs=(VMEM, VMEM),
             compiler_params=PARAMS,
-            cost_estimate=pl.CostEstimate(flops=block_rows * depth, bytes_accessed=6 * block_rows * depth, transcendentals=0),
-            name="pair_sums",
-        )(own, lax.ppermute(sent, ("zq", "zp"), pair))
-    chunks = jax.ShapeDtypeStruct((block_rows // 32, 2, 8, LANES), jnp.float32)
+            cost_estimate=pl.CostEstimate(flops=block_rows * depth // 2, bytes_accessed=3 * block_rows * depth, transcendentals=0),
+            name="second_pair_sums",
+        )(own, lax.ppermute(sent, ("zqq", "zqp"), pair))
+    chunks = jax.ShapeDtypeStruct((block_rows // 64, 2, 8, LANES), jnp.float32)
     panel = jax.ShapeDtypeStruct((2 * depth, width), jnp.bfloat16)
     sent, panel_high, panel_low = pl.pallas_call(
         lambda *refs: first_kernel(senders, *refs),
@@ -216,8 +260,8 @@
         cost_estimate=pl.CostEstimate(flops=3 * block_rows * depth * width, bytes_accessed=block_rows * depth * 4, transcendentals=0),
         name="multiply_own",
     )(place, *summed, panel_high, panel_low)
-    both = (kept + received).reshape(block_rows // 16, 8, LANES)
-    parts = lax.all_to_all(both, ("x", "yh", "zq"), split_axis=0, concat_axis=0, tiled=True)
+    both = (kept + received).reshape(block_rows // 32, 8, LANES)
+    parts = lax.all_to_all(both, ("x", "yh", "zqq"), split_axis=0, concat_axis=0, tiled=True)
     return pl.pallas_call(
         last_kernel,
         out_shape=jax.ShapeDtypeStruct((4, width), jnp.float32),
@@ -229,13 +273,13 @@
 
 
 def solution(mesh):
-    fine = Mesh(mesh.devices.reshape(2, 4, 2, 8, 2, 4), ("yh", "zq", "zp", "x", "core", "yl"))
+    fine = Mesh(mesh.devices.reshape(2, 2, 2, 2, 8, 2, 4), ("yh", "zqq", "zqp", "zp", "x", "core", "yl"))
     in_specs = (
         P(("x", "core", "yl"), None),
         P(("x", "core", "yl"), None),
         P(("x", "core", "yl")),
-        P(("yh", "zq", "zp"), None, "yl", ("x", "core")),
-        P(("yh", "zq", "zp")),
+        P(("yh", "zqq", "zqp", "zp"), None, "yl", ("x", "core")),
+        P(("yh", "zqq", "zqp", "zp")),
     )
-    out_specs = P(("yl", "x", "core", "yh", "zq", "zp"), None)
+    out_specs = P(("yl", "x", "core", "yh", "zqq", "zqp", "zp"), None)
     return jax.shard_map(per_device, mesh=fine, in_specs=in_specs, out_specs=out_specs, check_vma=False)

time: 91.7 us -> 102 us (1.11)
  waiting for transfers between devices: 13.4 us -> 22 us
  starting transfers between devices: 35.1 us -> 39.1 us
  local copies, waits for them, and re-layouts: 2.34 us -> 0.01 us
  Pallas kernels: 6.01 us -> 8.02 us
  blocking collectives: 32.7 us -> 31.1 us
    ppermute x2 -> x4, waiting for transfers between devices: 12.6 us -> 21.8 us  [the longest x2 11.9 us: per_device(): lax.ppermute(sent, ('zqq', 'zqp'), pair)]
    ppermute x2 -> x4, starting transfers between devices: 12.9 us -> 16.9 us  [the longest x2 12.9 us: per_device(): lax.ppermute(sent, ('zqq', 'zqp', 'zp'), pair)]
    unnamed x8 -> x2, local copies, waits for them, and re-layouts: 2.34 us -> 0.01 us
    all_to_all x1, blocking collectives: 32.7 us -> 31.1 us  [per_device(): lax.all_to_all(both, ('x', 'yh', 'zqq'), split_axis=0, concat_axis=0, til...]
    pallas_call x0 -> x2, Pallas kernels: none -> 1.2 us  [per_device(): pl.pallas_call(first_pair_kernel, out_shape=(quarter, quarter), in_specs=...]
    pallas_call x1, Pallas kernels: 1.49 us -> 2.59 us  [per_device(): pl.pallas_call(lambda *refs: pack_kernel(rows_axis, cols_axis, *refs), ou...]
  transfers between devices with their start and end apart: 4 -> 6, of which waited for: 4 -> 3; matrix products, arithmetic and copies ran while one was open for 0% -> 0% of each run, Pallas kernels for 2% -> 3%
where the time goes in v6:
time: 102 us; the launch traced here: 101 us
  starting transfers between devices  39.1 us (38%)
  blocking collectives  31.1 us (30%)
  waiting for transfers between devices  22 us (22%)
  Pallas kernels  8.02 us (8%)
    all_to_all x1, blocking collectives, per_device(): lax.all_to_all(both, ('x', 'yh', 'zqq'), split_axis=0, concat_axis=0, til...  31.1 us
    all_to_all x1, starting transfers between devices, per_device(): lax.all_to_all(packed.reshape(senders, 1, chunk * LANES), ('x', 'core', '...  18.4 us
    ppermute x2, starting transfers between devices, per_device(): lax.ppermute(sent, ('zqq', 'zqp', 'zp'), pair)  12.9 us
    ppermute x2, waiting for transfers between devices, per_device(): lax.ppermute(sent, ('zqq', 'zqp'), pair)  11.9 us
    ppermute x2, waiting for transfers between devices, per_device(): lax.ppermute(sent, ('zqq', 'zqp', 'zp'), pair)  9.96 us
    ppermute x2, starting transfers between devices, per_device(): lax.ppermute(sent, ('zqq', 'zqp'), pair)  4.04 us
    ppermute x1, starting transfers between devices, per_device(): received = lax.ppermute(sent, 'core', [(0, 1), (1, 0)])  3.75 us
    pallas_call x1, Pallas kernels, per_device(): pl.pallas_call(lambda *refs: pack_kernel(rows_axis, cols_axis, *refs), ou...  2.59 us
  transfers between devices with their start and end apart: 6, of which 3 were waited for; matrix products, arithmetic and copies ran while one was open for 0% of the time, Pallas kernels for 3%

profile of v6, /device:TPU:1, one launch (start us, length us, event | category | flops | bytes accessed | tf_op | source)
XLA Modules:
  0.0 101.3 jit_solution(9523387467519752598)
XLA Ops:
  0.0 2.6 %pack_rows.1 = f32[2112,128]{1,0:T(8,128)} custom-call(f32[64,256]{1,0:T(8,128)} %refs_0_.1, f32[64,256]{1,0:T(8,128)} %refs_1_.1, s32[1,64]{1,0:T(1,128)} %bitcast.13), custom_call_target="tpu_custom_call" | custom-call | tf_op jit(solution)/shard_map/pack_rows/pallas_call | solution.py:172
  2.6 0.0 copy-start
  2.6 18.4 %all-to-all-start = ((f32[64,1,4224]{2,1,0:T(1,128)}), f32[64,1,4224]{2,1,0:T(1,128)S(1)}, u32[]{:S(2)}, u32[]{:S(2)}) async-start(f32[64,1,4224]{2,1,0:T(1,128)} %bitcast.11), calls=%async_computation | async-start | bytes 2162688 | tf_op jit(solution)/shard_map/all_to_all | solution.py:186
  21.8 0.1 pad_add_fusion.place_ref.refs_0_
  21.9 0.1 pad_maximum_fusion.coef_ref
  22.0 0.0 copy-done
  22.0 1.0 left_factors.1
  23.0 11.0 %collective-permute-start.2 = (f32[256,512]{1,0:T(8,128)S(1)}, f32[256,512]{1,0:T(8,128)S(1)}, u32[]{:S(2)}, u32[]{:S(2)}) collective-permute-start(f32[256,512]{1,0:T(8,128)S(1)} %get-tuple-element.27), channel_id=1, source_target_pairs={{0,448},{64,128},{128,64},{192,256},{256,192},{320,384},{384,320},... | collective-permute-start | bytes 1572872 | tf_op jit(solution)/shard_map/ppermute | solution.py:230
  34.0 1.9 %collective-permute-start = (f32[256,512]{1,0:T(8,128)S(1)}, f32[256,512]{1,0:T(8,128)S(1)}, u32[]{:S(2)}, u32[]{:S(2)}) collective-permute-start(f32[256,512]{1,0:T(8,128)S(1)} %get-tuple-element.21), channel_id=1, source_target_pairs={{0,64},{64,0},{128,192},{192,128},{256,320},{320,256},{384,448},{4... | collective-permute-start | bytes 1572872 | tf_op jit(solution)/shard_map/ppermute | solution.py:230
  35.9 10.0 %collective-permute-done.2.other_ref = f32[256,512]{1,0:T(8,128)S(1)} collective-permute-done((f32[256,512]{1,0:T(8,128)S(1)}, f32[256,512]{1,0:T(8,128)S(1)}, u32[]{:S(2)}, u32[]{:S(2)}) %collective-permute-start.2) | collective-permute-done | bytes 524320 | tf_op jit(solution)/shard_map/ppermute | solution.py:230
  45.8 0.6 first_pair_sums.3
  46.5 2.1 %collective-permute-start.3 = (f32[128,512]{1,0:T(8,128)S(1)}, f32[128,512]{1,0:T(8,128)S(1)}, u32[]{:S(2)}, u32[]{:S(2)}) collective-permute-start(f32[128,512]{1,0:T(8,128)S(1)} %get-tuple-element.29), channel_id=1, source_target_pairs={{0,384},{128,256},{256,128},{384,0},{1,385},{129,257},{257,129},{3... | collective-permute-start | bytes 786440 | tf_op jit(solution)/shard_map/ppermute | solution.py:242
  48.6 0.0 collective-permute-done.other_ref
  48.6 0.6 first_pair_sums.2
  49.2 1.9 %collective-permute-start.1 = (f32[128,512]{1,0:T(8,128)S(1)}, f32[128,512]{1,0:T(8,128)S(1)}, u32[]{:S(2)}, u32[]{:S(2)}) collective-permute-start(f32[128,512]{1,0:T(8,128)S(1)} %get-tuple-element.23), channel_id=1, source_target_pairs={{0,128},{128,0},{256,384},{384,256},{1,129},{129,1},{257,385},{385... | collective-permute-start | bytes 786440 | tf_op jit(solution)/shard_map/ppermute | solution.py:242
  51.1 11.9 %collective-permute-done.3.other_ref = f32[128,512]{1,0:T(8,128)S(1)} collective-permute-done((f32[128,512]{1,0:T(8,128)S(1)}, f32[128,512]{1,0:T(8,128)S(1)}, u32[]{:S(2)}, u32[]{:S(2)}) %collective-permute-start.3) | collective-permute-done | bytes 262176 | tf_op jit(solution)/shard_map/ppermute | solution.py:242
  63.0 0.0 collective-permute-done.1.other_ref
  63.1 0.0 all-to-all-done
  63.1 1.7 %place_and_multiply.1 = (f32[16,2,8,128]{3,2,1,0:T(8,128)S(1)}, bf16[512,256]{1,0:T(8,128)(2,1)S(1)}, bf16[512,256]{1,0:T(8,128)(2,1)S(1)}) custom-call(s32[4]{0:T(128)S(1)} %pad_add_fusion.place_ref.refs_0_, f32[2112,128]{1,0:T(8,128)S(1)} %bitcast.9, bf16[128,512]{1,0:T(8,128)(2,1)S(1)} %get-tuple-element.24.refs_2_.high0, ...), custom_call_target="tpu_custom_call" | custom-call | tf_op jit(solution)/shard_map/place_and_multiply/pallas_call | solution.py:245
  64.8 3.8 %collective-permute-start.4 = (f32[16,2,8,128]{3,2,1,0:T(8,128)S(1)}, f32[16,2,8,128]{3,2,1,0:T(8,128)S(1)}, u32[]{:S(2)}, u32[]{:S(2)}) collective-permute-start(f32[16,2,8,128]{3,2,1,0:T(8,128)S(1)} %get-tuple-element.34), channel_id=1, source_target_pairs={{0,4},{4,0},{1,5},{5,1},{2,6},{6,2},{3,7},{7,3},{8,12},{12,8},{9,1... | collective-permute-start | bytes 393224 | tf_op jit(solution)/shard_map/ppermute | solution.py:253
  68.6 0.8 multiply_own.1
  69.4 0.1 collective-permute-done.4
  69.6 31.1 %all_to_all.10.parts_ref = f32[32,8,128]{2,1,0:T(8,128)S(1)} all-to-all(f32[32,8,128]{2,1,0:T(8,128)S(1)} %bitcast.12), channel_id=1, replica_groups=mesh['yh'=2,'zqq'=2,'zqp'=2,'zp'=2,'x'=8,'core'=2,'yl'=4] {'x','yh','zqq'}, dimensions={0} | all-to-all | bytes 262144 | tf_op jit(solution)/shard_map/all_to_all | solution.py:264
  100.7 0.6 sum_parts.1
  (3 shorter events, 0.1 us)
Async XLA Ops:
  2.6 19.4 %copy-start = (f32[1,2,1024,256]{3,2,1,0:T(8,128)S(1)}, f32[1,2,1024,256]{3,2,1,0:T(8,128)}, u32[]{:S(2)}) copy-start(f32[1,2,1024,256]{3,2,1,0:T(8,128)} %param.8) | copy-start | bytes 6291460
  2.6 60.5 %all-to-all-start = ((f32[64,1,4224]{2,1,0:T(1,128)}), f32[64,1,4224]{2,1,0:T(1,128)S(1)}, u32[]{:S(2)}, u32[]{:S(2)}) async-start(f32[64,1,4224]{2,1,0:T(1,128)} %bitcast.11), calls=%async_computation | async-start | bytes 2162688 | tf_op jit(solution)/shard_map/all_to_all | solution.py:186
  23.0 22.9 %collective-permute-start.2 = (f32[256,512]{1,0:T(8,128)S(1)}, f32[256,512]{1,0:T(8,128)S(1)}, u32[]{:S(2)}, u32[]{:S(2)}) collective-permute-start(f32[256,512]{1,0:T(8,128)S(1)} %get-tuple-element.27), channel_id=1, source_target_pairs={{0,448},{64,128},{128,64},{192,256},{256,192},{320,384},{384,320},... | collective-permute-start | bytes 1572872 | tf_op jit(solution)/shard_map/ppermute | solution.py:230
  34.0 14.6 %collective-permute-start = (f32[256,512]{1,0:T(8,128)S(1)}, f32[256,512]{1,0:T(8,128)S(1)}, u32[]{:S(2)}, u32[]{:S(2)}) collective-permute-start(f32[256,512]{1,0:T(8,128)S(1)} %get-tuple-element.21), channel_id=1, source_target_pairs={{0,64},{64,0},{128,192},{192,128},{256,320},{320,256},{384,448},{4... | collective-permute-start | bytes 1572872 | tf_op jit(solution)/shard_map/ppermute | solution.py:230
  46.5 16.5 %collective-permute-start.3 = (f32[128,512]{1,0:T(8,128)S(1)}, f32[128,512]{1,0:T(8,128)S(1)}, u32[]{:S(2)}, u32[]{:S(2)}) collective-permute-start(f32[128,512]{1,0:T(8,128)S(1)} %get-tuple-element.29), channel_id=1, source_target_pairs={{0,384},{128,256},{256,128},{384,0},{1,385},{129,257},{257,129},{3... | collective-permute-start | bytes 786440 | tf_op jit(solution)/shard_map/ppermute | solution.py:242
  49.2 13.8 %collective-permute-start.1 = (f32[128,512]{1,0:T(8,128)S(1)}, f32[128,512]{1,0:T(8,128)S(1)}, u32[]{:S(2)}, u32[]{:S(2)}) collective-permute-start(f32[128,512]{1,0:T(8,128)S(1)} %get-tuple-element.23), channel_id=1, source_target_pairs={{0,128},{128,0},{256,384},{384,256},{1,129},{129,1},{257,385},{385... | collective-permute-start | bytes 786440 | tf_op jit(solution)/shard_map/ppermute | solution.py:242
  64.8 4.7 %collective-permute-start.4 = (f32[16,2,8,128]{3,2,1,0:T(8,128)S(1)}, f32[16,2,8,128]{3,2,1,0:T(8,128)S(1)}, u32[]{:S(2)}, u32[]{:S(2)}) collective-permute-start(f32[16,2,8,128]{3,2,1,0:T(8,128)S(1)} %get-tuple-element.34), channel_id=1, source_target_pairs={{0,4},{4,0},{1,5},{5,1},{2,6},{6,2},{3,7},{7,3},{8,12},{12,8},{9,1... | collective-permute-start | bytes 393224 | tf_op jit(solution)/shard_map/ppermute | solution.py:253

commit v7 on v4

v7 whole, which is shorter than its diff:
```python
import math

import jax
import jax.numpy as jnp
from jax import lax
from jax.experimental import pallas as pl
from jax.experimental.pallas import tpu as pltpu
from jax.sharding import Mesh, PartitionSpec as P

POLES = 64
pole_radius = 1.5
weight_scale = 0.3

LANES = 128
SLOTS = 8
VMEM = pl.BlockSpec(memory_space=pltpu.VMEM)
SMEM = pl.BlockSpec(memory_space=pltpu.SMEM)
ANY = pl.BlockSpec(memory_space=pl.ANY)
INPUTS = pltpu.CompilerParams(vmem_limit_bytes=56 * 1024 * 1024)
PARAMS = pltpu.CompilerParams(vmem_limit_bytes=40 * 1024 * 1024)


def iota(shape, axis):
    return lax.broadcasted_iota(jnp.int32, shape, axis)


def pack_kernel(rows_axis, cols_axis, *refs):
    ham, mar, owner, sems = refs[4:]
    out_ref = refs[3]
    share, width = ham.shape
    shift = (share * cols_axis).bit_length() - 1
    copies = [pltpu.make_async_copy(ref, to, sems.at[i]) for i, (ref, to) in enumerate(zip(refs[:3], (ham, mar, owner)))]
    for copy in reversed(copies):
        copy.start()
    copies[2].wait()
    own_r = jnp.broadcast_to(owner[...].astype(jnp.float32), (share, share))
    own_c = jnp.sum(jnp.where(iota((share, share), 0) == iota((share, share), 1), own_r, 0.0), axis=1, keepdims=True)
    own_c = jnp.broadcast_to(own_c, (share, share)).astype(jnp.int32)
    own_r = own_r.astype(jnp.int32)
    same = (own_r >> shift) == (own_c >> shift)
    first, second = iota((share, share), 0), iota((share, share), 1)
    rank_r = jnp.sum(jnp.where(same & (first < second), 1.0, 0.0), axis=0, keepdims=True)
    rank_c = jnp.sum(jnp.where(same & (second < first), 1.0, 0.0), axis=1, keepdims=True)
    slot_r = (own_r[:1] >> shift) * SLOTS + rank_r.astype(jnp.int32)
    slot_c = (own_c[:, :1] >> shift) * SLOTS + rank_c.astype(jnp.int32)
    total = rows_axis * SLOTS
    packer = jnp.where(iota((total, share), 0) == jnp.broadcast_to(slot_r, (total, share)), 1.0, 0.0)
    within = (own_c[:, :1] & ((1 << shift) - 1)) + 1
    labels = jnp.where(
        iota((share, total), 1) == jnp.broadcast_to(slot_c, (share, total)),
        jnp.broadcast_to(within, (share, total)).astype(jnp.float32),
        0.0,
    )
    labels = jnp.sum(labels, axis=0, keepdims=True)
    chunk = 2 * width // LANES * SLOTS + 1
    for target in range(rows_axis * cols_axis):
        base = (target + 1) * chunk - 1
        out_ref[base : base + 1, :] = labels
    wide = 2 * SLOTS
    for which, ref in enumerate((ham, mar)):
        copies[which].wait()
        packed = jnp.dot(packer, ref[...], precision=lax.Precision.HIGHEST, preferred_element_type=jnp.float32)
        for row in range(rows_axis):
            x, core = divmod(row, 2)
            tile = packed[x * wide : (x + 1) * wide, core * LANES : (core + 1) * LANES]
            for col in range(cols_axis):
                base = (row * cols_axis + col) * chunk + which * wide
                out_ref[base : base + wide, :] = tile


def split(value):
    high = value.astype(jnp.bfloat16)
    return high, (value - high.astype(jnp.float32)).astype(jnp.bfloat16)


def left_kernel(place_ref, coef_ref, blocks_ref, *out_refs):
    rows, depth = blocks_ref.shape[1:]
    piece = rows // 16
    odd_here = place_ref[2] == 1
    for index in range(16):
        x, core = divmod(index, 2)
        re = blocks_ref[0, index * piece : (index + 1) * piece, :]
        im = blocks_ref[1, index * piece : (index + 1) * piece, :]
        for which in range(2):
            value = (coef_ref[2 * which] * re + coef_ref[2 * which + 1] * im).reshape(piece // 16, 2, 8, depth)
            first, second = value[:, 0], value[:, 1]
            upper = iota(first.shape, 1) < 4
            even = jnp.where(upper, first, pltpu.roll(second, 4, 1)).reshape(piece // 2, depth)
            odd = jnp.where(upper, pltpu.roll(first, 4, 1), second).reshape(piece // 2, depth)
            at = (slice(x * piece // 2, (x + 1) * piece // 2), slice(which * depth, (which + 1) * depth))
            out_refs[core][at] = jnp.where(odd_here, odd, even)
            out_refs[2 + core][at] = jnp.where(odd_here, even, odd)


def pair_kernel(own_ref, other_ref, sum_ref):
    sum_ref[...] = own_ref[...] + other_ref[...]


def product_kernel(senders, pieces, place_ref, rows_ref, own0, own1, mate0, mate1, out_ref, panel_ref):
    chunk = rows_ref.shape[0] // senders
    depth = panel_ref.shape[1] // 2
    labels = rows_ref[pl.ds(chunk - 1, senders, stride=chunk), :]
    lane = iota((senders, LANES), 1)
    wanted = (iota((senders, depth), 1) + 1).astype(jnp.float32)
    for block in range(2):
        places = []
        for slot in range(SLOTS):
            at = (2 * place_ref[0] + block) * SLOTS + slot
            label = jnp.sum(jnp.where(lane == at, labels, 0.0), axis=1, keepdims=True)
            places.append(jnp.where(jnp.broadcast_to(label, (senders, depth)) == wanted, 1.0, 0.0))
        places = jnp.concatenate(places, axis=0).astype(jnp.bfloat16)
        for which in range(2):
            start = (2 * which + block) * SLOTS
            values = [rows_ref[pl.ds(start + slot, senders, stride=chunk), :] for slot in range(SLOTS)]
            parts = jnp.concatenate(split(jnp.concatenate(values, axis=0)), axis=1)
            placed = lax.dot_general(places, parts, (((0,), (0,)), ((), ())), preferred_element_type=jnp.float32)
            panel_ref[block, which * depth : (which + 1) * depth, :] = placed.astype(jnp.bfloat16)
    for core in range(2):

        @pl.when(place_ref[1] == core)
        def _():
            for row_core, pair in enumerate(((own0, mate0), (own1, mate1))):
                total = None
                for block in range(2):
                    high, low = split(pair[block ^ core][...])
                    panel = panel_ref[block]
                    both = jnp.dot(high, panel, preferred_element_type=jnp.float32)
                    more = jnp.dot(low, panel[:, :LANES], preferred_element_type=jnp.float32)
                    term = both[:, :LANES] + (both[:, LANES:] + more)
                    total = term if total is None else total + term
                size = total.shape[0] // pieces
                for x in range(pieces):
                    start = (2 * x + row_core) * size
                    out_ref[start : start + size, :] = total[x * size : (x + 1) * size]


def last_kernel(pieces, parts_ref, out_ref):
    parts = parts_ref[...].reshape(pieces, 2, -1, 8, LANES)
    total = jnp.sum(jnp.sum(parts, axis=2), axis=0)
    total = total[:, :4] + total[:, 4:]
    out_ref[:, :LANES] = total[0]
    out_ref[:, LANES:] = total[1]


def per_device(hamiltonian, margin, owner, inverse_blocks, pole_index):
    rows_axis = lax.axis_size("x") * lax.axis_size("core")
    cols_axis = lax.axis_size("yl")
    share, width = hamiltonian.shape
    senders = rows_axis * cols_axis
    chunk = 2 * width // LANES * SLOTS + 1
    packed = pl.pallas_call(
        lambda *refs: pack_kernel(rows_axis, cols_axis, *refs),
        out_shape=jax.ShapeDtypeStruct((senders * chunk, LANES), jnp.float32),
        in_specs=[ANY] * 3,
        out_specs=VMEM,
        scratch_shapes=[
            pltpu.VMEM((share, width), jnp.float32),
            pltpu.VMEM((share, width), jnp.float32),
            pltpu.VMEM((1, share), jnp.int32),
            pltpu.SemaphoreType.DMA((3,)),
        ],
        compiler_params=INPUTS,
        name="pack_rows",
    )(hamiltonian, margin, owner.reshape(1, share))
    arrived = lax.all_to_all(
        packed.reshape(senders, 1, chunk * LANES), ("x", "core", "yl"), split_axis=0, concat_axis=0, tiled=True
    ).reshape(senders * chunk, LANES)

    theta = math.pi * (pole_index[0].astype(jnp.float32) + 0.5) / POLES
    energy, damping = pole_radius * jnp.cos(theta), pole_radius * jnp.sin(theta)
    weight_re, weight_im = weight_scale * jnp.cos(theta), weight_scale * jnp.sin(theta)
    shifted_re = weight_re * energy - weight_im * damping
    shifted_im = weight_re * damping + weight_im * energy
    coefs = jnp.stack([-weight_im, -weight_re, shifted_im, shifted_re])
    block_rows, depth = inverse_blocks.shape[2:]
    core = lax.axis_index("core")
    place = jnp.stack(
        [lax.axis_index("x"), core, lax.axis_index("zp")]
    ).astype(jnp.int32)
    factor = jax.ShapeDtypeStruct((block_rows // 4, 2 * depth), jnp.float32)
    factors = pl.pallas_call(
        left_kernel,
        out_shape=(factor,) * 4,
        in_specs=[SMEM, SMEM, VMEM],
        out_specs=(VMEM,) * 4,
        compiler_params=PARAMS,
        cost_estimate=pl.CostEstimate(flops=4 * block_rows * depth, bytes_accessed=16 * block_rows * depth, transcendentals=0),
        name="left_factors",
    )(place, coefs, inverse_blocks[0])
    z_axis = lax.axis_size("zq") * lax.axis_size("zp")
    pairs = (
        [(i, i ^ 1) for i in range(z_axis)],
        [(i, (i - 1 if i % 2 == 0 else i + 1) % z_axis) for i in range(z_axis)],
    )
    owns, mates = [], []
    for own, sent, pair in zip(factors[:2], factors[2:], pairs):
        total = pl.pallas_call(
            pair_kernel,
            out_shape=factor,
            in_specs=[VMEM] * 2,
            out_specs=VMEM,
            input_output_aliases={1: 0},
            compiler_params=PARAMS,
            cost_estimate=pl.CostEstimate(flops=block_rows * depth // 2, bytes_accessed=6 * block_rows * depth, transcendentals=0),
            name="pair_sums",
        )(own, lax.ppermute(sent, ("zq", "zp"), pair))
        owns.append(total)
        mates.append(lax.ppermute(total, "core", [(0, 1), (1, 0)]))
    pieces = lax.axis_size("x")
    partial = pl.pallas_call(
        lambda *refs: product_kernel(senders, pieces, *refs),
        out_shape=jax.ShapeDtypeStruct((block_rows // 2, LANES), jnp.float32),
        in_specs=[SMEM] + [VMEM] * 5,
        out_specs=VMEM,
        scratch_shapes=[pltpu.VMEM((2, 2 * depth, 2 * LANES), jnp.bfloat16)],
        compiler_params=PARAMS,
        name="place_and_multiply",
    )(place, arrived, *owns, *mates)
    parts = lax.all_to_all(
        partial.reshape(block_rows // 8, 4, LANES), ("x", "core", "yh", "zq"), split_axis=0, concat_axis=0, tiled=True
    )
    return pl.pallas_call(
        lambda *refs: last_kernel(pieces, *refs),
        out_shape=jax.ShapeDtypeStruct((4, width), jnp.float32),
        in_specs=[VMEM],
        out_specs=VMEM,
        compiler_params=PARAMS,
        name="sum_parts",
    )(parts.reshape(block_rows // 2, LANES))


def solution(mesh):
    fine = Mesh(mesh.devices.reshape(2, 4, 2, 8, 2, 4), ("yh", "zq", "zp", "x", "core", "yl"))
    in_specs = (
        P(("x", "core", "yl"), None),
        P(("x", "core", "yl"), None),
        P(("x", "core", "yl")),
        P(("yh", "zq", "zp"), None, "yl", ("x", "core")),
        P(("yh", "zq", "zp")),
    )
    out_specs = P(("yl", "x", "core", "yh", "zq", "zp"), None)
    return jax.shard_map(per_device, mesh=fine, in_specs=in_specs, out_specs=out_specs, check_vma=False)
```

time: 91.7 us -> 90.8 us (level)
  waiting for transfers between devices: 13.4 us -> 9.98 us
  blocking collectives: 32.7 us -> 35.6 us
  starting transfers between devices: 35.1 us -> 37.5 us
  local copies, waits for them, and re-layouts: 2.34 us -> 0.01 us
    ppermute x2, waiting for transfers between devices: 12.6 us -> 8.47 us  [per_device(): lax.ppermute(sent, ('zq', 'zp'), pair)]
    all_to_all x1, blocking collectives: 32.7 us -> 35.6 us  [per_device(): lax.all_to_all(partial.reshape(block_rows // 8, 4, LANES), ('x', 'core',...]
    ppermute x1 -> x2, starting transfers between devices: 3.79 us -> 6.2 us  [per_device(): mates.append(lax.ppermute(total, 'core', [(0, 1), (1, 0)]))]
    unnamed x8 -> x2, local copies, waits for them, and re-layouts: 2.34 us -> 0.01 us
    ppermute x1 -> x2, waiting for transfers between devices: 0.21 us -> 1.51 us  [per_device(): mates.append(lax.ppermute(total, 'core', [(0, 1), (1, 0)]))]
    pallas_call x1, Pallas kernels: 1.49 us -> 2.6 us  [per_device(): pl.pallas_call(lambda *refs: pack_kernel(rows_axis, cols_axis, *refs), ou...]
    pallas_call x5 -> x4, Pallas kernels: 3.56 us -> 2.74 us  [the longest x1 1.94 us: per_device(): pl.pallas_call(lambda *refs: product_kernel(senders, pieces, *refs), out_...]
  transfers between devices with their start and end apart: 4 -> 5, of which waited for: 4 -> 3; matrix products, arithmetic and copies ran while one was open for 0% -> 0% of each run, Pallas kernels for 2% -> 1%
where the time goes in v7:
time: 90.8 us; the launch traced here: 90.4 us
  starting transfers between devices  37.5 us (41%)
  blocking collectives  35.6 us (39%)
  waiting for transfers between devices  9.98 us (11%)
  Pallas kernels  6.31 us (7%)
    all_to_all x1, blocking collectives, per_device(): lax.all_to_all(partial.reshape(block_rows // 8, 4, LANES), ('x', 'core',...  35.6 us
    all_to_all x1, starting transfers between devices, per_device(): lax.all_to_all(packed.reshape(senders, 1, chunk * LANES), ('x', 'core', '...  18.4 us
    ppermute x2, starting transfers between devices, per_device(): lax.ppermute(sent, ('zq', 'zp'), pair)  12.9 us
    ppermute x2, waiting for transfers between devices, per_device(): lax.ppermute(sent, ('zq', 'zp'), pair)  8.47 us
    ppermute x2, starting transfers between devices, per_device(): mates.append(lax.ppermute(total, 'core', [(0, 1), (1, 0)]))  6.2 us
    pallas_call x1, Pallas kernels, per_device(): pl.pallas_call(lambda *refs: pack_kernel(rows_axis, cols_axis, *refs), ou...  2.6 us
    pallas_call x1, Pallas kernels, per_device(): pl.pallas_call(lambda *refs: product_kernel(senders, pieces, *refs), out_...  1.94 us
  transfers between devices with their start and end apart: 5, of which 3 were waited for; matrix products, arithmetic and copies ran while one was open for 0% of the time, Pallas kernels for 1%

profile of v7, /device:TPU:1, one launch (start us, length us, event | category | flops | bytes accessed | tf_op | source)
XLA Modules:
  0.0 90.4 jit_solution(7171631729725634123)
XLA Ops:
  0.0 2.6 %pack_rows.1 = f32[2112,128]{1,0:T(8,128)} custom-call(f32[64,256]{1,0:T(8,128)} %refs_0_.1, f32[64,256]{1,0:T(8,128)} %refs_1_.1, s32[1,64]{1,0:T(1,128)} %bitcast.14), custom_call_target="tpu_custom_call" | custom-call | tf_op jit(solution)/shard_map/pack_rows/pallas_call | solution.py:151
  2.6 0.0 copy-start
  2.6 18.4 %all-to-all-start = ((f32[64,1,4224]{2,1,0:T(1,128)}), f32[64,1,4224]{2,1,0:T(1,128)S(1)}, u32[]{:S(2)}, u32[]{:S(2)}) async-start(f32[64,1,4224]{2,1,0:T(1,128)} %bitcast.13), calls=%async_computation | async-start | bytes 2162688 | tf_op jit(solution)/shard_map/all_to_all | solution.py:165
  21.8 0.1 pad_add_fusion.place_ref.refs_0_
  21.9 0.1 pad_maximum_fusion.coef_ref
  22.0 0.0 copy-done
  22.0 1.0 %left_factors.1 = (f32[256,512]{1,0:T(8,128)S(1)}, f32[256,512]{1,0:T(8,128)S(1)}, f32[256,512]{1,0:T(8,128)S(1)}, f32[256,512]{1,0:T(8,128)S(1)}) custom-call(s32[3]{0:T(128)S(1)} %pad_add_fusion.place_ref.refs_0_, f32[4]{0:T(128)S(1)} %pad_maximum_fusion.coef_ref, f32[2,1024,256]{2,1,0:T(8,128)S(1)} %bitcast.10), custom_call_target="tpu_custom_call" | custom-call | flops 1048576 | bytes 4194304 | tf_op jit(solution)/shard_map/left_factors/pallas_call | solution.py:181
  23.0 1.9 %collective-permute-start = (f32[256,512]{1,0:T(8,128)S(1)}, f32[256,512]{1,0:T(8,128)S(1)}, u32[]{:S(2)}, u32[]{:S(2)}) collective-permute-start(f32[256,512]{1,0:T(8,128)S(1)} %get-tuple-element.10), channel_id=1, source_target_pairs={{0,64},{64,0},{128,192},{192,128},{256,320},{320,256},{384,448},{4... | collective-permute-start | bytes 1572872 | tf_op jit(solution)/shard_map/ppermute | solution.py:206
  24.9 11.0 %collective-permute-start.1 = (f32[256,512]{1,0:T(8,128)S(1)}, f32[256,512]{1,0:T(8,128)S(1)}, u32[]{:S(2)}, u32[]{:S(2)}) collective-permute-start(f32[256,512]{1,0:T(8,128)S(1)} %get-tuple-element.12), channel_id=1, source_target_pairs={{0,448},{64,128},{128,64},{192,256},{256,192},{320,384},{384,320},... | collective-permute-start | bytes 1572872 | tf_op jit(solution)/shard_map/ppermute | solution.py:206
  35.9 1.9 %collective-permute-done.other_ref = f32[256,512]{1,0:T(8,128)S(1)} collective-permute-done((f32[256,512]{1,0:T(8,128)S(1)}, f32[256,512]{1,0:T(8,128)S(1)}, u32[]{:S(2)}, u32[]{:S(2)}) %collective-permute-start) | collective-permute-done | bytes 524320 | tf_op jit(solution)/shard_map/ppermute | solution.py:206
  37.8 0.1 pair_sums.2.refs_2_
  37.9 3.3 %collective-permute-start.2 = (f32[256,512]{1,0:T(8,128)S(1)}, f32[256,512]{1,0:T(8,128)S(1)}, u32[]{:S(2)}, u32[]{:S(2)}) collective-permute-start(f32[256,512]{1,0:T(8,128)S(1)} %pair_sums.2.refs_2_), channel_id=1, source_target_pairs={{0,4},{4,0},{1,5},{5,1},{2,6},{6,2},{3,7},{7,3},{8,12},{12,8},{9,1... | collective-permute-start | bytes 1572872 | tf_op jit(solution)/shard_map/ppermute | solution.py:208
  41.2 6.5 %collective-permute-done.1.other_ref = f32[256,512]{1,0:T(8,128)S(1)} collective-permute-done((f32[256,512]{1,0:T(8,128)S(1)}, f32[256,512]{1,0:T(8,128)S(1)}, u32[]{:S(2)}, u32[]{:S(2)}) %collective-permute-start.1) | collective-permute-done | bytes 524320 | tf_op jit(solution)/shard_map/ppermute | solution.py:206
  47.8 0.1 pair_sums.3.refs_3_
  47.9 2.9 %collective-permute-start.3 = (f32[256,512]{1,0:T(8,128)S(1)}, f32[256,512]{1,0:T(8,128)S(1)}, u32[]{:S(2)}, u32[]{:S(2)}) collective-permute-start(f32[256,512]{1,0:T(8,128)S(1)} %pair_sums.3.refs_3_), channel_id=1, source_target_pairs={{0,4},{4,0},{1,5},{5,1},{2,6},{6,2},{3,7},{7,3},{8,12},{12,8},{9,1... | collective-permute-start | bytes 1572872 | tf_op jit(solution)/shard_map/ppermute | solution.py:208
  50.8 0.0 collective-permute-done.2.refs_4_
  50.8 1.5 %collective-permute-done.3.refs_5_ = f32[256,512]{1,0:T(8,128)S(1)} collective-permute-done((f32[256,512]{1,0:T(8,128)S(1)}, f32[256,512]{1,0:T(8,128)S(1)}, u32[]{:S(2)}, u32[]{:S(2)}) %collective-permute-start.3) | collective-permute-done | bytes 524320 | tf_op jit(solution)/shard_map/ppermute | solution.py:208
  52.3 0.0 all-to-all-done
  52.3 1.9 %place_and_multiply.1 = f32[512,128]{1,0:T(8,128)S(1)} custom-call(s32[3]{0:T(128)S(1)} %pad_add_fusion.place_ref.refs_0_, f32[2112,128]{1,0:T(8,128)S(1)} %bitcast.9, f32[256,512]{1,0:T(8,128)S(1)} %pair_sums.2.refs_2_, f32[256,512]{1,0:T(8,128)S(1)} %pair_sums.3.refs_3_, f32[256,512]{1,0:T(8,128)S(1)} %collective-permute-done.2.refs_4_, ...), custom_call_target="tpu_custom_call" | custom-call | tf_op jit(solution)/shard_map/place_and_multiply/pallas_call | solution.py:210
  54.2 35.6 %all_to_all.10 = f32[128,4,128]{2,1,0:T(4,128)S(1)} all-to-all(f32[128,4,128]{2,1,0:T(4,128)S(1)} %bitcast.11), channel_id=1, replica_groups=mesh['yh'=2,'zq'=4,'zp'=2,'x'=8,'core'=2,'yl'=4] {'x','core','yh','zq'}, dimensions={0} | all-to-all | bytes 524288 | tf_op jit(solution)/shard_map/all_to_all | solution.py:219
  89.8 0.6 sum_parts.1
Async XLA Ops:
  2.6 19.4 %copy-start = (f32[1,2,1024,256]{3,2,1,0:T(8,128)S(1)}, f32[1,2,1024,256]{3,2,1,0:T(8,128)}, u32[]{:S(2)}) copy-start(f32[1,2,1024,256]{3,2,1,0:T(8,128)} %param.8) | copy-start | bytes 6291460
  2.6 49.7 %all-to-all-start = ((f32[64,1,4224]{2,1,0:T(1,128)}), f32[64,1,4224]{2,1,0:T(1,128)S(1)}, u32[]{:S(2)}, u32[]{:S(2)}) async-start(f32[64,1,4224]{2,1,0:T(1,128)} %bitcast.13), calls=%async_computation | async-start | bytes 2162688 | tf_op jit(solution)/shard_map/all_to_all | solution.py:165
  23.0 14.8 %collective-permute-start = (f32[256,512]{1,0:T(8,128)S(1)}, f32[256,512]{1,0:T(8,128)S(1)}, u32[]{:S(2)}, u32[]{:S(2)}) collective-permute-start(f32[256,512]{1,0:T(8,128)S(1)} %get-tuple-element.10), channel_id=1, source_target_pairs={{0,64},{64,0},{128,192},{192,128},{256,320},{320,256},{384,448},{4... | collective-permute-start | bytes 1572872 | tf_op jit(solution)/shard_map/ppermute | solution.py:206
  24.9 22.9 %collective-permute-start.1 = (f32[256,512]{1,0:T(8,128)S(1)}, f32[256,512]{1,0:T(8,128)S(1)}, u32[]{:S(2)}, u32[]{:S(2)}) collective-permute-start(f32[256,512]{1,0:T(8,128)S(1)} %get-tuple-element.12), channel_id=1, source_target_pairs={{0,448},{64,128},{128,64},{192,256},{256,192},{320,384},{384,320},... | collective-permute-start | bytes 1572872 | tf_op jit(solution)/shard_map/ppermute | solution.py:206
  37.9 12.9 %collective-permute-start.2 = (f32[256,512]{1,0:T(8,128)S(1)}, f32[256,512]{1,0:T(8,128)S(1)}, u32[]{:S(2)}, u32[]{:S(2)}) collective-permute-start(f32[256,512]{1,0:T(8,128)S(1)} %pair_sums.2.refs_2_), channel_id=1, source_target_pairs={{0,4},{4,0},{1,5},{5,1},{2,6},{6,2},{3,7},{7,3},{8,12},{12,8},{9,1... | collective-permute-start | bytes 1572872 | tf_op jit(solution)/shard_map/ppermute | solution.py:208
  47.9 4.4 %collective-permute-start.3 = (f32[256,512]{1,0:T(8,128)S(1)}, f32[256,512]{1,0:T(8,128)S(1)}, u32[]{:S(2)}, u32[]{:S(2)}) collective-permute-start(f32[256,512]{1,0:T(8,128)S(1)} %pair_sums.3.refs_3_), channel_id=1, source_target_pairs={{0,4},{4,0},{1,5},{5,1},{2,6},{6,2},{3,7},{7,3},{8,12},{12,8},{9,1... | collective-permute-start | bytes 1572872 | tf_op jit(solution)/shard_map/ppermute | solution.py:208

commit v8 on v7

--- a/solution.py
+++ b/solution.py
@@ -119,7 +119,8 @@
 
         @pl.when(place_ref[1] == core)
         def _():
-            for row_core, pair in enumerate(((own0, mate0), (own1, mate1))):
+            totals = []
+            for pair in ((own0, mate0), (own1, mate1)):
                 total = None
                 for block in range(2):
                     high, low = split(pair[block ^ core][...])
@@ -128,18 +129,35 @@
                     more = jnp.dot(low, panel[:, :LANES], preferred_element_type=jnp.float32)
                     term = both[:, :LANES] + (both[:, LANES:] + more)
                     total = term if total is None else total + term
-                size = total.shape[0] // pieces
-                for x in range(pieces):
-                    start = (2 * x + row_core) * size
-                    out_ref[start : start + size, :] = total[x * size : (x + 1) * size]
-
-
-def last_kernel(pieces, parts_ref, out_ref):
-    parts = parts_ref[...].reshape(pieces, 2, -1, 8, LANES)
-    total = jnp.sum(jnp.sum(parts, axis=2), axis=0)
-    total = total[:, :4] + total[:, 4:]
-    out_ref[:, :LANES] = total[0]
-    out_ref[:, LANES:] = total[1]
+                totals.append(total.reshape(pieces, 2, 2, 8, LANES))
+            upper = iota(totals[0].shape, 3) < 4
+            even = jnp.where(upper, totals[0], pltpu.roll(totals[1], 4, 3))
+            odd = jnp.where(upper, pltpu.roll(totals[0], 4, 3), totals[1])
+            for z in range(2):
+                for yh in range(2):
+                    out_ref[:, 2 * z, yh] = even[:, yh, z]
+                    out_ref[:, 2 * z + 1, yh] = odd[:, yh, z]
+
+
+def sum_kernel(place_ref, parts_ref, here_ref, there_ref):
+    total = jnp.sum(parts_ref[...], axis=0)
+    first = place_ref[3] == 0
+    here_ref[...] = jnp.where(first, total[:8], total[8:])
+    there_ref[...] = jnp.where(first, total[8:], total[:8])
+
+
+def halves_kernel(place_ref, here_ref, other_ref, own_ref, mate_ref):
+    total = here_ref[...] + other_ref[...]
+    first = place_ref[1] == 0
+    own_ref[...] = jnp.where(first, total[:4], total[4:])
+    mate_ref[...] = jnp.where(first, total[4:], total[:4])
+
+
+def last_kernel(place_ref, own_ref, other_ref, out_ref):
+    first = place_ref[1] == 0
+    own, other = own_ref[...], other_ref[...]
+    out_ref[:, :LANES] = jnp.where(first, own, other)
+    out_ref[:, LANES:] = jnp.where(first, other, own)
 
 
 def per_device(hamiltonian, margin, owner, inverse_blocks, pole_index):
@@ -175,7 +193,7 @@
     block_rows, depth = inverse_blocks.shape[2:]
     core = lax.axis_index("core")
     place = jnp.stack(
-        [lax.axis_index("x"), core, lax.axis_index("zp")]
+        [lax.axis_index("x"), core, lax.axis_index("zp"), lax.axis_index("yh")]
     ).astype(jnp.int32)
     factor = jax.ShapeDtypeStruct((block_rows // 4, 2 * depth), jnp.float32)
     factors = pl.pallas_call(
@@ -209,7 +227,7 @@
     pieces = lax.axis_size("x")
     partial = pl.pallas_call(
         lambda *refs: product_kernel(senders, pieces, *refs),
-        out_shape=jax.ShapeDtypeStruct((block_rows // 2, LANES), jnp.float32),
+        out_shape=jax.ShapeDtypeStruct((pieces, 4, 2, 8, LANES), jnp.float32),
         in_specs=[SMEM] + [VMEM] * 5,
         out_specs=VMEM,
         scratch_shapes=[pltpu.VMEM((2, 2 * depth, 2 * LANES), jnp.bfloat16)],
@@ -217,16 +235,35 @@
         name="place_and_multiply",
     )(place, arrived, *owns, *mates)
     parts = lax.all_to_all(
-        partial.reshape(block_rows // 8, 4, LANES), ("x", "core", "yh", "zq"), split_axis=0, concat_axis=0, tiled=True
-    )
+        partial.reshape(block_rows // 32, 16, LANES), ("x", "zq"), split_axis=0, concat_axis=0, tiled=True
+    )
+    swap = [(0, 1), (1, 0)]
+    tile = jax.ShapeDtypeStruct((8, LANES), jnp.float32)
+    here, there = pl.pallas_call(
+        sum_kernel,
+        out_shape=(tile, tile),
+        in_specs=[SMEM, VMEM],
+        out_specs=(VMEM, VMEM),
+        compiler_params=PARAMS,
+        name="sum_parts",
+    )(place, parts)
+    tile = jax.ShapeDtypeStruct((4, LANES), jnp.float32)
+    own, mate = pl.pallas_call(
+        halves_kernel,
+        out_shape=(tile, tile),
+        in_specs=[SMEM, VMEM, VMEM],
+        out_specs=(VMEM, VMEM),
+        compiler_params=PARAMS,
+        name="sum_over_y",
+    )(place, here, lax.ppermute(there, "yh", swap))
     return pl.pallas_call(
-        lambda *refs: last_kernel(pieces, *refs),
+        last_kernel,
         out_shape=jax.ShapeDtypeStruct((4, width), jnp.float32),
-        in_specs=[VMEM],
+        in_specs=[SMEM, VMEM, VMEM],
         out_specs=VMEM,
         compiler_params=PARAMS,
-        name="sum_parts",
-    )(parts.reshape(block_rows // 2, LANES))
+        name="join_columns",
+    )(place, own, lax.ppermute(mate, "core", swap))
 
 
 def solution(mesh):

time: 90.8 us -> 93.9 us (1.034)
  blocking collectives: 35.6 us -> 24.2 us
  starting transfers between devices: 37.5 us -> 46.3 us
  waiting for transfers between devices: 9.98 us -> 13.8 us
  Pallas kernels: 6.31 us -> 7.96 us
    all_to_all x1, blocking collectives: 35.6 us -> 24.2 us  [per_device(): lax.all_to_all(partial.reshape(block_rows // 32, 16, LANES), ('x', 'zq'),...]
    ppermute x0 -> x2, starting transfers between devices: none -> 8.78 us  [the longest x1 5.21 us: per_device(): lax.ppermute(there, 'yh', swap)]
    ppermute x0 -> x2, waiting for transfers between devices: none -> 3.84 us  [the longest x1 3.04 us: per_device(): lax.ppermute(there, 'yh', swap)]
    pallas_call x1 -> x3, Pallas kernels: 0.61 us -> 2.26 us  [the longest x1 1.14 us: per_device(): pl.pallas_call(last_kernel, out_shape=jax.ShapeDtypeStruct((4, width), jn...]
  transfers between devices with their start and end apart: 5 -> 7, of which waited for: 3 -> 5; matrix products, arithmetic and copies ran while one was open for 0% -> 0% of each run, Pallas kernels for 1% -> 1%
where the time goes in v8:
time: 93.9 us; the launch traced here: 93.4 us
  starting transfers between devices  46.3 us (49%)
  blocking collectives  24.2 us (26%)
  waiting for transfers between devices  13.8 us (15%)
  Pallas kernels  7.96 us (8%)
  between operations  0.94 us (1%)
    all_to_all x1, blocking collectives, per_device(): lax.all_to_all(partial.reshape(block_rows // 32, 16, LANES), ('x', 'zq'),...  24.2 us
    all_to_all x1, starting transfers between devices, per_device(): lax.all_to_all(packed.reshape(senders, 1, chunk * LANES), ('x', 'core', '...  18.4 us
    ppermute x2, starting transfers between devices, per_device(): lax.ppermute(sent, ('zq', 'zp'), pair)  12.9 us
    ppermute x2, waiting for transfers between devices, per_device(): lax.ppermute(sent, ('zq', 'zp'), pair)  8.47 us
    ppermute x2, starting transfers between devices, per_device(): mates.append(lax.ppermute(total, 'core', [(0, 1), (1, 0)]))  6.2 us
    ppermute x1, starting transfers between devices, per_device(): lax.ppermute(there, 'yh', swap)  5.21 us
    ppermute x1, starting transfers between devices, per_device(): lax.ppermute(mate, 'core', swap)  3.57 us
    ppermute x1, waiting for transfers between devices, per_device(): lax.ppermute(there, 'yh', swap)  3.04 us
  transfers between devices with their start and end apart: 7, of which 5 were waited for; matrix products, arithmetic and copies ran while one was open for 0% of the time, Pallas kernels for 1%

profile of v8, /device:TPU:1, one launch (start us, length us, event | category | flops | bytes accessed | tf_op | source)
XLA Modules:
  0.0 93.4 jit_solution(15330268132801637668)
XLA Ops:
  0.0 2.6 %pack_rows.1 = f32[2112,128]{1,0:T(8,128)} custom-call(f32[64,256]{1,0:T(8,128)} %refs_0_.1, f32[64,256]{1,0:T(8,128)} %refs_1_.1, s32[1,64]{1,0:T(1,128)} %bitcast.13), custom_call_target="tpu_custom_call" | custom-call | tf_op jit(solution)/shard_map/pack_rows/pallas_call | solution.py:169
  2.6 0.0 copy-start
  2.6 18.4 %all-to-all-start = ((f32[64,1,4224]{2,1,0:T(1,128)}), f32[64,1,4224]{2,1,0:T(1,128)S(1)}, u32[]{:S(2)}, u32[]{:S(2)}) async-start(f32[64,1,4224]{2,1,0:T(1,128)} %bitcast.12), calls=%async_computation | async-start | bytes 2162688 | tf_op jit(solution)/shard_map/all_to_all | solution.py:183
  21.9 0.1 pad_add_fusion.place_ref.refs_0_
  21.9 0.1 pad_maximum_fusion.coef_ref
  22.0 1.0 %left_factors.1 = (f32[256,512]{1,0:T(8,128)S(1)}, f32[256,512]{1,0:T(8,128)S(1)}, f32[256,512]{1,0:T(8,128)S(1)}, f32[256,512]{1,0:T(8,128)S(1)}) custom-call(s32[4]{0:T(128)S(1)} %pad_add_fusion.place_ref.refs_0_, f32[4]{0:T(128)S(1)} %pad_maximum_fusion.coef_ref, f32[2,1024,256]{2,1,0:T(8,128)S(1)} %bitcast.10), custom_call_target="tpu_custom_call" | custom-call | flops 1048576 | bytes 4194304 | tf_op jit(solution)/shard_map/left_factors/pallas_call | solution.py:199
  23.0 1.9 %collective-permute-start = (f32[256,512]{1,0:T(8,128)S(1)}, f32[256,512]{1,0:T(8,128)S(1)}, u32[]{:S(2)}, u32[]{:S(2)}) collective-permute-start(f32[256,512]{1,0:T(8,128)S(1)} %get-tuple-element.14), channel_id=1, source_target_pairs={{0,64},{64,0},{128,192},{192,128},{256,320},{320,256},{384,448},{4... | collective-permute-start | bytes 1572872 | tf_op jit(solution)/shard_map/ppermute | solution.py:224
  24.9 11.0 %collective-permute-start.1 = (f32[256,512]{1,0:T(8,128)S(1)}, f32[256,512]{1,0:T(8,128)S(1)}, u32[]{:S(2)}, u32[]{:S(2)}) collective-permute-start(f32[256,512]{1,0:T(8,128)S(1)} %get-tuple-element.16), channel_id=1, source_target_pairs={{0,448},{64,128},{128,64},{192,256},{256,192},{320,384},{384,320},... | collective-permute-start | bytes 1572872 | tf_op jit(solution)/shard_map/ppermute | solution.py:224
  35.9 1.9 %collective-permute-done.other_ref = f32[256,512]{1,0:T(8,128)S(1)} collective-permute-done((f32[256,512]{1,0:T(8,128)S(1)}, f32[256,512]{1,0:T(8,128)S(1)}, u32[]{:S(2)}, u32[]{:S(2)}) %collective-permute-start) | collective-permute-done | bytes 524320 | tf_op jit(solution)/shard_map/ppermute | solution.py:224
  37.8 0.1 pair_sums.2.refs_2_
  37.9 3.3 %collective-permute-start.2 = (f32[256,512]{1,0:T(8,128)S(1)}, f32[256,512]{1,0:T(8,128)S(1)}, u32[]{:S(2)}, u32[]{:S(2)}) collective-permute-start(f32[256,512]{1,0:T(8,128)S(1)} %pair_sums.2.refs_2_), channel_id=1, source_target_pairs={{0,4},{4,0},{1,5},{5,1},{2,6},{6,2},{3,7},{7,3},{8,12},{12,8},{9,1... | collective-permute-start | bytes 1572872 | tf_op jit(solution)/shard_map/ppermute | solution.py:226
  41.2 6.5 %collective-permute-done.1.other_ref = f32[256,512]{1,0:T(8,128)S(1)} collective-permute-done((f32[256,512]{1,0:T(8,128)S(1)}, f32[256,512]{1,0:T(8,128)S(1)}, u32[]{:S(2)}, u32[]{:S(2)}) %collective-permute-start.1) | collective-permute-done | bytes 524320 | tf_op jit(solution)/shard_map/ppermute | solution.py:224
  47.8 0.1 pair_sums.3.refs_3_
  47.9 2.9 %collective-permute-start.3 = (f32[256,512]{1,0:T(8,128)S(1)}, f32[256,512]{1,0:T(8,128)S(1)}, u32[]{:S(2)}, u32[]{:S(2)}) collective-permute-start(f32[256,512]{1,0:T(8,128)S(1)} %pair_sums.3.refs_3_), channel_id=1, source_target_pairs={{0,4},{4,0},{1,5},{5,1},{2,6},{6,2},{3,7},{7,3},{8,12},{12,8},{9,1... | collective-permute-start | bytes 1572872 | tf_op jit(solution)/shard_map/ppermute | solution.py:226
  50.8 1.5 %collective-permute-done.3.refs_5_ = f32[256,512]{1,0:T(8,128)S(1)} collective-permute-done((f32[256,512]{1,0:T(8,128)S(1)}, f32[256,512]{1,0:T(8,128)S(1)}, u32[]{:S(2)}, u32[]{:S(2)}) %collective-permute-start.3) | collective-permute-done | bytes 524320 | tf_op jit(solution)/shard_map/ppermute | solution.py:226
  52.3 1.9 %place_and_multiply.1 = f32[8,4,2,8,128]{4,3,2,1,0:T(8,128)S(1)} custom-call(s32[4]{0:T(128)S(1)} %pad_add_fusion.place_ref.refs_0_, f32[2112,128]{1,0:T(8,128)S(1)} %bitcast.9, f32[256,512]{1,0:T(8,128)S(1)} %pair_sums.2.refs_2_, f32[256,512]{1,0:T(8,128)S(1)} %pair_sums.3.refs_3_, f32[256,512]{1,0:T(8,128)S(1)} %collective-permute-done.2.refs_4_, ...), custom_call_target="tpu_custom_call" | custom-call | tf_op jit(solution)/shard_map/place_and_multiply/pallas_call | solution.py:228
  54.2 24.2 %all_to_all.10.parts_ref = f32[32,16,128]{2,1,0:T(8,128)S(1)} all-to-all(f32[32,16,128]{2,1,0:T(8,128)S(1)} %bitcast.11), channel_id=1, replica_groups=mesh['yh'=2,'zq'=4,'zp'=2,'x'=8,'core'=2,'yl'=4] {'x','zq'}, dimensions={0} | all-to-all | bytes 524288 | tf_op jit(solution)/shard_map/all_to_all | solution.py:237
  78.4 0.6 sum_parts.1
  79.0 5.2 %collective-permute-start.4 = (f32[8,128]{1,0:T(8,128)S(1)}, f32[8,128]{1,0:T(8,128)S(1)}, u32[]{:S(2)}, u32[]{:S(2)}) collective-permute-start(f32[8,128]{1,0:T(8,128)S(1)} %get-tuple-element.18), channel_id=1, source_target_pairs={{0,512},{512,0},{1,513},{513,1},{2,514},{514,2},{3,515},{515,3},{4... | collective-permute-start | bytes 12296 | tf_op jit(solution)/shard_map/ppermute | solution.py:258
  84.2 3.0 %collective-permute-done.4.other_ref = f32[8,128]{1,0:T(8,128)S(1)} collective-permute-done((f32[8,128]{1,0:T(8,128)S(1)}, f32[8,128]{1,0:T(8,128)S(1)}, u32[]{:S(2)}, u32[]{:S(2)}) %collective-permute-start.4) | collective-permute-done | bytes 4128 | tf_op jit(solution)/shard_map/ppermute | solution.py:258
  87.3 0.5 sum_over_y.1
  87.8 3.6 %collective-permute-start.5 = (f32[4,128]{1,0:T(4,128)S(1)}, f32[4,128]{1,0:T(4,128)S(1)}, u32[]{:S(2)}, u32[]{:S(2)}) collective-permute-start(f32[4,128]{1,0:T(4,128)S(1)} %get-tuple-element.20), channel_id=1, source_target_pairs={{0,4},{4,0},{1,5},{5,1},{2,6},{6,2},{3,7},{7,3},{8,12},{12,8},{9,1... | collective-permute-start | bytes 6152 | tf_op jit(solution)/shard_map/ppermute | solution.py:266
  91.4 0.8 collective-permute-done.5.other_ref
  92.2 1.1 %join_columns.1 = f32[4,256]{1,0:T(4,128)} custom-call(s32[4]{0:T(128)S(1)} %pad_add_fusion.place_ref.refs_0_, f32[4,128]{1,0:T(4,128)S(1)} %get-tuple-element.19.own_ref, f32[4,128]{1,0:T(4,128)S(1)} %collective-permute-done.5.other_ref), custom_call_target="tpu_custom_call" | custom-call | tf_op jit(solution)/shard_map/join_columns/pallas_call | solution.py:259
  (3 shorter events, 0.0 us)
Async XLA Ops:
  2.6 19.4 %copy-start = (f32[1,2,1024,256]{3,2,1,0:T(8,128)S(1)}, f32[1,2,1024,256]{3,2,1,0:T(8,128)}, u32[]{:S(2)}) copy-start(f32[1,2,1024,256]{3,2,1,0:T(8,128)} %param.8) | copy-start | bytes 6291460
  2.6 49.7 %all-to-all-start = ((f32[64,1,4224]{2,1,0:T(1,128)}), f32[64,1,4224]{2,1,0:T(1,128)S(1)}, u32[]{:S(2)}, u32[]{:S(2)}) async-start(f32[64,1,4224]{2,1,0:T(1,128)} %bitcast.12), calls=%async_computation | async-start | bytes 2162688 | tf_op jit(solution)/shard_map/all_to_all | solution.py:183
  23.0 14.8 %collective-permute-start = (f32[256,512]{1,0:T(8,128)S(1)}, f32[256,512]{1,0:T(8,128)S(1)}, u32[]{:S(2)}, u32[]{:S(2)}) collective-permute-start(f32[256,512]{1,0:T(8,128)S(1)} %get-tuple-element.14), channel_id=1, source_target_pairs={{0,64},{64,0},{128,192},{192,128},{256,320},{320,256},{384,448},{4... | collective-permute-start | bytes 1572872 | tf_op jit(solution)/shard_map/ppermute | solution.py:224
  24.9 22.9 %collective-permute-start.1 = (f32[256,512]{1,0:T(8,128)S(1)}, f32[256,512]{1,0:T(8,128)S(1)}, u32[]{:S(2)}, u32[]{:S(2)}) collective-permute-start(f32[256,512]{1,0:T(8,128)S(1)} %get-tuple-element.16), channel_id=1, source_target_pairs={{0,448},{64,128},{128,64},{192,256},{256,192},{320,384},{384,320},... | collective-permute-start | bytes 1572872 | tf_op jit(solution)/shard_map/ppermute | solution.py:224
  37.9 12.9 %collective-permute-start.2 = (f32[256,512]{1,0:T(8,128)S(1)}, f32[256,512]{1,0:T(8,128)S(1)}, u32[]{:S(2)}, u32[]{:S(2)}) collective-permute-start(f32[256,512]{1,0:T(8,128)S(1)} %pair_sums.2.refs_2_), channel_id=1, source_target_pairs={{0,4},{4,0},{1,5},{5,1},{2,6},{6,2},{3,7},{7,3},{8,12},{12,8},{9,1... | collective-permute-start | bytes 1572872 | tf_op jit(solution)/shard_map/ppermute | solution.py:226
  47.9 4.4 %collective-permute-start.3 = (f32[256,512]{1,0:T(8,128)S(1)}, f32[256,512]{1,0:T(8,128)S(1)}, u32[]{:S(2)}, u32[]{:S(2)}) collective-permute-start(f32[256,512]{1,0:T(8,128)S(1)} %pair_sums.3.refs_3_), channel_id=1, source_target_pairs={{0,4},{4,0},{1,5},{5,1},{2,6},{6,2},{3,7},{7,3},{8,12},{12,8},{9,1... | collective-permute-start | bytes 1572872 | tf_op jit(solution)/shard_map/ppermute | solution.py:226
  79.0 8.3 %collective-permute-start.4 = (f32[8,128]{1,0:T(8,128)S(1)}, f32[8,128]{1,0:T(8,128)S(1)}, u32[]{:S(2)}, u32[]{:S(2)}) collective-permute-start(f32[8,128]{1,0:T(8,128)S(1)} %get-tuple-element.18), channel_id=1, source_target_pairs={{0,512},{512,0},{1,513},{513,1},{2,514},{514,2},{3,515},{515,3},{4... | collective-permute-start | bytes 12296 | tf_op jit(solution)/shard_map/ppermute | solution.py:258
  87.8 4.4 %collective-permute-start.5 = (f32[4,128]{1,0:T(4,128)S(1)}, f32[4,128]{1,0:T(4,128)S(1)}, u32[]{:S(2)}, u32[]{:S(2)}) collective-permute-start(f32[4,128]{1,0:T(4,128)S(1)} %get-tuple-element.20), channel_id=1, source_target_pairs={{0,4},{4,0},{1,5},{5,1},{2,6},{6,2},{3,7},{7,3},{8,12},{12,8},{9,1... | collective-permute-start | bytes 6152 | tf_op jit(solution)/shard_map/ppermute | solution.py:266

commit v9 on v4

--- a/solution.py
+++ b/solution.py
@@ -15,6 +15,8 @@
 SLOTS = 8
 VMEM = pl.BlockSpec(memory_space=pltpu.VMEM)
 SMEM = pl.BlockSpec(memory_space=pltpu.SMEM)
+ANY = pl.BlockSpec(memory_space=pl.ANY)
+INPUTS = pltpu.CompilerParams(vmem_limit_bytes=56 * 1024 * 1024)
 PARAMS = pltpu.CompilerParams(vmem_limit_bytes=40 * 1024 * 1024)
 
 
@@ -22,10 +24,19 @@
     return lax.broadcasted_iota(jnp.int32, shape, axis)
 
 
-def pack_kernel(rows_axis, cols_axis, ham_ref, mar_ref, owner_ref, out_ref):
-    share, width = ham_ref.shape
-    shift = (4096 // rows_axis).bit_length() - 1
-    own_r = jnp.broadcast_to(owner_ref[...].astype(jnp.float32), (share, share))
+def pack_kernel(rows_axis, cols_axis, place_ref, ham_ref, mar_ref, owner_ref, out_ref, held, owner, sems):
+    share, width = held.shape
+    shift = (share * cols_axis).bit_length() - 1
+    labels_copy = pltpu.make_async_copy(owner_ref, owner, sems.at[0])
+    labels_copy.start()
+    for which, ref in enumerate((ham_ref, mar_ref)):
+
+        @pl.when(place_ref[2] == which)
+        def _():
+            pltpu.make_async_copy(ref, held, sems.at[1]).start()
+
+    labels_copy.wait()
+    own_r = jnp.broadcast_to(owner[...].astype(jnp.float32), (share, share))
     own_c = jnp.sum(jnp.where(iota((share, share), 0) == iota((share, share), 1), own_r, 0.0), axis=1, keepdims=True)
     own_c = jnp.broadcast_to(own_c, (share, share)).astype(jnp.int32)
     own_r = own_r.astype(jnp.int32)
@@ -44,19 +55,18 @@
         0.0,
     )
     labels = jnp.sum(labels, axis=0, keepdims=True)
-    chunk = 2 * width // LANES * SLOTS + 1
-    for which, ref in enumerate((ham_ref, mar_ref)):
-        packed = jnp.dot(packer, ref[...], precision=lax.Precision.HIGHEST, preferred_element_type=jnp.float32)
-        for part in range(width // LANES):
-            offset = (which * (width // LANES) + part) * SLOTS
-            for row in range(rows_axis):
-                tile = packed[row * SLOTS : (row + 1) * SLOTS, part * LANES : (part + 1) * LANES]
-                for col in range(cols_axis):
-                    base = (row * cols_axis + col) * chunk + offset
-                    out_ref[base : base + SLOTS, :] = tile
+    chunk = width // LANES * SLOTS + 1
     for target in range(rows_axis * cols_axis):
         base = (target + 1) * chunk - 1
         out_ref[base : base + 1, :] = labels
+    pltpu.make_async_copy(ham_ref, held, sems.at[1]).wait()
+    packed = jnp.dot(packer, held[...], precision=lax.Precision.HIGHEST, preferred_element_type=jnp.float32)
+    for part in range(width // LANES):
+        for row in range(rows_axis):
+            tile = packed[row * SLOTS : (row + 1) * SLOTS, part * LANES : (part + 1) * LANES]
+            for col in range(cols_axis):
+                base = (row * cols_axis + col) * chunk + part * SLOTS
+                out_ref[base : base + SLOTS, :] = tile
 
 
 def split(value):
@@ -96,42 +106,52 @@
     out_ref[:, 1] = jnp.where(upper, pltpu.roll(left, 4, 1), right)
 
 
-def multiply(out_ref, which, highs, lows, panel_high_ref, panel_low_ref):
-    dot = lambda a, b: jnp.dot(a, b, preferred_element_type=jnp.float32)
-    for index in range(2):
-
-        @pl.when(which == index)
-        def _():
-            high, low, panel = highs[index][...], lows[index][...], panel_high_ref[...]
-            store_chunks(out_ref, dot(high, panel) + (dot(low, panel) + dot(high, panel_low_ref[...])))
-
-
-def first_kernel(senders, place_ref, rows_ref, high0, low0, high1, low1, out_ref, panel_high_ref, panel_low_ref):
-    row, core = place_ref[0], place_ref[1]
+def place_kernel(senders, place_ref, rows_ref, out_ref):
     chunk = rows_ref.shape[0] // senders
-    depth = panel_high_ref.shape[0] // 2
-    parts = (chunk - 1) // SLOTS
+    depth = out_ref.shape[0]
     labels = rows_ref[pl.ds(chunk - 1, senders, stride=chunk), :]
     lane = iota((senders, LANES), 1)
     wanted = (iota((senders, depth), 1) + 1).astype(jnp.float32)
     places = []
     for slot in range(SLOTS):
-        label = jnp.sum(jnp.where(lane == row * SLOTS + slot, labels, 0.0), axis=1, keepdims=True)
+        label = jnp.sum(jnp.where(lane == place_ref[0] * SLOTS + slot, labels, 0.0), axis=1, keepdims=True)
         places.append(jnp.where(jnp.broadcast_to(label, (senders, depth)) == wanted, 1.0, 0.0))
     places = jnp.concatenate(places, axis=0).astype(jnp.bfloat16)
-    for part in range(parts):
+    for part in range((chunk - 1) // SLOTS):
         values = [rows_ref[pl.ds(part * SLOTS + slot, senders, stride=chunk), :] for slot in range(SLOTS)]
-        pieces = split(jnp.concatenate(values, axis=0))
-        which, left = divmod(part, parts // 2)
-        at = (slice(which * depth, (which + 1) * depth), slice(left * LANES, (left + 1) * LANES))
-        for ref, piece in zip((panel_high_ref, panel_low_ref), pieces):
-            placed = lax.dot_general(places, piece, (((0,), (0,)), ((), ())), preferred_element_type=jnp.float32)
-            ref[at] = placed.astype(jnp.bfloat16)
-    multiply(out_ref, 1 - core, (high0, high1), (low0, low1), panel_high_ref, panel_low_ref)
-
-
-def second_kernel(place_ref, high0, low0, high1, low1, panel_high_ref, panel_low_ref, out_ref):
-    multiply(out_ref, place_ref[1], (high0, high1), (low0, low1), panel_high_ref, panel_low_ref)
+        pieces = jnp.concatenate(split(jnp.concatenate(values, axis=0)), axis=1)
+        placed = lax.dot_general(places, pieces, (((0,), (0,)), ((), ())), preferred_element_type=jnp.float32)
+        out_ref[:, part * LANES : (part + 1) * LANES] = placed[:, :LANES] + placed[:, LANES:]
+
+
+def multiply(out_ref, which, highs, lows, panels):
+    dot = lambda a, b: jnp.dot(a, b, preferred_element_type=jnp.float32)
+    for index in range(2):
+
+        @pl.when(which == index)
+        def _():
+            total = None
+            for field, (panel_high, panel_low) in enumerate(panels):
+                depth = panel_high.shape[0]
+                columns = slice(field * depth, (field + 1) * depth)
+                high, low = highs[index][:, columns], lows[index][:, columns]
+                term = dot(high, panel_high) + (dot(low, panel_high) + dot(high, panel_low))
+                total = term if total is None else total + term
+            store_chunks(out_ref, total)
+
+
+def ordered(place_ref, mine_ref, other_ref):
+    even = place_ref[2] == 0
+    mine, other = mine_ref[...], other_ref[...]
+    return split(jnp.where(even, mine, other)), split(jnp.where(even, other, mine))
+
+
+def first_kernel(place_ref, mine_ref, other_ref, high0, low0, high1, low1, out_ref):
+    multiply(out_ref, 1 - place_ref[1], (high0, high1), (low0, low1), ordered(place_ref, mine_ref, other_ref))
+
+
+def second_kernel(place_ref, mine_ref, other_ref, high0, low0, high1, low1, out_ref):
+    multiply(out_ref, place_ref[1], (high0, high1), (low0, low1), ordered(place_ref, mine_ref, other_ref))
 
 
 def last_kernel(parts_ref, out_ref):
@@ -145,15 +165,24 @@
     cols_axis = lax.axis_size("yl")
     share, width = hamiltonian.shape
     senders = rows_axis * cols_axis
-    chunk = 2 * width // LANES * SLOTS + 1
+    chunk = width // LANES * SLOTS + 1
+    core = lax.axis_index("core")
+    place = jnp.stack(
+        [lax.axis_index("x") * lax.axis_size("core") + core, core, lax.axis_index("zp")]
+    ).astype(jnp.int32)
     packed = pl.pallas_call(
         lambda *refs: pack_kernel(rows_axis, cols_axis, *refs),
         out_shape=jax.ShapeDtypeStruct((senders * chunk, LANES), jnp.float32),
-        in_specs=[VMEM] * 3,
-        out_specs=VMEM,
-        compiler_params=PARAMS,
+        in_specs=[SMEM] + [ANY] * 3,
+        out_specs=VMEM,
+        scratch_shapes=[
+            pltpu.VMEM((share, width), jnp.float32),
+            pltpu.VMEM((1, share), jnp.int32),
+            pltpu.SemaphoreType.DMA((2,)),
+        ],
+        compiler_params=INPUTS,
         name="pack_rows",
-    )(hamiltonian, margin, owner.reshape(1, share))
+    )(place, hamiltonian, margin, owner.reshape(1, share))
     arrived = lax.all_to_all(
         packed.reshape(senders, 1, chunk * LANES), ("x", "core", "yl"), split_axis=0, concat_axis=0, tiled=True
     ).reshape(senders * chunk, LANES)
@@ -165,10 +194,6 @@
     shifted_im = weight_re * damping + weight_im * energy
     coefs = jnp.stack([-weight_im, -weight_re, shifted_im, shifted_re])
     block_rows, depth = inverse_blocks.shape[2:]
-    core = lax.axis_index("core")
-    place = jnp.stack(
-        [lax.axis_index("x") * lax.axis_size("core") + core, core, lax.axis_index("zp")]
-    ).astype(jnp.int32)
     factor = jax.ShapeDtypeStruct((block_rows // 4, 2 * depth), jnp.float32)
     factors = pl.pallas_call(
         left_kernel,
@@ -197,15 +222,23 @@
             name="pair_sums",
         )(own, lax.ppermute(sent, ("zq", "zp"), pair))
     chunks = jax.ShapeDtypeStruct((block_rows // 32, 2, 8, LANES), jnp.float32)
-    panel = jax.ShapeDtypeStruct((2 * depth, width), jnp.bfloat16)
-    sent, panel_high, panel_low = pl.pallas_call(
-        lambda *refs: first_kernel(senders, *refs),
-        out_shape=(chunks, panel, panel),
-        in_specs=[SMEM] + [VMEM] * 5,
-        out_specs=(VMEM,) * 3,
-        compiler_params=PARAMS,
-        name="place_and_multiply",
-    )(place, arrived, *summed)
+    mine = pl.pallas_call(
+        lambda *refs: place_kernel(senders, *refs),
+        out_shape=jax.ShapeDtypeStruct((depth, width), jnp.float32),
+        in_specs=[SMEM, VMEM],
+        out_specs=VMEM,
+        compiler_params=PARAMS,
+        name="place_rows",
+    )(place, arrived)
+    other = lax.ppermute(mine, "zp", [(0, 1), (1, 0)])
+    sent = pl.pallas_call(
+        first_kernel,
+        out_shape=chunks,
+        in_specs=[SMEM] + [VMEM] * 6,
+        out_specs=VMEM,
+        compiler_params=PARAMS,
+        name="multiply_other",
+    )(place, mine, other, *summed)
     received = lax.ppermute(sent, "core", [(0, 1), (1, 0)])
     kept = pl.pallas_call(
         second_kernel,
@@ -215,7 +248,7 @@
         compiler_params=PARAMS,
         cost_estimate=pl.CostEstimate(flops=3 * block_rows * depth * width, bytes_accessed=block_rows * depth * 4, transcendentals=0),
         name="multiply_own",
-    )(place, *summed, panel_high, panel_low)
+    )(place, mine, other, *summed)
     both = (kept + received).reshape(block_rows // 16, 8, LANES)
     parts = lax.all_to_all(both, ("x", "yh", "zq"), split_axis=0, concat_axis=0, tiled=True)
     return pl.pallas_call(

time: 91.7 us -> 92.9 us (1.013)
  blocking collectives: 32.7 us -> 27.7 us
  starting transfers between devices: 35.1 us -> 38 us
  Pallas kernels: 6.01 us -> 8.35 us
    ppermute x0 -> x1, waiting for transfers between devices: none -> 5.53 us  [per_device(): other = lax.ppermute(mine, 'zp', [(0, 1), (1, 0)])]
    all_to_all x1, blocking collectives: 32.7 us -> 27.7 us  [per_device(): lax.all_to_all(both, ('x', 'yh', 'zq'), split_axis=0, concat_axis=0, tile...]
    ppermute x2, waiting for transfers between devices: 12.6 us -> 8.2 us  [per_device(): lax.ppermute(sent, ('zq', 'zp'), pair)]
    ppermute x0 -> x1, starting transfers between devices: none -> 3.3 us  [per_device(): other = lax.ppermute(mine, 'zp', [(0, 1), (1, 0)])]
    pallas_call x1, Pallas kernels: 1.49 us -> 2.72 us  [per_device(): pl.pallas_call(lambda *refs: pack_kernel(rows_axis, cols_axis, *refs), ou...]
    pallas_call x1 -> x2, Pallas kernels: 1.8 us -> 2.06 us  [the longest x1 1.06 us: per_device(): pl.pallas_call(first_kernel, out_shape=chunks, in_specs=[SMEM] + [VMEM] *...]
    unnamed x8 -> x6, local copies, waits for them, and re-layouts: 2.34 us -> 2.19 us
  transfers between devices with their start and end apart: 4 -> 5, of which waited for: 4 -> 5; matrix products, arithmetic and copies ran while one was open for 0% -> 0% of each run, Pallas kernels for 2% -> 4%
where the time goes in v9:
time: 92.9 us; the launch traced here: 91.7 us
  starting transfers between devices  38 us (41%)
  blocking collectives  27.7 us (30%)
  waiting for transfers between devices  13.9 us (15%)
  Pallas kernels  8.35 us (9%)
  local copies, waits for them, and re-layouts  2.19 us (2%)
    all_to_all x1, blocking collectives, per_device(): lax.all_to_all(both, ('x', 'yh', 'zq'), split_axis=0, concat_axis=0, tile...  27.7 us
    all_to_all x1, starting transfers between devices, per_device(): lax.all_to_all(packed.reshape(senders, 1, chunk * LANES), ('x', 'core', '...  18.3 us
    ppermute x2, starting transfers between devices, per_device(): lax.ppermute(sent, ('zq', 'zp'), pair)  12.9 us
    ppermute x2, waiting for transfers between devices, per_device(): lax.ppermute(sent, ('zq', 'zp'), pair)  8.2 us
    ppermute x1, waiting for transfers between devices, per_device(): other = lax.ppermute(mine, 'zp', [(0, 1), (1, 0)])  5.53 us
    ppermute x1, starting transfers between devices, per_device(): received = lax.ppermute(sent, 'core', [(0, 1), (1, 0)])  3.52 us
    ppermute x1, starting transfers between devices, per_device(): other = lax.ppermute(mine, 'zp', [(0, 1), (1, 0)])  3.3 us
    pallas_call x1, Pallas kernels, per_device(): pl.pallas_call(lambda *refs: pack_kernel(rows_axis, cols_axis, *refs), ou...  2.72 us
  transfers between devices with their start and end apart: 5, of which 5 were waited for; matrix products, arithmetic and copies ran while one was open for 0% of the time, Pallas kernels for 4%

profile of v9, /device:TPU:1, one launch (start us, length us, event | category | flops | bytes accessed | tf_op | source)
XLA Modules:
  0.0 91.7 jit_solution(15679315949044630795)
XLA Ops:
  0.0 0.6 pad_add_fusion.refs_0_.place_ref
  0.6 2.7 %pack_rows.1 = f32[1088,128]{1,0:T(8,128)} custom-call(s32[3]{0:T(128)} %pad_add_fusion.refs_0_.place_ref, f32[64,256]{1,0:T(8,128)} %refs_1_.1, f32[64,256]{1,0:T(8,128)} %refs_2_.1, s32[1,64]{1,0:T(1,128)} %bitcast.12), custom_call_target="tpu_custom_call" | custom-call | tf_op jit(solution)/shard_map/pack_rows/pallas_call | solution.py:173
  3.3 18.3 %all-to-all-start = ((f32[64,1,2176]{2,1,0:T(1,128)}), f32[64,1,2176]{2,1,0:T(1,128)S(1)}, u32[]{:S(2)}, u32[]{:S(2)}) async-start(f32[64,1,2176]{2,1,0:T(1,128)} %bitcast.10), calls=%async_computation | async-start | bytes 1114112 | tf_op jit(solution)/shard_map/all_to_all | solution.py:186
  22.4 0.1 pad_maximum_fusion.coef_ref
  22.5 1.6 %copy-done = f32[1,2,1024,256]{3,2,1,0:T(8,128)S(1)} copy-done((f32[1,2,1024,256]{3,2,1,0:T(8,128)S(1)}, f32[1,2,1024,256]{3,2,1,0:T(8,128)}, u32[]{:S(2)}) %copy-start) | copy-done | bytes 2097176
  24.1 0.6 copy-done.1
  24.6 1.7 %left_factors.1 = (f32[256,512]{1,0:T(8,128)S(1)}, f32[256,512]{1,0:T(8,128)S(1)}, f32[256,512]{1,0:T(8,128)S(1)}, f32[256,512]{1,0:T(8,128)}) custom-call(s32[3]{0:T(128)S(1)} %copy-done.1, f32[4]{0:T(128)S(1)} %pad_maximum_fusion.coef_ref, f32[2,1024,256]{2,1,0:T(8,128)S(1)} %bitcast.9), custom_call_target="tpu_custom_call" | custom-call | flops 1048576 | bytes 4194304 | tf_op jit(solution)/shard_map/left_factors/pallas_call | solution.py:198
  26.3 11.0 %collective-permute-start.2 = (f32[256,512]{1,0:T(8,128)}, f32[256,512]{1,0:T(8,128)S(1)}, u32[]{:S(2)}, u32[]{:S(2)}) collective-permute-start(f32[256,512]{1,0:T(8,128)} %get-tuple-element.18), channel_id=1, source_target_pairs={{0,448},{64,128},{128,64},{192,256},{256,192},{320,384},{384,320},... | collective-permute-start | bytes 1572872 | tf_op jit(solution)/shard_map/ppermute | solution.py:223
  37.3 1.9 %collective-permute-start.1 = (f32[256,512]{1,0:T(8,128)S(1)}, f32[256,512]{1,0:T(8,128)S(1)}, u32[]{:S(2)}, u32[]{:S(2)}) collective-permute-start(f32[256,512]{1,0:T(8,128)S(1)} %get-tuple-element.14), channel_id=1, source_target_pairs={{0,64},{64,0},{128,192},{192,128},{256,320},{320,256},{384,448},{4... | collective-permute-start | bytes 1572872 | tf_op jit(solution)/shard_map/ppermute | solution.py:223
  39.2 0.1 all-to-all-done
  39.3 0.0 copy-done.2
  39.3 1.0 %place_rows.1.mine_ref = f32[256,256]{1,0:T(8,128)S(1)} custom-call(s32[3]{0:T(128)S(1)} %copy-done.2, f32[1088,128]{1,0:T(8,128)S(1)} %bitcast.8), custom_call_target="tpu_custom_call" | custom-call | tf_op jit(solution)/shard_map/place_rows/pallas_call | solution.py:225
  40.3 3.3 %collective-permute-start = (f32[256,256]{1,0:T(8,128)S(1)}, f32[256,256]{1,0:T(8,128)S(1)}, u32[]{:S(2)}, u32[]{:S(2)}) collective-permute-start(f32[256,256]{1,0:T(8,128)S(1)} %place_rows.1.mine_ref), channel_id=1, source_target_pairs={{0,64},{64,0},{1,65},{65,1},{2,66},{66,2},{3,67},{67,3},{4,68},{68... | collective-permute-start | bytes 786440 | tf_op jit(solution)/shard_map/ppermute | solution.py:233
  43.6 5.8 %collective-permute-done.2.other_ref = f32[256,512]{1,0:T(8,128)S(1)} collective-permute-done((f32[256,512]{1,0:T(8,128)}, f32[256,512]{1,0:T(8,128)S(1)}, u32[]{:S(2)}, u32[]{:S(2)}) %collective-permute-start.2) | collective-permute-done | bytes 524320 | tf_op jit(solution)/shard_map/ppermute | solution.py:223
  49.4 0.1 pair_sums.3
  49.5 2.4 %collective-permute-done.1.other_ref = f32[256,512]{1,0:T(8,128)S(1)} collective-permute-done((f32[256,512]{1,0:T(8,128)S(1)}, f32[256,512]{1,0:T(8,128)S(1)}, u32[]{:S(2)}, u32[]{:S(2)}) %collective-permute-start.1) | collective-permute-done | bytes 524320 | tf_op jit(solution)/shard_map/ppermute | solution.py:223
  51.9 0.1 pair_sums.2
  52.0 5.5 %collective-permute-done.other_ref = f32[256,256]{1,0:T(8,128)S(1)} collective-permute-done((f32[256,256]{1,0:T(8,128)S(1)}, f32[256,256]{1,0:T(8,128)S(1)}, u32[]{:S(2)}, u32[]{:S(2)}) %collective-permute-start) | collective-permute-done | bytes 262176 | tf_op jit(solution)/shard_map/ppermute | solution.py:233
  57.6 1.1 %multiply_other.1 = f32[32,2,8,128]{3,2,1,0:T(8,128)S(1)} custom-call(s32[3]{0:T(128)S(1)} %copy-done.2, f32[256,256]{1,0:T(8,128)S(1)} %place_rows.1.mine_ref, f32[256,256]{1,0:T(8,128)S(1)} %collective-permute-done.other_ref, bf16[256,512]{1,0:T(8,128)(2,1)S(1)} %get-tuple-element.15.high0, bf16[256,512]{1,0:T(8,128)(2,1)S(1)} %get-tuple-element.16.low0, ...), custom_call_target="tpu_custom_call" | custom-call | tf_op jit(solution)/shard_map/multiply_other/pallas_call | solution.py:234
  58.6 3.5 %collective-permute-start.3 = (f32[32,2,8,128]{3,2,1,0:T(8,128)S(1)}, f32[32,2,8,128]{3,2,1,0:T(8,128)S(1)}, u32[]{:S(2)}, u32[]{:S(2)}) collective-permute-start(f32[32,2,8,128]{3,2,1,0:T(8,128)S(1)} %multiply_other.1), channel_id=1, source_target_pairs={{0,4},{4,0},{1,5},{5,1},{2,6},{6,2},{3,7},{7,3},{8,12},{12,8},{9,1... | collective-permute-start | bytes 786440 | tf_op jit(solution)/shard_map/ppermute | solution.py:242
  62.1 1.1 %multiply_own.1 = f32[32,2,8,128]{3,2,1,0:T(8,128)S(1)} custom-call(s32[3]{0:T(128)S(1)} %copy-done.2, f32[256,256]{1,0:T(8,128)S(1)} %place_rows.1.mine_ref, f32[256,256]{1,0:T(8,128)S(1)} %collective-permute-done.other_ref, bf16[256,512]{1,0:T(8,128)(2,1)S(1)} %get-tuple-element.15.high0, bf16[256,512]{1,0:T(8,128)(2,1)S(1)} %get-tuple-element.16.low0, ...), custom_call_target="tpu_custom_call" | custom-call | flops 201326592 | bytes 1048576 | tf_op jit(solution)/shard_map/multiply_own/pallas_call | solution.py:243
  63.2 0.1 collective-permute-done.3
  63.3 27.7 %all_to_all.10.parts_ref = f32[64,8,128]{2,1,0:T(8,128)S(1)} all-to-all(f32[64,8,128]{2,1,0:T(8,128)S(1)} %bitcast.11), channel_id=1, replica_groups=mesh['yh'=2,'zq'=4,'zp'=2,'x'=8,'core'=2,'yl'=4] {'x','yh','zq'}, dimensions={0} | all-to-all | bytes 524288 | tf_op jit(solution)/shard_map/all_to_all | solution.py:253
  91.0 0.7 sum_parts.1
  (4 shorter events, 0.0 us)
Async XLA Ops:
  0.6 38.8 %copy-start.2 = (s32[3]{0:T(128)S(1)}, s32[3]{0:T(128)}, u32[]{:S(2)}) copy-start(s32[3]{0:T(128)} %pad_add_fusion.refs_0_.place_ref) | copy-start | bytes 40
  3.3 36.0 %all-to-all-start = ((f32[64,1,2176]{2,1,0:T(1,128)}), f32[64,1,2176]{2,1,0:T(1,128)S(1)}, u32[]{:S(2)}, u32[]{:S(2)}) async-start(f32[64,1,2176]{2,1,0:T(1,128)} %bitcast.10), calls=%async_computation | async-start | bytes 1114112 | tf_op jit(solution)/shard_map/all_to_all | solution.py:186
  22.5 1.6 %copy-start = (f32[1,2,1024,256]{3,2,1,0:T(8,128)S(1)}, f32[1,2,1024,256]{3,2,1,0:T(8,128)}, u32[]{:S(2)}) copy-start(f32[1,2,1024,256]{3,2,1,0:T(8,128)} %param.8) | copy-start | bytes 6291460
  24.1 0.6 copy-start.1
  26.3 23.1 %collective-permute-start.2 = (f32[256,512]{1,0:T(8,128)}, f32[256,512]{1,0:T(8,128)S(1)}, u32[]{:S(2)}, u32[]{:S(2)}) collective-permute-start(f32[256,512]{1,0:T(8,128)} %get-tuple-element.18), channel_id=1, source_target_pairs={{0,448},{64,128},{128,64},{192,256},{256,192},{320,384},{384,320},... | collective-permute-start | bytes 1572872 | tf_op jit(solution)/shard_map/ppermute | solution.py:223
  37.3 14.6 %collective-permute-start.1 = (f32[256,512]{1,0:T(8,128)S(1)}, f32[256,512]{1,0:T(8,128)S(1)}, u32[]{:S(2)}, u32[]{:S(2)}) collective-permute-start(f32[256,512]{1,0:T(8,128)S(1)} %get-tuple-element.14), channel_id=1, source_target_pairs={{0,64},{64,0},{128,192},{192,128},{256,320},{320,256},{384,448},{4... | collective-permute-start | bytes 1572872 | tf_op jit(solution)/shard_map/ppermute | solution.py:223
  40.3 17.2 %collective-permute-start = (f32[256,256]{1,0:T(8,128)S(1)}, f32[256,256]{1,0:T(8,128)S(1)}, u32[]{:S(2)}, u32[]{:S(2)}) collective-permute-start(f32[256,256]{1,0:T(8,128)S(1)} %place_rows.1.mine_ref), channel_id=1, source_target_pairs={{0,64},{64,0},{1,65},{65,1},{2,66},{66,2},{3,67},{67,3},{4,68},{68... | collective-permute-start | bytes 786440 | tf_op jit(solution)/shard_map/ppermute | solution.py:233
  58.6 4.7 %collective-permute-start.3 = (f32[32,2,8,128]{3,2,1,0:T(8,128)S(1)}, f32[32,2,8,128]{3,2,1,0:T(8,128)S(1)}, u32[]{:S(2)}, u32[]{:S(2)}) collective-permute-start(f32[32,2,8,128]{3,2,1,0:T(8,128)S(1)} %multiply_other.1), channel_id=1, source_target_pairs={{0,4},{4,0},{1,5},{5,1},{2,6},{6,2},{3,7},{7,3},{8,12},{12,8},{9,1... | collective-permute-start | bytes 786440 | tf_op jit(solution)/shard_map/ppermute | solution.py:242

commit v10 on v7

--- a/solution.py
+++ b/solution.py
@@ -12,6 +12,7 @@
 weight_scale = 0.3
 
 LANES = 128
+PANEL_FLOPS = 5000000000
 SLOTS = 8
 VMEM = pl.BlockSpec(memory_space=pltpu.VMEM)
 SMEM = pl.BlockSpec(memory_space=pltpu.SMEM)
@@ -24,15 +25,18 @@
     return lax.broadcasted_iota(jnp.int32, shape, axis)
 
 
-def pack_kernel(rows_axis, cols_axis, *refs):
-    ham, mar, owner, sems = refs[4:]
-    out_ref = refs[3]
-    share, width = ham.shape
+def pack_kernel(rows_axis, cols_axis, ham_ref, mar_ref, owner_ref, out_ref, held, owner, sems):
+    share, width = held.shape
     shift = (share * cols_axis).bit_length() - 1
-    copies = [pltpu.make_async_copy(ref, to, sems.at[i]) for i, (ref, to) in enumerate(zip(refs[:3], (ham, mar, owner)))]
-    for copy in reversed(copies):
-        copy.start()
-    copies[2].wait()
+    labels_copy = pltpu.make_async_copy(owner_ref, owner, sems.at[0])
+    labels_copy.start()
+    for which, ref in enumerate((ham_ref, mar_ref)):
+
+        @pl.when(lax.axis_index("zp") == which)
+        def _():
+            pltpu.make_async_copy(ref, held, sems.at[1]).start()
+
+    labels_copy.wait()
     own_r = jnp.broadcast_to(owner[...].astype(jnp.float32), (share, share))
     own_c = jnp.sum(jnp.where(iota((share, share), 0) == iota((share, share), 1), own_r, 0.0), axis=1, keepdims=True)
     own_c = jnp.broadcast_to(own_c, (share, share)).astype(jnp.int32)
@@ -52,20 +56,19 @@
         0.0,
     )
     labels = jnp.sum(labels, axis=0, keepdims=True)
-    chunk = 2 * width // LANES * SLOTS + 1
+    chunk = width // LANES * SLOTS + 1
     for target in range(rows_axis * cols_axis):
         base = (target + 1) * chunk - 1
         out_ref[base : base + 1, :] = labels
+    pltpu.make_async_copy(ham_ref, held, sems.at[1]).wait()
+    packed = jnp.dot(packer, held[...], precision=lax.Precision.HIGHEST, preferred_element_type=jnp.float32)
     wide = 2 * SLOTS
-    for which, ref in enumerate((ham, mar)):
-        copies[which].wait()
-        packed = jnp.dot(packer, ref[...], precision=lax.Precision.HIGHEST, preferred_element_type=jnp.float32)
-        for row in range(rows_axis):
-            x, core = divmod(row, 2)
-            tile = packed[x * wide : (x + 1) * wide, core * LANES : (core + 1) * LANES]
-            for col in range(cols_axis):
-                base = (row * cols_axis + col) * chunk + which * wide
-                out_ref[base : base + wide, :] = tile
+    for row in range(rows_axis):
+        x, core = divmod(row, 2)
+        tile = packed[x * wide : (x + 1) * wide, core * LANES : (core + 1) * LANES]
+        for col in range(cols_axis):
+            base = (row * cols_axis + col) * chunk
+            out_ref[base : base + wide, :] = tile
 
 
 def split(value):
@@ -96,9 +99,9 @@
     sum_ref[...] = own_ref[...] + other_ref[...]
 
 
-def product_kernel(senders, pieces, place_ref, rows_ref, own0, own1, mate0, mate1, out_ref, panel_ref):
+def place_kernel(senders, place_ref, rows_ref, out_ref):
     chunk = rows_ref.shape[0] // senders
-    depth = panel_ref.shape[1] // 2
+    depth = out_ref.shape[0] // 2
     labels = rows_ref[pl.ds(chunk - 1, senders, stride=chunk), :]
     lane = iota((senders, LANES), 1)
     wanted = (iota((senders, depth), 1) + 1).astype(jnp.float32)
@@ -109,12 +112,23 @@
             label = jnp.sum(jnp.where(lane == at, labels, 0.0), axis=1, keepdims=True)
             places.append(jnp.where(jnp.broadcast_to(label, (senders, depth)) == wanted, 1.0, 0.0))
         places = jnp.concatenate(places, axis=0).astype(jnp.bfloat16)
-        for which in range(2):
-            start = (2 * which + block) * SLOTS
-            values = [rows_ref[pl.ds(start + slot, senders, stride=chunk), :] for slot in range(SLOTS)]
-            parts = jnp.concatenate(split(jnp.concatenate(values, axis=0)), axis=1)
-            placed = lax.dot_general(places, parts, (((0,), (0,)), ((), ())), preferred_element_type=jnp.float32)
-            panel_ref[block, which * depth : (which + 1) * depth, :] = placed.astype(jnp.bfloat16)
+        values = [rows_ref[pl.ds(block * SLOTS + slot, senders, stride=chunk), :] for slot in range(SLOTS)]
+        parts = jnp.concatenate(split(jnp.concatenate(values, axis=0)), axis=1)
+        placed = lax.dot_general(places, parts, (((0,), (0,)), ((), ())), preferred_element_type=jnp.float32)
+        out_ref[block * depth : (block + 1) * depth, :] = placed[:, :LANES] + placed[:, LANES:]
+
+
+def panel_kernel(place_ref, mine_ref, other_ref, panel_ref):
+    depth = panel_ref.shape[1] // 2
+    even = place_ref[2] == 0
+    for block in range(2):
+        rows = slice(block * depth, (block + 1) * depth)
+        mine, other = mine_ref[rows], other_ref[rows]
+        for which, value in enumerate((jnp.where(even, mine, other), jnp.where(even, other, mine))):
+            panel_ref[block, which * depth : (which + 1) * depth, :] = jnp.concatenate(split(value), axis=1)
+
+
+def product_kernel(pieces, place_ref, panel_ref, own0, own1, mate0, mate1, out_ref):
     for core in range(2):
 
         @pl.when(place_ref[1] == core)
@@ -147,7 +161,11 @@
     cols_axis = lax.axis_size("yl")
     share, width = hamiltonian.shape
     senders = rows_axis * cols_axis
-    chunk = 2 * width // LANES * SLOTS + 1
+    chunk = width // LANES * SLOTS + 1
+    core = lax.axis_index("core")
+    place = jnp.stack(
+        [lax.axis_index("x"), core, lax.axis_index("zp")]
+    ).astype(jnp.int32)
     packed = pl.pallas_call(
         lambda *refs: pack_kernel(rows_axis, cols_axis, *refs),
         out_shape=jax.ShapeDtypeStruct((senders * chunk, LANES), jnp.float32),
@@ -155,9 +173,8 @@
         out_specs=VMEM,
         scratch_shapes=[
             pltpu.VMEM((share, width), jnp.float32),
-            pltpu.VMEM((share, width), jnp.float32),
             pltpu.VMEM((1, share), jnp.int32),
-            pltpu.SemaphoreType.DMA((3,)),
+            pltpu.SemaphoreType.DMA((2,)),
         ],
         compiler_params=INPUTS,
         name="pack_rows",
@@ -173,10 +190,6 @@
     shifted_im = weight_re * damping + weight_im * energy
     coefs = jnp.stack([-weight_im, -weight_re, shifted_im, shifted_re])
     block_rows, depth = inverse_blocks.shape[2:]
-    core = lax.axis_index("core")
-    place = jnp.stack(
-        [lax.axis_index("x"), core, lax.axis_index("zp")]
-    ).astype(jnp.int32)
     factor = jax.ShapeDtypeStruct((block_rows // 4, 2 * depth), jnp.float32)
     factors = pl.pallas_call(
         left_kernel,
@@ -206,16 +219,33 @@
         )(own, lax.ppermute(sent, ("zq", "zp"), pair))
         owns.append(total)
         mates.append(lax.ppermute(total, "core", [(0, 1), (1, 0)]))
+    mine = pl.pallas_call(
+        lambda *refs: place_kernel(senders, *refs),
+        out_shape=jax.ShapeDtypeStruct((2 * depth, LANES), jnp.float32),
+        in_specs=[SMEM, VMEM],
+        out_specs=VMEM,
+        compiler_params=PARAMS,
+        name="place_rows",
+    )(place, arrived)
+    other = lax.ppermute(mine, "zp", [(0, 1), (1, 0)])
+    panel = pl.pallas_call(
+        panel_kernel,
+        out_shape=jax.ShapeDtypeStruct((2, 2 * depth, 2 * LANES), jnp.bfloat16),
+        in_specs=[SMEM, VMEM, VMEM],
+        out_specs=VMEM,
+        compiler_params=PARAMS,
+        cost_estimate=pl.CostEstimate(flops=PANEL_FLOPS, bytes_accessed=2**20, transcendentals=0),
+        name="split_panel",
+    )(place, mine, other)
     pieces = lax.axis_size("x")
     partial = pl.pallas_call(
-        lambda *refs: product_kernel(senders, pieces, *refs),
+        lambda *refs: product_kernel(pieces, *refs),
         out_shape=jax.ShapeDtypeStruct((block_rows // 2, LANES), jnp.float32),
         in_specs=[SMEM] + [VMEM] * 5,
         out_specs=VMEM,
-        scratch_shapes=[pltpu.VMEM((2, 2 * depth, 2 * LANES), jnp.bfloat16)],
-        compiler_params=PARAMS,
-        name="place_and_multiply",
-    )(place, arrived, *owns, *mates)
+        compiler_params=PARAMS,
+        name="multiply",
+    )(place, panel, *owns, *mates)
     parts = lax.all_to_all(
         partial.reshape(block_rows // 8, 4, LANES), ("x", "core", "yh", "zq"), split_axis=0, concat_axis=0, tiled=True
     )

time: 90.8 us -> 91.1 us (level)
  waiting for transfers between devices: 9.98 us -> 6.28 us
  starting transfers between devices: 37.5 us -> 39.3 us
  local copies, waits for them, and re-layouts: 0.01 us -> 1.59 us
  Pallas kernels: 6.31 us -> 7.36 us
    ppermute x2, waiting for transfers between devices: 8.47 us -> 4.82 us  [per_device(): lax.ppermute(sent, ('zq', 'zp'), pair)]
    ppermute x0 -> x1, starting transfers between devices: none -> 1.92 us  [per_device(): other = lax.ppermute(mine, 'zp', [(0, 1), (1, 0)])]
    unnamed x2, local copies, waits for them, and re-layouts: 0.01 us -> 1.59 us
    pallas_call x1 -> x3, Pallas kernels: 1.94 us -> 2.95 us  [the longest x1 1.27 us: per_device(): pl.pallas_call(lambda *refs: product_kernel(pieces, *refs), out_shape=jax...]
  transfers between devices with their start and end apart: 5 -> 6, of which waited for: 3 -> 3; matrix products, arithmetic and copies ran while one was open for 0% -> 0% of each run, Pallas kernels for 1% -> 4%
where the time goes in v10:
time: 91.1 us; the launch traced here: 90.6 us
  starting transfers between devices  39.3 us (43%)
  blocking collectives  35 us (38%)
  Pallas kernels  7.36 us (8%)
  waiting for transfers between devices  6.28 us (7%)
  local copies, waits for them, and re-layouts  1.59 us (2%)
  between operations  0.93 us (1%)
    all_to_all x1, blocking collectives, per_device(): lax.all_to_all(partial.reshape(block_rows // 8, 4, LANES), ('x', 'core',...  35 us
    all_to_all x1, starting transfers between devices, per_device(): lax.all_to_all(packed.reshape(senders, 1, chunk * LANES), ('x', 'core', '...  18.3 us
    ppermute x2, starting transfers between devices, per_device(): lax.ppermute(sent, ('zq', 'zp'), pair)  12.9 us
    ppermute x2, starting transfers between devices, per_device(): mates.append(lax.ppermute(total, 'core', [(0, 1), (1, 0)]))  6.24 us
    ppermute x2, waiting for transfers between devices, per_device(): lax.ppermute(sent, ('zq', 'zp'), pair)  4.82 us
    pallas_call x1, Pallas kernels, per_device(): pl.pallas_call(lambda *refs: pack_kernel(rows_axis, cols_axis, *refs), ou...  1.93 us
    ppermute x1, starting transfers between devices, per_device(): other = lax.ppermute(mine, 'zp', [(0, 1), (1, 0)])  1.92 us
  transfers between devices with their start and end apart: 6, of which 3 were waited for; matrix products, arithmetic and copies ran while one was open for 0% of the time, Pallas kernels for 4%

profile of v10, /device:TPU:1, one launch (start us, length us, event | category | flops | bytes accessed | tf_op | source)
XLA Modules:
  0.0 90.6 jit_solution(8408211157094116983)
XLA Ops:
  0.0 1.9 %pack_rows.1 = f32[1088,128]{1,0:T(8,128)} custom-call(f32[64,256]{1,0:T(8,128)} %refs_0_.1, f32[64,256]{1,0:T(8,128)} %refs_1_.1, s32[1,64]{1,0:T(1,128)} %bitcast.14), custom_call_target="tpu_custom_call" | custom-call | tf_op jit(solution)/shard_map/pack_rows/pallas_call | solution.py:169
  1.9 18.3 %all-to-all-start = ((f32[64,1,2176]{2,1,0:T(1,128)}), f32[64,1,2176]{2,1,0:T(1,128)S(1)}, u32[]{:S(2)}, u32[]{:S(2)}) async-start(f32[64,1,2176]{2,1,0:T(1,128)} %bitcast.13), calls=%async_computation | async-start | bytes 1114112 | tf_op jit(solution)/shard_map/all_to_all | solution.py:182
  21.0 0.1 pad_add_fusion.refs_0_.place_ref
  21.1 0.1 pad_maximum_fusion.coef_ref
  21.2 1.6 %copy-done = f32[1,2,1024,256]{3,2,1,0:T(8,128)S(1)} copy-done((f32[1,2,1024,256]{3,2,1,0:T(8,128)S(1)}, f32[1,2,1024,256]{3,2,1,0:T(8,128)}, u32[]{:S(2)}) %copy-start) | copy-done | bytes 2097176
  22.8 1.7 %left_factors.1 = (f32[256,512]{1,0:T(8,128)S(1)}, f32[256,512]{1,0:T(8,128)S(1)}, f32[256,512]{1,0:T(8,128)}, f32[256,512]{1,0:T(8,128)S(1)}) custom-call(s32[3]{0:T(128)S(1)} %pad_add_fusion.refs_0_.place_ref, f32[4]{0:T(128)S(1)} %pad_maximum_fusion.coef_ref, f32[2,1024,256]{2,1,0:T(8,128)S(1)} %bitcast.10), custom_call_target="tpu_custom_call" | custom-call | flops 1048576 | bytes 4194304 | tf_op jit(solution)/shard_map/left_factors/pallas_call | solution.py:194
  24.4 1.9 %collective-permute-start.1 = (f32[256,512]{1,0:T(8,128)}, f32[256,512]{1,0:T(8,128)S(1)}, u32[]{:S(2)}, u32[]{:S(2)}) collective-permute-start(f32[256,512]{1,0:T(8,128)} %get-tuple-element.10), channel_id=1, source_target_pairs={{0,64},{64,0},{128,192},{192,128},{256,320},{320,256},{384,448},{4... | collective-permute-start | bytes 1572872 | tf_op jit(solution)/shard_map/ppermute | solution.py:219
  26.4 11.0 %collective-permute-start.2 = (f32[256,512]{1,0:T(8,128)S(1)}, f32[256,512]{1,0:T(8,128)S(1)}, u32[]{:S(2)}, u32[]{:S(2)}) collective-permute-start(f32[256,512]{1,0:T(8,128)S(1)} %get-tuple-element.12), channel_id=1, source_target_pairs={{0,448},{64,128},{128,64},{192,256},{256,192},{320,384},{384,320},... | collective-permute-start | bytes 1572872 | tf_op jit(solution)/shard_map/ppermute | solution.py:219
  37.4 0.6 all-to-all-done
  38.0 1.1 %place_rows.1.mine_ref = f32[512,128]{1,0:T(8,128)S(1)} custom-call(s32[3]{0:T(128)S(1)} %pad_add_fusion.refs_0_.place_ref, f32[1088,128]{1,0:T(8,128)S(1)} %bitcast.9), custom_call_target="tpu_custom_call" | custom-call | tf_op jit(solution)/shard_map/place_rows/pallas_call | solution.py:222
  39.0 1.9 %collective-permute-start = (f32[512,128]{1,0:T(8,128)S(1)}, f32[512,128]{1,0:T(8,128)S(1)}, u32[]{:S(2)}, u32[]{:S(2)}) collective-permute-start(f32[512,128]{1,0:T(8,128)S(1)} %place_rows.1.mine_ref), channel_id=1, source_target_pairs={{0,64},{64,0},{1,65},{65,1},{2,66},{66,2},{3,67},{67,3},{4,68},{68... | collective-permute-start | bytes 786440 | tf_op jit(solution)/shard_map/ppermute | solution.py:230
  40.9 0.0 collective-permute-done.1.other_ref
  41.0 0.1 pair_sums.2.refs_2_
  41.1 3.4 %collective-permute-start.3 = (f32[256,512]{1,0:T(8,128)S(1)}, f32[256,512]{1,0:T(8,128)S(1)}, u32[]{:S(2)}, u32[]{:S(2)}) collective-permute-start(f32[256,512]{1,0:T(8,128)S(1)} %pair_sums.2.refs_2_), channel_id=1, source_target_pairs={{0,4},{4,0},{1,5},{5,1},{2,6},{6,2},{3,7},{7,3},{8,12},{12,8},{9,1... | collective-permute-start | bytes 1572872 | tf_op jit(solution)/shard_map/ppermute | solution.py:221
  44.4 4.8 %collective-permute-done.2.other_ref = f32[256,512]{1,0:T(8,128)S(1)} collective-permute-done((f32[256,512]{1,0:T(8,128)S(1)}, f32[256,512]{1,0:T(8,128)S(1)}, u32[]{:S(2)}, u32[]{:S(2)}) %collective-permute-start.2) | collective-permute-done | bytes 524320 | tf_op jit(solution)/shard_map/ppermute | solution.py:219
  49.2 0.1 pair_sums.3.refs_3_
  49.3 2.9 %collective-permute-start.4 = (f32[256,512]{1,0:T(8,128)S(1)}, f32[256,512]{1,0:T(8,128)S(1)}, u32[]{:S(2)}, u32[]{:S(2)}) collective-permute-start(f32[256,512]{1,0:T(8,128)S(1)} %pair_sums.3.refs_3_), channel_id=1, source_target_pairs={{0,4},{4,0},{1,5},{5,1},{2,6},{6,2},{3,7},{7,3},{8,12},{12,8},{9,1... | collective-permute-start | bytes 1572872 | tf_op jit(solution)/shard_map/ppermute | solution.py:221
  52.2 0.0 collective-permute-done.other_ref
  52.2 0.6 split_panel.1.refs_1_
  52.9 0.0 collective-permute-done.3.refs_4_
  52.9 0.9 collective-permute-done.4.refs_5_
  53.7 1.3 %multiply.21 = f32[512,128]{1,0:T(8,128)S(1)} custom-call(s32[3]{0:T(128)S(1)} %pad_add_fusion.refs_0_.place_ref, bf16[2,512,256]{2,1,0:T(8,128)(2,1)S(1)} %split_panel.1.refs_1_, f32[256,512]{1,0:T(8,128)S(1)} %pair_sums.2.refs_2_, f32[256,512]{1,0:T(8,128)S(1)} %pair_sums.3.refs_3_, f32[256,512]{1,0:T(8,128)S(1)} %collective-permute-done.3.refs_4_, ...), custom_call_target="tpu_custom_call" | custom-call | tf_op jit(solution)/shard_map/multiply/pallas_call | solution.py:241
  55.0 35.0 %all_to_all.10 = f32[128,4,128]{2,1,0:T(4,128)S(1)} all-to-all(f32[128,4,128]{2,1,0:T(4,128)S(1)} %bitcast.11), channel_id=1, replica_groups=mesh['yh'=2,'zq'=4,'zp'=2,'x'=8,'core'=2,'yl'=4] {'x','core','yh','zq'}, dimensions={0} | all-to-all | bytes 524288 | tf_op jit(solution)/shard_map/all_to_all | solution.py:249
  90.0 0.6 sum_parts.1
  (1 shorter events, 0.0 us)
Async XLA Ops:
  1.9 36.0 %all-to-all-start = ((f32[64,1,2176]{2,1,0:T(1,128)}), f32[64,1,2176]{2,1,0:T(1,128)S(1)}, u32[]{:S(2)}, u32[]{:S(2)}) async-start(f32[64,1,2176]{2,1,0:T(1,128)} %bitcast.13), calls=%async_computation | async-start | bytes 1114112 | tf_op jit(solution)/shard_map/all_to_all | solution.py:182
  21.2 1.6 %copy-start = (f32[1,2,1024,256]{3,2,1,0:T(8,128)S(1)}, f32[1,2,1024,256]{3,2,1,0:T(8,128)}, u32[]{:S(2)}) copy-start(f32[1,2,1024,256]{3,2,1,0:T(8,128)} %param.8) | copy-start | bytes 6291460
  24.4 16.5 %collective-permute-start.1 = (f32[256,512]{1,0:T(8,128)}, f32[256,512]{1,0:T(8,128)S(1)}, u32[]{:S(2)}, u32[]{:S(2)}) collective-permute-start(f32[256,512]{1,0:T(8,128)} %get-tuple-element.10), channel_id=1, source_target_pairs={{0,64},{64,0},{128,192},{192,128},{256,320},{320,256},{384,448},{4... | collective-permute-start | bytes 1572872 | tf_op jit(solution)/shard_map/ppermute | solution.py:219
  26.4 22.9 %collective-permute-start.2 = (f32[256,512]{1,0:T(8,128)S(1)}, f32[256,512]{1,0:T(8,128)S(1)}, u32[]{:S(2)}, u32[]{:S(2)}) collective-permute-start(f32[256,512]{1,0:T(8,128)S(1)} %get-tuple-element.12), channel_id=1, source_target_pairs={{0,448},{64,128},{128,64},{192,256},{256,192},{320,384},{384,320},... | collective-permute-start | bytes 1572872 | tf_op jit(solution)/shard_map/ppermute | solution.py:219
  39.0 13.2 %collective-permute-start = (f32[512,128]{1,0:T(8,128)S(1)}, f32[512,128]{1,0:T(8,128)S(1)}, u32[]{:S(2)}, u32[]{:S(2)}) collective-permute-start(f32[512,128]{1,0:T(8,128)S(1)} %place_rows.1.mine_ref), channel_id=1, source_target_pairs={{0,64},{64,0},{1,65},{65,1},{2,66},{66,2},{3,67},{67,3},{4,68},{68... | collective-permute-start | bytes 786440 | tf_op jit(solution)/shard_map/ppermute | solution.py:230
  41.1 11.8 %collective-permute-start.3 = (f32[256,512]{1,0:T(8,128)S(1)}, f32[256,512]{1,0:T(8,128)S(1)}, u32[]{:S(2)}, u32[]{:S(2)}) collective-permute-start(f32[256,512]{1,0:T(8,128)S(1)} %pair_sums.2.refs_2_), channel_id=1, source_target_pairs={{0,4},{4,0},{1,5},{5,1},{2,6},{6,2},{3,7},{7,3},{8,12},{12,8},{9,1... | collective-permute-start | bytes 1572872 | tf_op jit(solution)/shard_map/ppermute | solution.py:221
  49.3 4.4 %collective-permute-start.4 = (f32[256,512]{1,0:T(8,128)S(1)}, f32[256,512]{1,0:T(8,128)S(1)}, u32[]{:S(2)}, u32[]{:S(2)}) collective-permute-start(f32[256,512]{1,0:T(8,128)S(1)} %pair_sums.3.refs_3_), channel_id=1, source_target_pairs={{0,4},{4,0},{1,5},{5,1},{2,6},{6,2},{3,7},{7,3},{8,12},{12,8},{9,1... | collective-permute-start | bytes 1572872 | tf_op jit(solution)/shard_map/ppermute | solution.py:221

commit v11 on v10

--- a/solution.py
+++ b/solution.py
@@ -12,7 +12,7 @@
 weight_scale = 0.3
 
 LANES = 128
-PANEL_FLOPS = 5000000000
+PANEL_FLOPS = 10000000000
 SLOTS = 8
 VMEM = pl.BlockSpec(memory_space=pltpu.VMEM)
 SMEM = pl.BlockSpec(memory_space=pltpu.SMEM)
@@ -95,8 +95,10 @@
             out_refs[2 + core][at] = jnp.where(odd_here, even, odd)
 
 
-def pair_kernel(own_ref, other_ref, sum_ref):
-    sum_ref[...] = own_ref[...] + other_ref[...]
+def pair_kernel(own0, other0, own1, other1, sum_ref):
+    rows = own0.shape[0]
+    sum_ref[:rows] = own0[...] + other0[...]
+    sum_ref[rows:] = own1[...] + other1[...]
 
 
 def place_kernel(senders, place_ref, rows_ref, out_ref):
@@ -128,15 +130,17 @@
             panel_ref[block, which * depth : (which + 1) * depth, :] = jnp.concatenate(split(value), axis=1)
 
 
-def product_kernel(pieces, place_ref, panel_ref, own0, own1, mate0, mate1, out_ref):
+def product_kernel(pieces, place_ref, panel_ref, own_ref, mate_ref, out_ref):
     for core in range(2):
 
         @pl.when(place_ref[1] == core)
         def _():
-            for row_core, pair in enumerate(((own0, mate0), (own1, mate1))):
+            half = own_ref.shape[0] // 2
+            for row_core in range(2):
+                rows = slice(row_core * half, (row_core + 1) * half)
                 total = None
                 for block in range(2):
-                    high, low = split(pair[block ^ core][...])
+                    high, low = split((own_ref, mate_ref)[block ^ core][rows])
                     panel = panel_ref[block]
                     both = jnp.dot(high, panel, preferred_element_type=jnp.float32)
                     more = jnp.dot(low, panel[:, :LANES], preferred_element_type=jnp.float32)
@@ -205,20 +209,17 @@
         [(i, i ^ 1) for i in range(z_axis)],
         [(i, (i - 1 if i % 2 == 0 else i + 1) % z_axis) for i in range(z_axis)],
     )
-    owns, mates = [], []
-    for own, sent, pair in zip(factors[:2], factors[2:], pairs):
-        total = pl.pallas_call(
-            pair_kernel,
-            out_shape=factor,
-            in_specs=[VMEM] * 2,
-            out_specs=VMEM,
-            input_output_aliases={1: 0},
-            compiler_params=PARAMS,
-            cost_estimate=pl.CostEstimate(flops=block_rows * depth // 2, bytes_accessed=6 * block_rows * depth, transcendentals=0),
-            name="pair_sums",
-        )(own, lax.ppermute(sent, ("zq", "zp"), pair))
-        owns.append(total)
-        mates.append(lax.ppermute(total, "core", [(0, 1), (1, 0)]))
+    others = [lax.ppermute(sent, ("zq", "zp"), pair) for sent, pair in zip(factors[2:], pairs)]
+    total = pl.pallas_call(
+        pair_kernel,
+        out_shape=jax.ShapeDtypeStruct((block_rows // 2, 2 * depth), jnp.float32),
+        in_specs=[VMEM] * 4,
+        out_specs=VMEM,
+        compiler_params=PARAMS,
+        cost_estimate=pl.CostEstimate(flops=block_rows * depth, bytes_accessed=12 * block_rows * depth, transcendentals=0),
+        name="pair_sums",
+    )(factors[0], others[0], factors[1], others[1])
+    mate = lax.ppermute(total, "core", [(0, 1), (1, 0)])
     mine = pl.pallas_call(
         lambda *refs: place_kernel(senders, *refs),
         out_shape=jax.ShapeDtypeStruct((2 * depth, LANES), jnp.float32),
@@ -241,11 +242,11 @@
     partial = pl.pallas_call(
         lambda *refs: product_kernel(pieces, *refs),
         out_shape=jax.ShapeDtypeStruct((block_rows // 2, LANES), jnp.float32),
-        in_specs=[SMEM] + [VMEM] * 5,
+        in_specs=[SMEM] + [VMEM] * 3,
         out_specs=VMEM,
         compiler_params=PARAMS,
         name="multiply",
-    )(place, panel, *owns, *mates)
+    )(place, panel, total, mate)
     parts = lax.all_to_all(
         partial.reshape(block_rows // 8, 4, LANES), ("x", "core", "yh", "zq"), split_axis=0, concat_axis=0, tiled=True
     )

time: 91.1 us -> 91.5 us (level)
  waiting for transfers between devices: 6.28 us -> 10.5 us
  starting transfers between devices: 39.3 us -> 36 us
    ppermute x2, waiting for transfers between devices: 4.82 us -> 8.29 us  [per_device(): lax.ppermute(sent, ('zq', 'zp'), pair)]
    ppermute x2 -> x1, starting transfers between devices: 6.24 us -> 2.88 us  [per_device(): mate = lax.ppermute(total, 'core', [(0, 1), (1, 0)])]
  transfers between devices with their start and end apart: 6 -> 5, of which waited for: 3 -> 3; matrix products, arithmetic and copies ran while one was open for 0% -> 0% of each run, Pallas kernels for 4% -> 4%
where the time goes in v11:
time: 91.5 us; the launch traced here: 91.1 us
  starting transfers between devices  36 us (39%)
  blocking collectives  34.7 us (38%)
  waiting for transfers between devices  10.5 us (11%)
  Pallas kernels  7.26 us (8%)
  local copies, waits for them, and re-layouts  1.59 us (2%)
    all_to_all x1, blocking collectives, per_device(): lax.all_to_all(partial.reshape(block_rows // 8, 4, LANES), ('x', 'core',...  34.7 us
    all_to_all x1, starting transfers between devices, per_device(): lax.all_to_all(packed.reshape(senders, 1, chunk * LANES), ('x', 'core', '...  18.3 us
    ppermute x2, starting transfers between devices, per_device(): lax.ppermute(sent, ('zq', 'zp'), pair)  12.9 us
    ppermute x2, waiting for transfers between devices, per_device(): lax.ppermute(sent, ('zq', 'zp'), pair)  8.29 us
    ppermute x1, starting transfers between devices, per_device(): mate = lax.ppermute(total, 'core', [(0, 1), (1, 0)])  2.88 us
    pallas_call x1, Pallas kernels, per_device(): pl.pallas_call(lambda *refs: pack_kernel(rows_axis, cols_axis, *refs), ou...  1.93 us
    ppermute x1, starting transfers between devices, per_device(): other = lax.ppermute(mine, 'zp', [(0, 1), (1, 0)])  1.92 us
  transfers between devices with their start and end apart: 5, of which 3 were waited for; matrix products, arithmetic and copies ran while one was open for 0% of the time, Pallas kernels for 4%

profile of v11, /device:TPU:1, one launch (start us, length us, event | category | flops | bytes accessed | tf_op | source)
XLA Modules:
  0.0 91.1 jit_solution(1434605619893311903)
XLA Ops:
  0.0 1.9 %pack_rows.1 = f32[1088,128]{1,0:T(8,128)} custom-call(f32[64,256]{1,0:T(8,128)} %refs_0_.1, f32[64,256]{1,0:T(8,128)} %refs_1_.1, s32[1,64]{1,0:T(1,128)} %bitcast.14), custom_call_target="tpu_custom_call" | custom-call | tf_op jit(solution)/shard_map/pack_rows/pallas_call | solution.py:173
  1.9 18.3 %all-to-all-start = ((f32[64,1,2176]{2,1,0:T(1,128)}), f32[64,1,2176]{2,1,0:T(1,128)S(1)}, u32[]{:S(2)}, u32[]{:S(2)}) async-start(f32[64,1,2176]{2,1,0:T(1,128)} %bitcast.13), calls=%async_computation | async-start | bytes 1114112 | tf_op jit(solution)/shard_map/all_to_all | solution.py:186
  21.0 0.1 pad_add_fusion.refs_0_.place_ref
  21.1 0.1 pad_maximum_fusion.coef_ref
  21.2 0.0 copy-start
  21.2 1.6 %copy-done = f32[1,2,1024,256]{3,2,1,0:T(8,128)S(1)} copy-done((f32[1,2,1024,256]{3,2,1,0:T(8,128)S(1)}, f32[1,2,1024,256]{3,2,1,0:T(8,128)}, u32[]{:S(2)}) %copy-start) | copy-done | bytes 2097176
  22.8 1.7 %left_factors.1 = (f32[256,512]{1,0:T(8,128)S(1)}, f32[256,512]{1,0:T(8,128)S(1)}, f32[256,512]{1,0:T(8,128)}, f32[256,512]{1,0:T(8,128)S(1)}) custom-call(s32[3]{0:T(128)S(1)} %pad_add_fusion.refs_0_.place_ref, f32[4]{0:T(128)S(1)} %pad_maximum_fusion.coef_ref, f32[2,1024,256]{2,1,0:T(8,128)S(1)} %bitcast.10), custom_call_target="tpu_custom_call" | custom-call | flops 1048576 | bytes 4194304 | tf_op jit(solution)/shard_map/left_factors/pallas_call | solution.py:198
  24.4 1.9 %collective-permute-start.1 = (f32[256,512]{1,0:T(8,128)}, f32[256,512]{1,0:T(8,128)S(1)}, u32[]{:S(2)}, u32[]{:S(2)}) collective-permute-start(f32[256,512]{1,0:T(8,128)} %get-tuple-element.10), channel_id=1, source_target_pairs={{0,64},{64,0},{128,192},{192,128},{256,320},{320,256},{384,448},{4... | collective-permute-start | bytes 1572872 | tf_op jit(solution)/shard_map/ppermute | solution.py:212
  26.4 11.0 %collective-permute-start.2 = (f32[256,512]{1,0:T(8,128)S(1)}, f32[256,512]{1,0:T(8,128)S(1)}, u32[]{:S(2)}, u32[]{:S(2)}) collective-permute-start(f32[256,512]{1,0:T(8,128)S(1)} %get-tuple-element.12), channel_id=1, source_target_pairs={{0,448},{64,128},{128,64},{192,256},{256,192},{320,384},{384,320},... | collective-permute-start | bytes 1572872 | tf_op jit(solution)/shard_map/ppermute | solution.py:212
  37.4 0.6 all-to-all-done
  38.0 1.0 %place_rows.1.mine_ref = f32[512,128]{1,0:T(8,128)S(1)} custom-call(s32[3]{0:T(128)S(1)} %pad_add_fusion.refs_0_.place_ref, f32[1088,128]{1,0:T(8,128)S(1)} %bitcast.9), custom_call_target="tpu_custom_call" | custom-call | tf_op jit(solution)/shard_map/place_rows/pallas_call | solution.py:223
  39.0 1.9 %collective-permute-start = (f32[512,128]{1,0:T(8,128)S(1)}, f32[512,128]{1,0:T(8,128)S(1)}, u32[]{:S(2)}, u32[]{:S(2)}) collective-permute-start(f32[512,128]{1,0:T(8,128)S(1)} %place_rows.1.mine_ref), channel_id=1, source_target_pairs={{0,64},{64,0},{1,65},{65,1},{2,66},{66,2},{3,67},{67,3},{4,68},{68... | collective-permute-start | bytes 786440 | tf_op jit(solution)/shard_map/ppermute | solution.py:231
  40.9 0.0 collective-permute-done.1.other0
  41.0 8.3 %collective-permute-done.2.other1 = f32[256,512]{1,0:T(8,128)S(1)} collective-permute-done((f32[256,512]{1,0:T(8,128)S(1)}, f32[256,512]{1,0:T(8,128)S(1)}, u32[]{:S(2)}, u32[]{:S(2)}) %collective-permute-start.2) | collective-permute-done | bytes 524320 | tf_op jit(solution)/shard_map/ppermute | solution.py:212
  49.2 0.1 pair_sums.1.refs_2_
  49.4 2.9 %collective-permute-start.3 = (f32[512,512]{1,0:T(8,128)S(1)}, f32[512,512]{1,0:T(8,128)S(1)}, u32[]{:S(2)}, u32[]{:S(2)}) collective-permute-start(f32[512,512]{1,0:T(8,128)S(1)} %pair_sums.1.refs_2_), channel_id=1, source_target_pairs={{0,4},{4,0},{1,5},{5,1},{2,6},{6,2},{3,7},{7,3},{8,12},{12,8},{9,1... | collective-permute-start | bytes 3145736 | tf_op jit(solution)/shard_map/ppermute | solution.py:222
  52.2 0.0 collective-permute-done.other_ref
  52.3 0.6 split_panel.1.refs_1_
  52.9 1.6 %collective-permute-done.3.refs_3_ = f32[512,512]{1,0:T(8,128)S(1)} collective-permute-done((f32[512,512]{1,0:T(8,128)S(1)}, f32[512,512]{1,0:T(8,128)S(1)}, u32[]{:S(2)}, u32[]{:S(2)}) %collective-permute-start.3) | collective-permute-done | bytes 1048608 | tf_op jit(solution)/shard_map/ppermute | solution.py:222
  54.5 1.3 %multiply.21 = f32[512,128]{1,0:T(8,128)S(1)} custom-call(s32[3]{0:T(128)S(1)} %pad_add_fusion.refs_0_.place_ref, bf16[2,512,256]{2,1,0:T(8,128)(2,1)S(1)} %split_panel.1.refs_1_, f32[512,512]{1,0:T(8,128)S(1)} %pair_sums.1.refs_2_, f32[512,512]{1,0:T(8,128)S(1)} %collective-permute-done.3.refs_3_), custom_call_target="tpu_custom_call" | custom-call | tf_op jit(solution)/shard_map/multiply/pallas_call | solution.py:242
  55.8 34.7 %all_to_all.10 = f32[128,4,128]{2,1,0:T(4,128)S(1)} all-to-all(f32[128,4,128]{2,1,0:T(4,128)S(1)} %bitcast.11), channel_id=1, replica_groups=mesh['yh'=2,'zq'=4,'zp'=2,'x'=8,'core'=2,'yl'=4] {'x','core','yh','zq'}, dimensions={0} | all-to-all | bytes 524288 | tf_op jit(solution)/shard_map/all_to_all | solution.py:250
  90.5 0.6 sum_parts.1
Async XLA Ops:
  1.9 36.0 %all-to-all-start = ((f32[64,1,2176]{2,1,0:T(1,128)}), f32[64,1,2176]{2,1,0:T(1,128)S(1)}, u32[]{:S(2)}, u32[]{:S(2)}) async-start(f32[64,1,2176]{2,1,0:T(1,128)} %bitcast.13), calls=%async_computation | async-start | bytes 1114112 | tf_op jit(solution)/shard_map/all_to_all | solution.py:186
  21.2 1.6 %copy-start = (f32[1,2,1024,256]{3,2,1,0:T(8,128)S(1)}, f32[1,2,1024,256]{3,2,1,0:T(8,128)}, u32[]{:S(2)}) copy-start(f32[1,2,1024,256]{3,2,1,0:T(8,128)} %param.8) | copy-start | bytes 6291460
  24.4 16.5 %collective-permute-start.1 = (f32[256,512]{1,0:T(8,128)}, f32[256,512]{1,0:T(8,128)S(1)}, u32[]{:S(2)}, u32[]{:S(2)}) collective-permute-start(f32[256,512]{1,0:T(8,128)} %get-tuple-element.10), channel_id=1, source_target_pairs={{0,64},{64,0},{128,192},{192,128},{256,320},{320,256},{384,448},{4... | collective-permute-start | bytes 1572872 | tf_op jit(solution)/shard_map/ppermute | solution.py:212
  26.4 22.9 %collective-permute-start.2 = (f32[256,512]{1,0:T(8,128)S(1)}, f32[256,512]{1,0:T(8,128)S(1)}, u32[]{:S(2)}, u32[]{:S(2)}) collective-permute-start(f32[256,512]{1,0:T(8,128)S(1)} %get-tuple-element.12), channel_id=1, source_target_pairs={{0,448},{64,128},{128,64},{192,256},{256,192},{320,384},{384,320},... | collective-permute-start | bytes 1572872 | tf_op jit(solution)/shard_map/ppermute | solution.py:212
  39.0 13.2 %collective-permute-start = (f32[512,128]{1,0:T(8,128)S(1)}, f32[512,128]{1,0:T(8,128)S(1)}, u32[]{:S(2)}, u32[]{:S(2)}) collective-permute-start(f32[512,128]{1,0:T(8,128)S(1)} %place_rows.1.mine_ref), channel_id=1, source_target_pairs={{0,64},{64,0},{1,65},{65,1},{2,66},{66,2},{3,67},{67,3},{4,68},{68... | collective-permute-start | bytes 786440 | tf_op jit(solution)/shard_map/ppermute | solution.py:231
  49.4 5.2 %collective-permute-start.3 = (f32[512,512]{1,0:T(8,128)S(1)}, f32[512,512]{1,0:T(8,128)S(1)}, u32[]{:S(2)}, u32[]{:S(2)}) collective-permute-start(f32[512,512]{1,0:T(8,128)S(1)} %pair_sums.1.refs_2_), channel_id=1, source_target_pairs={{0,4},{4,0},{1,5},{5,1},{2,6},{6,2},{3,7},{7,3},{8,12},{12,8},{9,1... | collective-permute-start | bytes 3145736 | tf_op jit(solution)/shard_map/ppermute | solution.py:222

commit v12 on v4

--- a/solution.py
+++ b/solution.py
@@ -15,6 +15,8 @@
 SLOTS = 8
 VMEM = pl.BlockSpec(memory_space=pltpu.VMEM)
 SMEM = pl.BlockSpec(memory_space=pltpu.SMEM)
+ANY = pl.BlockSpec(memory_space=pl.ANY)
+INPUTS = pltpu.CompilerParams(vmem_limit_bytes=56 * 1024 * 1024)
 PARAMS = pltpu.CompilerParams(vmem_limit_bytes=40 * 1024 * 1024)
 
 
@@ -22,10 +24,16 @@
     return lax.broadcasted_iota(jnp.int32, shape, axis)
 
 
-def pack_kernel(rows_axis, cols_axis, ham_ref, mar_ref, owner_ref, out_ref):
-    share, width = ham_ref.shape
-    shift = (4096 // rows_axis).bit_length() - 1
-    own_r = jnp.broadcast_to(owner_ref[...].astype(jnp.float32), (share, share))
+def pack_kernel(rows_axis, cols_axis, *refs):
+    ham, mar, owner, sems = refs[4:]
+    out_ref = refs[3]
+    share, width = ham.shape
+    shift = (share * cols_axis).bit_length() - 1
+    copies = [pltpu.make_async_copy(ref, to, sems.at[i]) for i, (ref, to) in enumerate(zip(refs[:3], (ham, mar, owner)))]
+    for copy in reversed(copies):
+        copy.start()
+    copies[2].wait()
+    own_r = jnp.broadcast_to(owner[...].astype(jnp.float32), (share, share))
     own_c = jnp.sum(jnp.where(iota((share, share), 0) == iota((share, share), 1), own_r, 0.0), axis=1, keepdims=True)
     own_c = jnp.broadcast_to(own_c, (share, share)).astype(jnp.int32)
     own_r = own_r.astype(jnp.int32)
@@ -45,7 +53,11 @@
     )
     labels = jnp.sum(labels, axis=0, keepdims=True)
     chunk = 2 * width // LANES * SLOTS + 1
-    for which, ref in enumerate((ham_ref, mar_ref)):
+    for target in range(rows_axis * cols_axis):
+        base = (target + 1) * chunk - 1
+        out_ref[base : base + 1, :] = labels
+    for which, ref in enumerate((ham, mar)):
+        copies[which].wait()
         packed = jnp.dot(packer, ref[...], precision=lax.Precision.HIGHEST, preferred_element_type=jnp.float32)
         for part in range(width // LANES):
             offset = (which * (width // LANES) + part) * SLOTS
@@ -54,9 +66,6 @@
                 for col in range(cols_axis):
                     base = (row * cols_axis + col) * chunk + offset
                     out_ref[base : base + SLOTS, :] = tile
-    for target in range(rows_axis * cols_axis):
-        base = (target + 1) * chunk - 1
-        out_ref[base : base + 1, :] = labels
 
 
 def split(value):
@@ -149,9 +158,15 @@
     packed = pl.pallas_call(
         lambda *refs: pack_kernel(rows_axis, cols_axis, *refs),
         out_shape=jax.ShapeDtypeStruct((senders * chunk, LANES), jnp.float32),
-        in_specs=[VMEM] * 3,
+        in_specs=[ANY] * 3,
         out_specs=VMEM,
-        compiler_params=PARAMS,
+        scratch_shapes=[
+            pltpu.VMEM((share, width), jnp.float32),
+            pltpu.VMEM((share, width), jnp.float32),
+            pltpu.VMEM((1, share), jnp.int32),
+            pltpu.SemaphoreType.DMA((3,)),
+        ],
+        compiler_params=INPUTS,
         name="pack_rows",
     )(hamiltonian, margin, owner.reshape(1, share))
     arrived = lax.all_to_all(

time: 91.7 us -> 90.4 us (0.986)
  local copies, waits for them, and re-layouts: 2.34 us -> 0.01 us
  Pallas kernels: 6.01 us -> 7.11 us
    unnamed x8 -> x2, local copies, waits for them, and re-layouts: 2.34 us -> 0.01 us
    pallas_call x1, Pallas kernels: 1.49 us -> 2.58 us  [per_device(): pl.pallas_call(lambda *refs: pack_kernel(rows_axis, cols_axis, *refs), ou...]
where the time goes in v12:
time: 90.4 us; the launch traced here: 89.4 us
  starting transfers between devices  35.1 us (39%)
  blocking collectives  32.7 us (36%)
  waiting for transfers between devices  13.4 us (15%)
  Pallas kernels  7.11 us (8%)
    all_to_all x1, blocking collectives, per_device(): lax.all_to_all(both, ('x', 'yh', 'zq'), split_axis=0, concat_axis=0, tile...  32.7 us
    all_to_all x1, starting transfers between devices, per_device(): lax.all_to_all(packed.reshape(senders, 1, chunk * LANES), ('x', 'core', '...  18.4 us
    ppermute x2, starting transfers between devices, per_device(): lax.ppermute(sent, ('zq', 'zp'), pair)  12.9 us
    ppermute x2, waiting for transfers between devices, per_device(): lax.ppermute(sent, ('zq', 'zp'), pair)  12.6 us
    ppermute x1, starting transfers between devices, per_device(): received = lax.ppermute(sent, 'core', [(0, 1), (1, 0)])  3.79 us
    pallas_call x1, Pallas kernels, per_device(): pl.pallas_call(lambda *refs: pack_kernel(rows_axis, cols_axis, *refs), ou...  2.58 us
  transfers between devices with their start and end apart: 4, of which 4 were waited for; matrix products, arithmetic and copies ran while one was open for 0% of the time, Pallas kernels for 2%

profile of v12, /device:TPU:1, one launch (start us, length us, event | category | flops | bytes accessed | tf_op | source)
XLA Modules:
  0.0 89.4 jit_solution(11365289866029026290)
XLA Ops:
  0.0 2.6 %pack_rows.1 = f32[2112,128]{1,0:T(8,128)} custom-call(f32[64,256]{1,0:T(8,128)} %refs_0_.1, f32[64,256]{1,0:T(8,128)} %refs_1_.1, s32[1,64]{1,0:T(1,128)} %bitcast.12), custom_call_target="tpu_custom_call" | custom-call | tf_op jit(solution)/shard_map/pack_rows/pallas_call | solution.py:158
  2.6 0.0 copy-start
  2.6 18.4 %all-to-all-start = ((f32[64,1,4224]{2,1,0:T(1,128)}), f32[64,1,4224]{2,1,0:T(1,128)S(1)}, u32[]{:S(2)}, u32[]{:S(2)}) async-start(f32[64,1,4224]{2,1,0:T(1,128)} %bitcast.10), calls=%async_computation | async-start | bytes 2162688 | tf_op jit(solution)/shard_map/all_to_all | solution.py:172
  21.8 0.1 pad_add_fusion.place_ref.refs_0_
  21.9 0.1 pad_maximum_fusion.coef_ref
  22.0 0.0 copy-done
  22.0 1.0 %left_factors.1 = (f32[256,512]{1,0:T(8,128)S(1)}, f32[256,512]{1,0:T(8,128)S(1)}, f32[256,512]{1,0:T(8,128)S(1)}, f32[256,512]{1,0:T(8,128)S(1)}) custom-call(s32[3]{0:T(128)S(1)} %pad_add_fusion.place_ref.refs_0_, f32[4]{0:T(128)S(1)} %pad_maximum_fusion.coef_ref, f32[2,1024,256]{2,1,0:T(8,128)S(1)} %bitcast.9), custom_call_target="tpu_custom_call" | custom-call | flops 1048576 | bytes 4194304 | tf_op jit(solution)/shard_map/left_factors/pallas_call | solution.py:188
  23.0 11.0 %collective-permute-start.1 = (f32[256,512]{1,0:T(8,128)S(1)}, f32[256,512]{1,0:T(8,128)S(1)}, u32[]{:S(2)}, u32[]{:S(2)}) collective-permute-start(f32[256,512]{1,0:T(8,128)S(1)} %get-tuple-element.21), channel_id=1, source_target_pairs={{0,448},{64,128},{128,64},{192,256},{256,192},{320,384},{384,320},... | collective-permute-start | bytes 1572872 | tf_op jit(solution)/shard_map/ppermute | solution.py:213
  33.9 1.9 %collective-permute-start = (f32[256,512]{1,0:T(8,128)S(1)}, f32[256,512]{1,0:T(8,128)S(1)}, u32[]{:S(2)}, u32[]{:S(2)}) collective-permute-start(f32[256,512]{1,0:T(8,128)S(1)} %get-tuple-element.17), channel_id=1, source_target_pairs={{0,64},{64,0},{128,192},{192,128},{256,320},{320,256},{384,448},{4... | collective-permute-start | bytes 1572872 | tf_op jit(solution)/shard_map/ppermute | solution.py:213
  35.9 10.0 %collective-permute-done.1.other_ref = f32[256,512]{1,0:T(8,128)S(1)} collective-permute-done((f32[256,512]{1,0:T(8,128)S(1)}, f32[256,512]{1,0:T(8,128)S(1)}, u32[]{:S(2)}, u32[]{:S(2)}) %collective-permute-start.1) | collective-permute-done | bytes 524320 | tf_op jit(solution)/shard_map/ppermute | solution.py:213
  45.8 0.1 pair_sums.3
  45.9 2.6 %collective-permute-done.other_ref = f32[256,512]{1,0:T(8,128)S(1)} collective-permute-done((f32[256,512]{1,0:T(8,128)S(1)}, f32[256,512]{1,0:T(8,128)S(1)}, u32[]{:S(2)}, u32[]{:S(2)}) %collective-permute-start) | collective-permute-done | bytes 524320 | tf_op jit(solution)/shard_map/ppermute | solution.py:213
  48.6 0.1 pair_sums.2
  48.7 0.6 all-to-all-done
  49.3 1.8 %place_and_multiply.1 = (f32[32,2,8,128]{3,2,1,0:T(8,128)S(1)}, bf16[512,256]{1,0:T(8,128)(2,1)S(1)}, bf16[512,256]{1,0:T(8,128)(2,1)S(1)}) custom-call(s32[3]{0:T(128)S(1)} %pad_add_fusion.place_ref.refs_0_, f32[2112,128]{1,0:T(8,128)S(1)} %bitcast.8, bf16[256,512]{1,0:T(8,128)(2,1)S(1)} %get-tuple-element.18.refs_2_.high0, ...), custom_call_target="tpu_custom_call" | custom-call | tf_op jit(solution)/shard_map/place_and_multiply/pallas_call | solution.py:216
  51.1 3.8 %collective-permute-start.2 = (f32[32,2,8,128]{3,2,1,0:T(8,128)S(1)}, f32[32,2,8,128]{3,2,1,0:T(8,128)S(1)}, u32[]{:S(2)}, u32[]{:S(2)}) collective-permute-start(f32[32,2,8,128]{3,2,1,0:T(8,128)S(1)} %get-tuple-element.26), channel_id=1, source_target_pairs={{0,4},{4,0},{1,5},{5,1},{2,6},{6,2},{3,7},{7,3},{8,12},{12,8},{9,1... | collective-permute-start | bytes 786440 | tf_op jit(solution)/shard_map/ppermute | solution.py:224
  54.9 0.9 %multiply_own.1 = f32[32,2,8,128]{3,2,1,0:T(8,128)S(1)} custom-call(s32[3]{0:T(128)S(1)} %pad_add_fusion.place_ref.refs_0_, bf16[256,512]{1,0:T(8,128)(2,1)S(1)} %get-tuple-element.18.refs_2_.high0, bf16[256,512]{1,0:T(8,128)(2,1)S(1)} %get-tuple-element.19.refs_3_.low0, bf16[256,512]{1,0:T(8,128)(2,1)S(1)} %get-tuple-element.22.refs_4_.high1, ...), custom_call_target="tpu_custom_call" | custom-call | flops 201326592 | bytes 1048576 | tf_op jit(solution)/shard_map/multiply_own/pallas_call | solution.py:225
  55.8 0.2 collective-permute-done.2
  56.1 32.7 %all_to_all.10.parts_ref = f32[64,8,128]{2,1,0:T(8,128)S(1)} all-to-all(f32[64,8,128]{2,1,0:T(8,128)S(1)} %bitcast.11), channel_id=1, replica_groups=mesh['yh'=2,'zq'=4,'zp'=2,'x'=8,'core'=2,'yl'=4] {'x','yh','zq'}, dimensions={0} | all-to-all | bytes 524288 | tf_op jit(solution)/shard_map/all_to_all | solution.py:235
  88.7 0.7 sum_parts.1
  (1 shorter events, 0.0 us)
Async XLA Ops:
  2.6 19.4 %copy-start = (f32[1,2,1024,256]{3,2,1,0:T(8,128)S(1)}, f32[1,2,1024,256]{3,2,1,0:T(8,128)}, u32[]{:S(2)}) copy-start(f32[1,2,1024,256]{3,2,1,0:T(8,128)} %param.8) | copy-start | bytes 6291460
  2.6 46.7 %all-to-all-start = ((f32[64,1,4224]{2,1,0:T(1,128)}), f32[64,1,4224]{2,1,0:T(1,128)S(1)}, u32[]{:S(2)}, u32[]{:S(2)}) async-start(f32[64,1,4224]{2,1,0:T(1,128)} %bitcast.10), calls=%async_computation | async-start | bytes 2162688 | tf_op jit(solution)/shard_map/all_to_all | solution.py:172
  23.0 22.9 %collective-permute-start.1 = (f32[256,512]{1,0:T(8,128)S(1)}, f32[256,512]{1,0:T(8,128)S(1)}, u32[]{:S(2)}, u32[]{:S(2)}) collective-permute-start(f32[256,512]{1,0:T(8,128)S(1)} %get-tuple-element.21), channel_id=1, source_target_pairs={{0,448},{64,128},{128,64},{192,256},{256,192},{320,384},{384,320},... | collective-permute-start | bytes 1572872 | tf_op jit(solution)/shard_map/ppermute | solution.py:213
  33.9 14.6 %collective-permute-start = (f32[256,512]{1,0:T(8,128)S(1)}, f32[256,512]{1,0:T(8,128)S(1)}, u32[]{:S(2)}, u32[]{:S(2)}) collective-permute-start(f32[256,512]{1,0:T(8,128)S(1)} %get-tuple-element.17), channel_id=1, source_target_pairs={{0,64},{64,0},{128,192},{192,128},{256,320},{320,256},{384,448},{4... | collective-permute-start | bytes 1572872 | tf_op jit(solution)/shard_map/ppermute | solution.py:213
  51.1 4.9 %collective-permute-start.2 = (f32[32,2,8,128]{3,2,1,0:T(8,128)S(1)}, f32[32,2,8,128]{3,2,1,0:T(8,128)S(1)}, u32[]{:S(2)}, u32[]{:S(2)}) collective-permute-start(f32[32,2,8,128]{3,2,1,0:T(8,128)S(1)} %get-tuple-element.26), channel_id=1, source_target_pairs={{0,4},{4,0},{1,5},{5,1},{2,6},{6,2},{3,7},{7,3},{8,12},{12,8},{9,1... | collective-permute-start | bytes 786440 | tf_op jit(solution)/shard_map/ppermute | solution.py:224
